TPU v7x, 32 devices: a whole 2x2x4 slice. The times are simulated.
32 devices in a mesh: head: 4 (over z), batch: 4 (over y, core), dp: 2 (over x).
Axes of the slice: x: 2, y: 2, z: 4, core: 2. Of those that a mesh axis runs over, the one named last changes fastest.
Arguments:
- layer_input: bfloat16 [8, 4096, 1024], P(('batch', 'dp'), 'head'), may hold values from -6 to 6
- lengths: int32 [8, 3], P(('batch', 'dp')), may hold values from 1024 to 2048, as said below
- norm1_gain: float32 [1024], replicated, may hold values from 0.5 to 1.5
- qkv_weight: bfloat16 [3, 1024, 1024], P(None, None, 'head'), may hold values from -0.1875 to 0.1875
- kernels: float32 [3, 3, 1024], P(None, None, 'head'), may hold values from -1 to 1
- out_weight: bfloat16 [1024, 1024], P('head'), may hold values from -1.5 to 1.5
- out_bias: float32 [1024], replicated, may hold values from -4 to 4
- norm2_gain: float32 [1024], replicated, may hold values from 0.5 to 1.5
- up_weight: bfloat16 [1024, 4096], P(None, 'head'), may hold values from -0.1875 to 0.1875
- up_bias: float32 [4096], P('head'), may hold values from -6 to 6
- down_weight: bfloat16 [4096, 1024], P('head'), may hold values from -0.09375 to 0.09375
- down_bias: float32 [1024], replicated, may hold values from -6 to 6
- out_grad: bfloat16 [8, 4096, 1024], P(('batch', 'dp'), 'head'), may hold values from -6 to 6
Outputs:
- layer_output: bfloat16 [8, 4096, 1024], P(('batch', 'dp'), 'head')
- layer_input_grad: bfloat16 [8, 4096, 1024], P(('batch', 'dp'), 'head')
- norm1_gain_grad: float32 [1024], replicated
- qkv_weight_grad: float32 [3, 1024, 1024], P(None, None, 'head')
- kernels_grad: float32 [3, 3, 1024], P(None, None, 'head')
- out_weight_grad: float32 [1024, 1024], P('head')
- out_bias_grad: float32 [1024], replicated
- norm2_gain_grad: float32 [1024], replicated
- up_weight_grad: float32 [1024, 4096], P(None, 'head')
- up_bias_grad: float32 [4096], P('head')
- down_weight_grad: float32 [4096, 1024], P('head')
- down_bias_grad: float32 [1024], replicated
Inputs may be any that keep to these rules, and one draw needn't show every extreme that they name: Each group's three lengths are two of 1024 and one of 2048, in an order drawn for each group.
All inputs are finite; a program needn't handle non-finite values.
Results may differ from a plain program's by a relative error of at most 0.02.
Values may be sent and summed in bfloat16 or wider, within the bound.
A program may use at most 256 MiB of HBM per device.

v0:
```python
import math

import jax
import jax.numpy as jnp
from jax import lax
from jax.sharding import PartitionSpec as P

HS = 64
LONG = 2048


EPSILON = 1e-06


def rms_norm(values, gain_vector):
    return (
        values
        * lax.rsqrt(jnp.mean(values * values, axis=-1, keepdims=True) + EPSILON)
        * gain_vector
    )


def norm_backward(values, gain_vector, upstream):
    factor = lax.rsqrt(jnp.mean(values * values, axis=-1, keepdims=True) + EPSILON)
    unit_rows = values * factor
    scaled = gain_vector * upstream
    result = factor * (scaled - unit_rows * jnp.mean(scaled * unit_rows, axis=-1, keepdims=True))
    return (result, upstream * unit_rows)


def shifted(values, offset):
    return jnp.concatenate(
        [jnp.zeros((offset, values.shape[1]), values.dtype), values[:-offset]], axis=0
    )


def depthwise(values, kernel, position):
    one_back = jnp.where(position[:, None] >= 1, shifted(values, 1), 0.0)
    two_back = jnp.where(position[:, None] >= 2, shifted(values, 2), 0.0)
    return kernel[0] * values + kernel[1] * one_back + kernel[2] * two_back


def sequence_layout(seq_lengths, stream_length):
    boundary = jnp.cumsum(seq_lengths)
    places = jnp.arange(stream_length, dtype=jnp.int32)
    past_end = places[:, None] >= boundary[None, :]
    document = jnp.sum(past_end.astype(jnp.int32), axis=1)
    begins = jnp.max(jnp.where(past_end, boundary[None, :], 0), axis=1)
    return (document, places - begins)


def key_window(stream_length):
    return min(LONG, stream_length)


def window_start(position, first_row, window_rows, stream_length):
    row_place = lax.dynamic_index_in_dim(position, first_row, 0, keepdims=False)
    return jnp.clip(first_row - row_place, 0, stream_length - window_rows)


def block_mask(document, first_row, block_rows, key_start, window_rows):
    key_ids = key_start + jnp.arange(window_rows, dtype=jnp.int32)
    row_ids = first_row + jnp.arange(block_rows, dtype=jnp.int32)
    query_docs = lax.dynamic_slice_in_dim(document, first_row, block_rows, 0)
    key_docs = lax.dynamic_slice_in_dim(document, key_start, window_rows, 0)
    return (key_ids[None, :] <= row_ids[:, None]) & (key_docs[None, :] == query_docs[:, None])


def attention_forward(queries, key_rows, values, document, position, block_rows):
    stream_length, head_count, head_size = queries.shape
    score_scale = 1.0 / math.sqrt(head_size)
    window_rows = key_window(stream_length)

    def one_block(block_index):
        first_row = block_index * block_rows
        key_start = window_start(position, first_row, window_rows, stream_length)
        query_block = lax.dynamic_slice_in_dim(queries, first_row, block_rows, 0)
        key_block = lax.dynamic_slice_in_dim(key_rows, key_start, window_rows, 0)
        value_block = lax.dynamic_slice_in_dim(values, key_start, window_rows, 0)
        allowed = block_mask(document, first_row, block_rows, key_start, window_rows)
        scores = (
            jnp.einsum("qhd,khd->hqk", query_block, key_block, preferred_element_type=jnp.float32)
            * score_scale
        )
        scores = jnp.where(allowed[None], scores, -1e30)
        row_peak = jnp.max(scores, axis=-1, keepdims=True)
        exponent = jnp.exp(scores - row_peak)
        total_mass = jnp.sum(exponent, axis=-1, keepdims=True)
        soft_weights = (exponent / total_mass).astype(jnp.bfloat16)
        outcome = jnp.einsum(
            "hqk,khd->qhd", soft_weights, value_block, preferred_element_type=jnp.float32
        )
        return (outcome.astype(jnp.bfloat16), (row_peak + jnp.log(total_mass))[..., 0])

    block_outs, log_mass = lax.map(
        one_block, jnp.arange(stream_length // block_rows, dtype=jnp.int32)
    )
    return (block_outs.reshape(stream_length, head_count * head_size), log_mass)


def attention_backward(
    queries, key_rows, values, grad_out, log_mass, document, position, block_rows
):
    stream_length, head_count, head_size = queries.shape
    score_scale = 1.0 / math.sqrt(head_size)
    window_rows = key_window(stream_length)

    def one_block(running, block_index):
        key_grad, value_grad = running
        first_row = block_index * block_rows
        key_start = window_start(position, first_row, window_rows, stream_length)
        query_block = lax.dynamic_slice_in_dim(queries, first_row, block_rows, 0)
        grad_block = lax.dynamic_slice_in_dim(grad_out, first_row, block_rows, 0)
        key_block = lax.dynamic_slice_in_dim(key_rows, key_start, window_rows, 0)
        value_block = lax.dynamic_slice_in_dim(values, key_start, window_rows, 0)
        allowed = block_mask(document, first_row, block_rows, key_start, window_rows)
        scores = (
            jnp.einsum("qhd,khd->hqk", query_block, key_block, preferred_element_type=jnp.float32)
            * score_scale
        )
        scores = jnp.where(allowed[None], scores, -1e30)
        block_mass = lax.dynamic_index_in_dim(log_mass, block_index, 0, keepdims=False)
        soft_weights = jnp.exp(scores - block_mass[..., None])
        soft_grad = jnp.einsum(
            "qhd,khd->hqk", grad_block, value_block, preferred_element_type=jnp.float32
        )
        score_grad = soft_weights * (
            soft_grad - jnp.sum(soft_weights * soft_grad, axis=-1, keepdims=True)
        )
        score_grad = score_grad.astype(jnp.bfloat16)
        query_grad = (
            jnp.einsum("hqk,khd->qhd", score_grad, key_block, preferred_element_type=jnp.float32)
            * score_scale
        )
        key_part = (
            jnp.einsum("hqk,qhd->khd", score_grad, query_block, preferred_element_type=jnp.float32)
            * score_scale
        )
        value_part = jnp.einsum(
            "hqk,qhd->khd",
            soft_weights.astype(jnp.bfloat16),
            grad_block,
            preferred_element_type=jnp.float32,
        )
        key_grad = lax.dynamic_update_slice_in_dim(
            key_grad,
            lax.dynamic_slice_in_dim(key_grad, key_start, window_rows, 0) + key_part,
            key_start,
            0,
        )
        value_grad = lax.dynamic_update_slice_in_dim(
            value_grad,
            lax.dynamic_slice_in_dim(value_grad, key_start, window_rows, 0) + value_part,
            key_start,
            0,
        )
        return ((key_grad, value_grad), query_grad)

    zero_state = jnp.zeros(queries.shape, jnp.float32)
    (key_grad, value_grad), query_grads = lax.scan(
        one_block,
        (zero_state, zero_state),
        jnp.arange(stream_length // block_rows, dtype=jnp.int32),
    )
    return (query_grads.reshape(stream_length, head_count, head_size), key_grad, value_grad)


def on_device(
    layer_input,
    lengths,
    norm1_gain,
    qkv_weight,
    kernels,
    out_weight,
    out_bias,
    norm2_gain,
    up_weight,
    up_bias,
    down_weight,
    down_bias,
    out_grad,
):
    row_count = layer_input.shape[1]
    head_parts = lax.axis_size("head")
    stream_length = row_count * head_parts
    block_rows = min(512, stream_length)
    local_cols = qkv_weight.shape[2]
    local_heads = local_cols // HS
    document, position = sequence_layout(lengths[0], stream_length)
    own_input = layer_input[0]
    own_float = own_input.astype(jnp.float32)
    own_cotangent = out_grad[0]
    sent_rows = rms_norm(own_float, norm1_gain).astype(jnp.bfloat16)
    gathered = lax.all_gather(sent_rows, "head", axis=0, tiled=True)
    linear = jnp.einsum("td,jdc->jtc", gathered, qkv_weight, preferred_element_type=jnp.float32)

    def convolve(linear_in, kernel_in):
        return jnp.stack(
            [depthwise(linear_in[member], kernel_in[member], position) for member in range(3)]
        )

    convolved, conv_pull = jax.vjp(convolve, linear, kernels)
    conv_low = convolved.astype(jnp.bfloat16).reshape(3, stream_length, local_heads, HS)
    attended, log_mass = attention_forward(
        conv_low[0], conv_low[1], conv_low[2], document, position, block_rows
    )
    hidden_own = (
        own_float
        + lax.psum_scatter(
            jnp.dot(attended, out_weight, preferred_element_type=jnp.float32).astype(jnp.bfloat16),
            "head",
            scatter_dimension=0,
            tiled=True,
        ).astype(jnp.float32)
        + out_bias
    )
    normed_two = lax.all_gather(
        rms_norm(hidden_own, norm2_gain).astype(jnp.bfloat16), "head", axis=0, tiled=True
    )
    gate_value = jnp.dot(normed_two, up_weight, preferred_element_type=jnp.float32) + up_bias
    activation = jnp.square(jnp.maximum(gate_value, 0.0)).astype(jnp.bfloat16)
    output_rows = (
        hidden_own
        + lax.psum_scatter(
            jnp.dot(activation, down_weight, preferred_element_type=jnp.float32).astype(
                jnp.bfloat16
            ),
            "head",
            scatter_dimension=0,
            tiled=True,
        ).astype(jnp.float32)
        + down_bias
    )
    out_rows = output_rows.astype(jnp.bfloat16)[None]
    grad_full = lax.all_gather(own_cotangent, "head", axis=0, tiled=True)
    down_grad = jnp.einsum("tf,td->fd", activation, grad_full, preferred_element_type=jnp.float32)
    down_bias_grad = jnp.sum(own_cotangent.astype(jnp.float32), axis=0)
    act_grad = jnp.einsum("td,fd->tf", grad_full, down_weight, preferred_element_type=jnp.float32)
    gate_grad = (2.0 * jnp.maximum(gate_value, 0.0) * act_grad).astype(jnp.bfloat16)
    up_grad = jnp.einsum("td,tf->df", normed_two, gate_grad, preferred_element_type=jnp.float32)
    up_bias_grad = jnp.sum(gate_grad.astype(jnp.float32), axis=0)
    normed_grad = lax.psum_scatter(
        jnp.einsum("tf,df->td", gate_grad, up_weight, preferred_element_type=jnp.float32).astype(
            jnp.bfloat16
        ),
        "head",
        scatter_dimension=0,
        tiled=True,
    ).astype(jnp.float32)
    back_own, gain_rows = norm_backward(hidden_own, norm2_gain, normed_grad)
    hidden_grad_own = own_cotangent.astype(jnp.float32) + back_own
    own_low = hidden_grad_own.astype(jnp.bfloat16)
    hidden_low = lax.all_gather(own_low, "head", axis=0, tiled=True)
    gain_two_grad = jnp.sum(gain_rows, axis=0)
    out_bias_grad = jnp.sum(own_low.astype(jnp.float32), axis=0)
    out_weight_grad = jnp.einsum(
        "tc,td->cd", attended, hidden_low, preferred_element_type=jnp.float32
    )
    attended_grad = jnp.einsum(
        "td,cd->tc", hidden_low, out_weight, preferred_element_type=jnp.float32
    )
    attended_grad = attended_grad.astype(jnp.bfloat16).reshape(stream_length, local_heads, HS)
    query_grad, key_grad, value_grad = attention_backward(
        conv_low[0],
        conv_low[1],
        conv_low[2],
        attended_grad,
        log_mass,
        document,
        position,
        block_rows,
    )
    conv_grad = jnp.stack([query_grad, key_grad, value_grad]).reshape(3, stream_length, local_cols)
    linear_grad, kernel_grad = conv_pull(conv_grad)
    linear_low = linear_grad.astype(jnp.bfloat16)
    normed_back = lax.all_gather(sent_rows, "head", axis=0, tiled=True)
    qkv_grad = jnp.einsum(
        "td,jtc->jdc", normed_back, linear_low, preferred_element_type=jnp.float32
    )
    normed_one_grad = lax.psum_scatter(
        jnp.einsum(
            "jtc,jdc->td", linear_low, qkv_weight, preferred_element_type=jnp.float32
        ).astype(jnp.bfloat16),
        "head",
        scatter_dimension=0,
        tiled=True,
    ).astype(jnp.float32)
    back_in, gain_rows_one = norm_backward(own_float, norm1_gain, normed_one_grad)
    layer_grad = (hidden_grad_own + back_in).astype(jnp.bfloat16)[None]
    gain_one_grad = jnp.sum(gain_rows_one, axis=0)
    weight_sums = (
        lax.psum(qkv_grad.astype(jnp.bfloat16), ("batch", "dp")).astype(jnp.float32),
        lax.psum(kernel_grad.astype(jnp.bfloat16), ("batch", "dp")).astype(jnp.float32),
        lax.psum(out_weight_grad.astype(jnp.bfloat16), ("batch", "dp")).astype(jnp.float32),
        lax.psum(up_grad.astype(jnp.bfloat16), ("batch", "dp")).astype(jnp.float32),
        lax.psum(up_bias_grad.astype(jnp.bfloat16), ("batch", "dp")).astype(jnp.float32),
        lax.psum(down_grad.astype(jnp.bfloat16), ("batch", "dp")).astype(jnp.float32),
    )
    small_sums = lax.psum(
        (gain_one_grad, gain_two_grad, out_bias_grad, down_bias_grad), ("head", "batch", "dp")
    )
    return (
        out_rows,
        layer_grad,
        small_sums[0],
        weight_sums[0],
        weight_sums[1],
        weight_sums[2],
        small_sums[2],
        small_sums[1],
        weight_sums[3],
        weight_sums[4],
        weight_sums[5],
        small_sums[3],
    )


def solution(mesh):
    return jax.shard_map(
        on_device,
        mesh=mesh,
        in_specs=(
            P(("batch", "dp"), "head", None),
            P(("batch", "dp"), None),
            P(),
            P(None, None, "head"),
            P(None, None, "head"),
            P("head", None),
            P(),
            P(),
            P(None, "head"),
            P("head"),
            P("head", None),
            P(),
            P(("batch", "dp"), "head", None),
        ),
        out_specs=(
            P(("batch", "dp"), "head", None),
            P(("batch", "dp"), "head", None),
            P(),
            P(None, None, "head"),
            P(None, None, "head"),
            P("head", None),
            P(),
            P(),
            P(None, "head"),
            P("head"),
            P("head", None),
            P(),
        ),
        check_vma=False,
    )
```

profile of v0, /device:TPU:0, one launch (start us, length us, event | category | flops | bytes accessed | tf_op | source)
XLA Modules:
  0.0 2285.3 jit_solution(5492304788257533718)
XLA Ops:
  14.2 151.9 %all-gather.6.cloned.1.call-done = bf16[4096,1024]{1,0:T(8,128)(2,1)} async-done(((bf16[1024,1024]{1,0:T(8,128)(2,1)}), bf16[4096,1024]{1,0:T(8,128)(2,1)}) %all-gather.6.cloned.1.call-update) | async-done | bytes 8388624 | tf_op jit(solution)/shard_map/all_gather | solution.py:194
  216.6 155.0 %while.26 = (s32[]{:T(128)}, bf16[8,512,4,64]{1,3,2,0:T(8,128)(2,1)}, f32[8,4,512]{2,1,0:T(4,128)S(1)}, s32[8]{0:T(128)S(1)}, s32[4096]{0:T(1024)S(1)}, /*index=...) while((s32[]{:T(128)}, ...), condition=%wide.region_7.8_spmd, body=%wide.region_4.7_spmd.sunk | while | flops 1127350784 | bytes 65653048 | solution.py:95
  382.8 142.4 %reduce-scatter.5.cloned.1.call-done = bf16[1024,1024]{1,0:T(8,128)(2,1)} async-done(((bf16[4096,1024]{1,0:T(8,128)(2,1)}), bf16[1024,1024]{1,0:T(8,128)(2,1)}) %reduce-scatter.5.cloned.1.call-update) | async-done | bytes 2097168 | tf_op jit(solution)/shard_map/reduce_scatter | solution.py:209
  531.6 149.9 %all-gather.8.cloned.1.call-done = bf16[4096,1024]{1,0:T(8,128)(2,1)} async-done(((bf16[1024,1024]{1,0:T(8,128)(2,1)}), bf16[4096,1024]{1,0:T(8,128)(2,1)}) %all-gather.8.cloned.1.call-update) | async-done | bytes 8388624 | tf_op jit(solution)/shard_map/all_gather | solution.py:217
  681.5 16.1 fusion.107
  697.6 133.3 %all-gather.12.cloned.1.call-done = bf16[1,4096,1024]{2,1,0:T(8,128)(2,1)} async-done(((bf16[1,1024,1024]{2,1,0:T(8,128)(2,1)}), bf16[1,4096,1024]{2,1,0:T(8,128)(2,1)}) %all-gather.12.cloned.1.call-update) | async-done | bytes 8388624 | tf_op jit(solution)/shard_map/all_gather | solution.py:235
  830.8 19.4 fusion.106
  850.3 14.7 convolution_convert_fusion
  865.1 142.8 %reduce-scatter.9.cloned.1.call-done = bf16[1024,1024]{1,0:T(8,128)(2,1)} async-done(((bf16[4096,1024]{1,0:T(8,128)(2,1)}), bf16[1024,1024]{1,0:T(8,128)(2,1)}) %reduce-scatter.9.cloned.1.call-update) | async-done | bytes 2097168 | tf_op jit(solution)/shard_map/reduce_scatter | solution.py:242
  1019.8 15.0 convolution_convert_fusion.4
  1034.8 15.9 fusion.91
  1050.7 118.2 %all-gather.10.cloned.1.call-done = bf16[4096,1024]{1,0:T(8,128)(2,1)} async-done(((bf16[1024,1024]{1,0:T(8,128)(2,1)}), bf16[4096,1024]{1,0:T(8,128)(2,1)}) %all-gather.10.cloned.1.call-update) | async-done | bytes 8388624 | tf_op jit(solution)/shard_map/all_gather | solution.py:253
  1181.0 625.8 %while.27 = (s32[]{:T(128)}, f32[4096,4,64]{0,2,1:T(8,128)}, f32[4096,4,64]{0,2,1:T(8,128)}, f32[8,512,4,64]{1,3,2,0:T(8,128)}, s32[8]{0:T(128)S(1)}, /*index=5*...) while((s32[]{:T(128)}, f32[4096,4,64]{0,2,1:T(8,128)}, ...), condition=%wide.region_15.16_spmd, body=%wide.region_13.15_spmd.sunk | while | flops 2752119296 | bytes 248097216 | solution.py:160
  1216.5 13.0 multiply_reduce_fusion.11
  1295.3 13.0 multiply_reduce_fusion.11
  1373.8 13.0 multiply_reduce_fusion.11
  1608.9 13.0 multiply_reduce_fusion.11
  1836.3 17.8 multiply_reduce_fusion.2
  1872.4 14.7 bitcast_convert_fusion
  1887.8 17.6 convolution_convert_fusion.1
  1947.1 27.6 %all-reduce.32.cloned.1.call-done = (bf16[3,1024,256]{1,2,0:T(8,128)(2,1)}, bf16[256,1024]{1,0:T(8,128)(2,1)}, bf16[1024,1024]{1,0:T(8,128)(2,1)}, bf16[1024,1024]{1,0:T(8,128)(2,1)}) async-done(((bf16[3,1024,256]{1,2,0:T(8,128)(2,1)}, bf16[256,1024]{1,0:T(8,128)(2,1)}, bf16[1024,1024]{1,0:T(8,128)(2,1)}, bf16[1024,1024]{1,0:T(8,128)(2,1)}), (bf16[3,1024,256]{1,2,0:T(8,128)(2,1)}, ...) | async-done | bytes 6291472 | tf_op jit(solution)/shard_map/psum | solution.py:292
  1986.9 134.9 %reduce-scatter.11.cloned.1.call-done = bf16[1024,1024]{1,0:T(8,128)(2,1)} async-done(((bf16[4096,1024]{1,0:T(8,128)(2,1)}), bf16[1024,1024]{1,0:T(8,128)(2,1)}) %reduce-scatter.11.cloned.1.call-update) | async-done | bytes 2097168 | tf_op jit(solution)/shard_map/reduce_scatter | solution.py:280
  2125.5 46.2 %all-reduce.27 = (f32[1024]{0:T(1024)}, f32[1024]{0:T(1024)}, f32[1024]{0:T(1024)}, f32[1024]{0:T(1024)}) all-reduce(f32[1024]{0:T(1024)S(1)} %get-tuple-element.167, f32[1024]{0:T(1024)S(1)} %copy-done.42, f32[1024]{0:T(1024)S(1)} %copy-done.43, ...), channel_id=1, replica_groups=mesh['head'=4,'batch'=4,'dp'=2] {'head','batch','dp'}, use_global_device_ids=true, to_apply=%region_19.20 | all-reduce | flops 4096 | bytes 32768 | tf_op jit(solution)/shard_map/psum | solution.py:299
  2171.7 98.8 %reduce-scatter.7.cloned.1.call-done = bf16[1024,1024]{1,0:T(8,128)(2,1)} async-done(((bf16[4096,1024]{1,0:T(8,128)(2,1)}), bf16[1024,1024]{1,0:T(8,128)(2,1)}) %reduce-scatter.7.cloned.1.call-update) | async-done | bytes 2097168 | tf_op jit(solution)/shard_map/reduce_scatter | solution.py:224
  (503 shorter events, 903.1 us)
Async XLA Ops:
  7.2 823.6 %copy-start = (bf16[1024,1024]{1,0:T(8,128)(2,1)S(1)}, bf16[1024,1024]{1,0:T(8,128)(2,1)}, u32[]{:S(2)}) copy-start(bf16[1024,1024]{1,0:T(8,128)(2,1)} %param.27) | copy-start | bytes 6291460
  7.2 158.8 %all-gather.6.cloned.1.call-start = ((), (), s32[]{:S(2)}) async-start(), calls=%async_computation.4 | async-start | bytes 10485760 | tf_op jit(solution)/shard_map/all_gather | solution.py:194
  13.5 511.7 %reduce-scatter.5.cloned.1.call-start = ((), (), s32[]{:S(2)}) async-start(), calls=%async_computation.5 | async-start | bytes 10485760 | tf_op jit(solution)/shard_map/reduce_scatter | solution.py:209
  14.0 191.0 %copy-start.46 = (f32[1,1,256]{2,1,0:T(1,128)}, f32[1,1,256]{2,1,0:T(1,128)S(1)}, u32[]{:S(2)}) copy-start(f32[1,1,256]{2,1,0:T(1,128)S(1)} %get-tuple-element.256) | copy-start | bytes 3076
  14.0 191.0 %copy-start.48 = (f32[1,1,256]{2,1,0:T(1,128)}, f32[1,1,256]{2,1,0:T(1,128)S(1)}, u32[]{:S(2)}) copy-start(f32[1,1,256]{2,1,0:T(1,128)S(1)} %get-tuple-element.259) | copy-start | bytes 3076
  14.1 191.0 %copy-start.50 = (f32[1,1,256]{2,1,0:T(1,128)}, f32[1,1,256]{2,1,0:T(1,128)S(1)}, u32[]{:S(2)}) copy-start(f32[1,1,256]{2,1,0:T(1,128)S(1)} %get-tuple-element.257) | copy-start | bytes 3076
  14.1 191.0 %copy-start.52 = (f32[1,1,256]{2,1,0:T(1,128)}, f32[1,1,256]{2,1,0:T(1,128)S(1)}, u32[]{:S(2)}) copy-start(f32[1,1,256]{2,1,0:T(1,128)S(1)} %get-tuple-element.263) | copy-start | bytes 3076
  14.1 191.0 %copy-start.54 = (f32[1,1,256]{2,1,0:T(1,128)}, f32[1,1,256]{2,1,0:T(1,128)S(1)}, u32[]{:S(2)}) copy-start(f32[1,1,256]{2,1,0:T(1,128)S(1)} %get-tuple-element.258) | copy-start | bytes 3076
  14.1 191.0 %copy-start.56 = (f32[1,1,256]{2,1,0:T(1,128)}, f32[1,1,256]{2,1,0:T(1,128)S(1)}, u32[]{:S(2)}) copy-start(f32[1,1,256]{2,1,0:T(1,128)S(1)} %get-tuple-element.264) | copy-start | bytes 3076
  14.1 191.0 %copy-start.25 = (pred[4096]{0:T(1024)(128)(4,1)}, pred[4096]{0:T(1024)(128)(4,1)S(1)}, u32[]{:S(2)}) copy-start(pred[4096]{0:T(1024)(128)(4,1)S(1)} %get-tuple-element.254) | copy-start | bytes 12292
  382.4 299.1 %all-gather.8.cloned.1.call-start = ((), (), s32[]{:S(2)}) async-start(), calls=%async_computation.6 | async-start | bytes 10485760 | tf_op jit(solution)/shard_map/all_gather | solution.py:217
  528.7 484.6 %copy-start.31 = (f32[1024]{0:T(1024)}, f32[1024]{0:T(1024)S(1)}, u32[]{:S(2)}) copy-start(f32[1024]{0:T(1024)S(1)} %add_rsqrt_fusion) | copy-start | bytes 12292
  531.0 299.8 %all-gather.12.cloned.1.call-start = ((), (), s32[]{:S(2)}) async-start(), calls=%async_computation.11 | async-start | bytes 10485760 | tf_op jit(solution)/shard_map/all_gather | solution.py:235
  531.6 299.3 %copy-start.68 = (f32[1024]{0:T(1024)S(1)}, f32[1024]{0:T(1024)}, u32[]{:S(2)}) copy-start(f32[1024]{0:T(1024)} %param.26) | copy-start | bytes 12292
  531.6 476.3 %reduce-scatter.9.cloned.1.call-start = ((), (), s32[]{:S(2)}) async-start(), calls=%async_computation.8 | async-start | bytes 10485760 | tf_op jit(solution)/shard_map/reduce_scatter | solution.py:242
  865.0 303.9 %all-gather.10.cloned.1.call-start = ((), (), s32[]{:S(2)}) async-start(), calls=%async_computation.9 | async-start | bytes 10485760 | tf_op jit(solution)/shard_map/all_gather | solution.py:253
  1018.4 956.4 %all-reduce.32.cloned.1.call-start = ((), (), s32[]{:S(2)}) async-start(), calls=%async_computation.12 | async-start | bytes 12582912 | tf_op jit(solution)/shard_map/psum | solution.py:292
  1872.4 249.5 %reduce-scatter.11.cloned.1.call-start = ((), (), s32[]{:S(2)}) async-start(), calls=%async_computation.10 | async-start | bytes 10485760 | tf_op jit(solution)/shard_map/reduce_scatter | solution.py:280
  1887.1 383.4 %reduce-scatter.7.cloned.1.call-start = ((), (), s32[]{:S(2)}) async-start(), calls=%async_computation.7 | async-start | bytes 10485760 | tf_op jit(solution)/shard_map/reduce_scatter | solution.py:224
  1984.4 286.1 %copy-start.32 = (f32[1024]{0:T(1024)S(1)}, f32[1024]{0:T(1024)}, u32[]{:S(2)}) copy-start(f32[1024]{0:T(1024)} %copy-done.31) | copy-start | bytes 12292
  1984.4 286.1 %copy-start.34 = (f32[1024]{0:T(1024)S(1)}, f32[1024]{0:T(1024)}, u32[]{:S(2)}) copy-start(f32[1024]{0:T(1024)} %param.23) | copy-start | bytes 12292
  1984.4 286.1 %copy-start.36 = (f32[1024]{0:T(1024)S(1)}, f32[1024]{0:T(1024)}, u32[]{:S(2)}) copy-start(f32[1024]{0:T(1024)} %param.24) | copy-start | bytes 12292
  1984.4 286.1 %copy-start.40 = (f32[1024]{0:T(1024)S(1)}, f32[1024]{0:T(1024)}, u32[]{:S(2)}) copy-start(f32[1024]{0:T(1024)} %copy-done.39) | copy-start | bytes 12292
  1984.4 286.1 %copy-start.65 = (f32[1024]{0:T(1024)S(1)}, f32[1024]{0:T(1024)}, u32[]{:S(2)}) copy-start(f32[1024]{0:T(1024)} %param.28) | copy-start | bytes 12292
  (91 other events, 2141.9 us)
Sparse Core Ops, SparseCore 0:
  13.7 152.3 all-gather.5
  382.5 142.6 reduce-scatter.4
  531.1 150.3 all-gather.7
  682.9 147.8 all-gather.11
  865.2 142.6 reduce-scatter.8
  1018.5 150.3 all-gather.9
  1872.5 102.2 all-reduce.31
  1977.3 144.5 reduce-scatter.10
  2124.3 146.1 reduce-scatter.6
where the time goes:
time: 2300 us; the launch traced here: 2290 us
  waiting for transfers between devices  1100 us (48%)
  matrix products  507 us (22%)
  local copies, waits for them, and re-layouts  297 us (13%)
  other arithmetic  268 us (12%)
  blocking collectives  58.7 us (3%)
  loops' own time  38.1 us (2%)
    all_gather x1, waiting for transfers between devices, on_device(): gathered = lax.all_gather(sent_rows, 'head', axis=0, tiled=True)  152 us
    all_gather x1, waiting for transfers between devices, on_device(): lax.all_gather(rms_norm(hidden_own, norm2_gain).astype(jnp.bfloat16), 'he...  150 us
    reduce_scatter x1, waiting for transfers between devices, on_device(): lax.psum_scatter(jnp.einsum('tf,df->td', gate_grad, up_weight, preferred_...  143 us
    reduce_scatter x1, waiting for transfers between devices, on_device(): lax.psum_scatter(jnp.dot(attended, out_weight, preferred_element_type=jnp...  142 us
    reduce_scatter x1, waiting for transfers between devices, on_device(): lax.psum_scatter(jnp.einsum('jtc,jdc->td', linear_low, qkv_weight, prefer...  135 us
    all_gather x1, waiting for transfers between devices, on_device(): grad_full = lax.all_gather(own_cotangent, 'head', axis=0, tiled=True)  133 us
    all_gather x1, waiting for transfers between devices, on_device(): hidden_low = lax.all_gather(own_low, 'head', axis=0, tiled=True)  118 us
    dot_general x8, matrix products, one_block(): jnp.einsum('qhd,khd->hqk', grad_block, value_block, preferred_element_typ...  104 us
  transfers between devices with their start and end apart: 9, of which 9 were waited for; matrix products, arithmetic and copies ran while one was open for 6% of the time, Pallas kernels for 0%

commit v1 on v0

v1 whole, which is shorter than its diff:
```python
import functools, math
import jax, jax.numpy as jnp
from jax import lax
from jax.sharding import PartitionSpec as P
from jax.experimental import pallas as pl
from jax.experimental.pallas import tpu as pltpu

HS = 64
LONG = 2048
LANES = 128
LOG2E = math.log2(math.e)
LN2 = math.log(2.0)
NT = (((1,), (1,)), ((), ()))
NN = (((1,), (0,)), ((), ()))


def dot(a, b, dims=NN):
    return lax.dot_general(a, b, dims, preferred_element_type=jnp.float32)


def spans(first, last, step):
    return [(at, min(step, last - at)) for at in range(first, last, step)]


def forward_kernel(before_ref, q_ref, k_ref, v_ref, out_ref, mass_ref, s0_ref, s1_ref, *, shards, bq, kc):
    rows = q_ref.shape[0]
    own = (shards - 1) * rows
    lane = lax.broadcasted_iota(jnp.int32, (bq, LANES), 1) < HS
    scale = 1.0 / math.sqrt(HS)

    def block(at, first):
        query = q_ref[pl.ds(at, bq), :] * jnp.bfloat16(scale)
        zero = jnp.zeros_like(query)
        queries = (jnp.where(lane, query, zero), jnp.where(lane, zero, query))
        stores = (s0_ref, s1_ref)
        peaks = [None, None]
        parts = spans(first, own + at, kc) + [(own + at, bq)]
        for start, size in parts:
            key = k_ref[pl.ds(start, size), :]
            for h in range(2):
                s = dot(queries[h], key, NT)
                if start == own + at:
                    row = lax.broadcasted_iota(jnp.int32, (bq, size), 0)
                    col = lax.broadcasted_iota(jnp.int32, (bq, size), 1)
                    s = jnp.where(col <= row, s, -1e30)
                stores[h][:, pl.ds(start, size)] = s
                top = jnp.max(s, axis=1, keepdims=True)
                peaks[h] = top if peaks[h] is None else jnp.maximum(peaks[h], top)
        sums = [None, None]
        scaled = [peak * LOG2E for peak in peaks]
        for start, size in parts:
            value = v_ref[pl.ds(start, size), :]
            wide = lax.broadcasted_iota(jnp.int32, (size, LANES), 1) < HS
            one = jnp.ones_like(value)
            values = (jnp.where(wide, value, one), jnp.where(wide, one, value))
            for h in range(2):
                p = jnp.exp2(stores[h][:, pl.ds(start, size)] * LOG2E - scaled[h]).astype(jnp.bfloat16)
                o = dot(p, values[h])
                sums[h] = o if sums[h] is None else sums[h] + o
        total = pltpu.roll(jnp.where(lane, sums[1], sums[0]), HS, 1)
        out_ref[pl.ds(at, bq), :] = (jnp.where(lane, sums[0], sums[1]) / total).astype(out_ref.dtype)
        mass = jnp.where(lane, peaks[0], peaks[1]) + jnp.log(total)
        mass = mass.T
        mass_ref[0, 0:1, pl.ds(at, bq)] = mass[0:1]
        mass_ref[0, 1:2, pl.ds(at, bq)] = mass[HS:HS + 1]

    for before in range(shards):
        @pl.when(before_ref[0] == before)
        def _():
            for at in range(0, rows, bq):
                block(at, own - before * rows)


def attention_forward(before, queries, key_rows, values):
    rows, width = queries.shape
    window = key_rows.shape[0]
    shards = window // rows
    pairs = width // LANES
    bq = min(256, rows)
    column = lambda n: pl.BlockSpec((n, LANES), lambda i, b: (0, i))
    return pl.pallas_call(
        functools.partial(forward_kernel, shards=shards, bq=bq, kc=512),
        out_shape=(jax.ShapeDtypeStruct((rows, width), jnp.bfloat16), jax.ShapeDtypeStruct((pairs, 8, rows), jnp.float32)),
        grid_spec=pltpu.PrefetchScalarGridSpec(
            num_scalar_prefetch=1, grid=(pairs,),
            in_specs=[column(rows), column(window), column(window)],
            out_specs=[column(rows), pl.BlockSpec((1, 8, rows), lambda i, b: (i, 0, 0))],
            scratch_shapes=[pltpu.VMEM((bq, window), jnp.float32)] * 2,
        ),
        compiler_params=pltpu.CompilerParams(vmem_limit_bytes=48 << 20),
    )(before, queries, key_rows, values)


def backward_kernel(before_ref, q_ref, k_ref, v_ref, g_ref, o_ref, mass_ref, dq_ref, dk_ref, dv_ref, kt_ref, *, shards, bq, kc):
    rows = q_ref.shape[0]
    window = k_ref.shape[0]
    own = window - rows
    lane = lax.broadcasted_iota(jnp.int32, (bq, LANES), 1) < HS
    scale = 1.0 / math.sqrt(HS)
    dk_ref[...] = jnp.zeros_like(dk_ref)
    dv_ref[...] = jnp.zeros_like(dv_ref)
    kt_ref[...] = k_ref[...].astype(jnp.float32).T.astype(jnp.bfloat16)

    def block(at, first):
        query = q_ref[pl.ds(at, bq), :] * jnp.bfloat16(scale)
        grad = g_ref[pl.ds(at, bq), :]
        zero = jnp.zeros_like(query)
        queries = (jnp.where(lane, query, zero), jnp.where(lane, zero, query))
        grads = (jnp.where(lane, grad, zero), jnp.where(lane, zero, grad))
        product = (grad.astype(jnp.float32) * o_ref[pl.ds(at, bq), :].astype(jnp.float32)).T
        query_grads = [jnp.zeros((HS, bq), jnp.float32)] * 2
        deltas = [jnp.sum(product[h * HS:(h + 1) * HS], axis=0, keepdims=True) for h in range(2)]
        masses = [mass_ref[0, h:h + 1, pl.ds(at, bq)] * LOG2E for h in range(2)]
        parts = spans(first, own + at, kc) + [(own + at, bq)]
        for start, size in parts:
            key = k_ref[pl.ds(start, size), :]
            value = v_ref[pl.ds(start, size), :]
            key_part = value_part = None
            for h in range(2):
                s = dot(key, queries[h], NT)
                if start == own + at:
                    row = lax.broadcasted_iota(jnp.int32, (size, bq), 1)
                    col = lax.broadcasted_iota(jnp.int32, (size, bq), 0)
                    s = jnp.where(col <= row, s, -1e30)
                p = jnp.exp2(s * LOG2E - masses[h])
                dp = dot(value, grads[h], NT)
                ds = (p * (dp - deltas[h])).astype(jnp.bfloat16)
                a = dot(p.astype(jnp.bfloat16), grads[h])
                b = dot(ds, queries[h])
                value_part = a if value_part is None else value_part + a
                key_part = b if key_part is None else key_part + b
                query_grads[h] += dot(kt_ref[h * HS:(h + 1) * HS, pl.ds(start, size)], ds)
            dk_ref[pl.ds(start, size), :] += key_part
            dv_ref[pl.ds(start, size), :] += value_part
        dq_ref[pl.ds(at, bq), :] = jnp.concatenate(query_grads, axis=0).T * scale

    for before in range(shards):
        @pl.when(before_ref[0] == before)
        def _():
            for at in range(0, rows, bq):
                block(at, own - before * rows)


def attention_backward(before, queries, key_rows, values, grads, outs, mass):
    rows, width = queries.shape
    window = key_rows.shape[0]
    shards = window // rows
    pairs = width // LANES
    bq = min(256, rows)
    column = lambda n: pl.BlockSpec((n, LANES), lambda i, b: (0, i))
    return pl.pallas_call(
        functools.partial(backward_kernel, shards=shards, bq=bq, kc=256),
        out_shape=(jax.ShapeDtypeStruct((rows, width), jnp.float32), jax.ShapeDtypeStruct((window, width), jnp.float32), jax.ShapeDtypeStruct((window, width), jnp.float32)),
        grid_spec=pltpu.PrefetchScalarGridSpec(
            num_scalar_prefetch=1, grid=(pairs,),
            in_specs=[column(rows), column(window), column(window), column(rows), column(rows), pl.BlockSpec((1, 8, rows), lambda i, b: (i, 0, 0))],
            out_specs=[column(rows), column(window), column(window)],
            scratch_shapes=[pltpu.VMEM((LANES, window), jnp.bfloat16)],
        ),
        compiler_params=pltpu.CompilerParams(vmem_limit_bytes=48 << 20),
    )(before, queries, key_rows, values, grads, outs, mass)

EPSILON = 1e-06
ALL = ("head", "batch", "dp")


def factor_of(values):
    return lax.rsqrt(jnp.mean(values * values, axis=-1, keepdims=True) + EPSILON)


def norm_backward(values, gain, upstream):
    factor = factor_of(values)
    unit = values * factor
    scaled = gain * upstream
    result = factor * (scaled - unit * jnp.mean(scaled * unit, axis=-1, keepdims=True))
    return result, upstream * unit


def back(values, offset):
    if offset == 0:
        return values
    return jnp.pad(values[:-offset], ((offset, 0), (0, 0)))


def ahead(values, offset):
    if offset == 0:
        return values
    return jnp.pad(values[offset:], ((0, offset), (0, 0)))


def nt(a, b):
    return lax.dot_general(a, b, NT, preferred_element_type=jnp.float32)


def nn(a, b):
    return lax.dot_general(a, b, NN, preferred_element_type=jnp.float32)


def tn(a, b):
    return lax.dot_general(a, b, (((0,), (0,)), ((), ())), preferred_element_type=jnp.float32)


def on_device(
    layer_input, lengths, norm1_gain, qkv_weight, kernels, out_weight, out_bias,
    norm2_gain, up_weight, up_bias, down_weight, down_bias, out_grad,
):
    rows = layer_input.shape[1]
    parts = lax.axis_size("head")
    copies = lax.axis_size("batch") * lax.axis_size("dp")
    shards = max(1, LONG // rows)
    place = lax.axis_index("head")
    mine = lax.axis_index("batch") * lax.axis_size("dp") + lax.axis_index("dp")
    width = qkv_weight.shape[1]

    first_row = place * rows
    ends = jnp.cumsum(lengths[0])
    begins = jnp.max(jnp.where(ends <= first_row, ends, 0))
    before = ((first_row - begins) // rows).astype(jnp.int32)

    def gathered(weight):
        share = weight.shape[-2] // copies
        piece = lax.dynamic_slice_in_dim(weight, mine * share, share, weight.ndim - 2)
        return lax.all_gather(piece, ALL, axis=weight.ndim - 2, tiled=True)

    def reduced(grad):
        axis = grad.ndim - 2
        piece = lax.psum_scatter(grad.astype(jnp.bfloat16), ALL, scatter_dimension=axis, tiled=True)
        return lax.all_gather(piece, ("batch", "dp"), axis=axis, tiled=True).astype(jnp.float32)

    qkv_rows = gathered(qkv_weight.transpose(0, 2, 1))
    out_rows = gathered(out_weight)
    up_rows = gathered(up_weight.T)
    down_rows = gathered(down_weight)
    kernel_all = lax.all_gather(kernels, "head", axis=2, tiled=True)
    up_bias_all = lax.all_gather(up_bias, "head", axis=0, tiled=True)

    own_float = layer_input[0].astype(jnp.float32)
    cotangent = out_grad[0]
    own_factor = factor_of(own_float)
    normed_own = (own_float * own_factor * norm1_gain).astype(jnp.bfloat16)
    pieces = [normed_own]
    for hop in range(1, shards):
        came = lax.ppermute(normed_own, "head", [(i, i + hop) for i in range(parts - hop)])
        pieces.insert(0, jnp.where(before >= hop, came, jnp.zeros_like(came)))
    window = jnp.concatenate(pieces, axis=0)
    window_rows = shards * rows
    edge = 16 if shards > 1 else 0
    late = window[window_rows - rows - edge:]

    linear = [nt(late, qkv_rows[0]).astype(jnp.bfloat16)] + [nt(window, qkv_rows[j]).astype(jnp.bfloat16) for j in (1, 2)]

    def convolve(j):
        values = linear[j].astype(jnp.float32)
        return sum(kernel_all[j, i] * back(values, i) for i in range(3)).astype(jnp.bfloat16)

    queries, key_rows, values = convolve(0)[edge:], convolve(1), convolve(2)
    attended, mass = attention_forward(before[None], queries, key_rows, values)
    hidden = own_float + nn(attended, out_rows) + out_bias
    normed_two = (hidden * factor_of(hidden) * norm2_gain).astype(jnp.bfloat16)
    gate = jnp.maximum(nt(normed_two, up_rows) + up_bias_all, 0.0)
    activation = jnp.square(gate).astype(jnp.bfloat16)
    gate_low = gate.astype(jnp.bfloat16)
    layer_output = (hidden + nn(activation, down_rows) + down_bias).astype(jnp.bfloat16)

    gate_grad = (2.0 * gate_low.astype(jnp.float32) * nt(cotangent, down_rows)).astype(jnp.bfloat16)
    down_grad = reduced(tn(activation, cotangent))
    up_grad = reduced(tn(gate_grad, normed_two)).T
    down_bias_grad = jnp.sum(cotangent.astype(jnp.float32), axis=0)
    up_bias_grad = jnp.sum(gate_grad.astype(jnp.float32), axis=0)
    normed_two_grad = nn(gate_grad, up_rows)
    back_two, gain_rows = norm_backward(hidden, norm2_gain, normed_two_grad)
    hidden_grad = cotangent.astype(jnp.float32) + back_two
    hidden_low = hidden_grad.astype(jnp.bfloat16)
    gain_two_grad = jnp.sum(gain_rows, axis=0)
    out_bias_grad = jnp.sum(hidden_low.astype(jnp.float32), axis=0)
    out_weight_grad = reduced(tn(attended, hidden_low))
    attended_grad = nt(hidden_low, out_rows).astype(jnp.bfloat16)

    conv_grad = attention_backward(before[None], queries, key_rows, values, attended_grad, attended, mass)
    conv_grad = [jnp.pad(conv_grad[0], ((edge, 0), (0, 0)))] + list(conv_grad[1:])
    kernels_grad = jnp.stack([
        jnp.stack([jnp.sum(conv_grad[j] * back(linear[j].astype(jnp.float32), i), axis=0) for i in range(3)])
        for j in range(3)
    ])
    linear_grad = [
        sum(kernel_all[j, i] * ahead(conv_grad[j], i) for i in range(3)).astype(jnp.bfloat16) for j in range(3)
    ]
    inputs = (late, window, window)
    qkv_grad = reduced(jnp.stack([tn(linear_grad[j], inputs[j]) for j in range(3)])).transpose(0, 2, 1)
    normed_grad = nn(linear_grad[1], qkv_rows[1]) + nn(linear_grad[2], qkv_rows[2])
    query_part = nn(linear_grad[0], qkv_rows[0])
    normed_grad = normed_grad + jnp.pad(query_part, ((window_rows - rows - edge, 0), (0, 0)))
    normed_own_grad = normed_grad[window_rows - rows:]
    for hop in range(1, shards):
        at = window_rows - (hop + 1) * rows
        part = normed_grad[at:at + rows].astype(jnp.bfloat16)
        part = jnp.where(before >= hop, part, jnp.zeros_like(part))
        came = lax.ppermute(part, "head", [(i + hop, i) for i in range(parts - hop)])
        normed_own_grad = normed_own_grad + came.astype(jnp.float32)
    back_one, gain_rows_one = norm_backward(own_float, norm1_gain, normed_own_grad)
    layer_grad = (hidden_grad + back_one).astype(jnp.bfloat16)
    gain_one_grad = jnp.sum(gain_rows_one, axis=0)

    gain_one_grad, gain_two_grad, out_bias_grad, down_bias_grad, up_bias_grad, kernels_grad = lax.psum(
        (gain_one_grad, gain_two_grad, out_bias_grad, down_bias_grad, up_bias_grad, kernels_grad), ALL
    )
    up_bias_grad = lax.dynamic_slice_in_dim(up_bias_grad, place * up_bias.shape[0], up_bias.shape[0], 0)
    kernels_grad = lax.dynamic_slice_in_dim(kernels_grad, place * kernels.shape[2], kernels.shape[2], 2)
    return (
        layer_output[None], layer_grad[None], gain_one_grad, qkv_grad, kernels_grad, out_weight_grad,
        out_bias_grad, gain_two_grad, up_grad, up_bias_grad, down_grad, down_bias_grad,
    )


def solution(mesh):
    rows = P(("batch", "dp"), "head", None)
    return jax.shard_map(
        on_device,
        mesh=mesh,
        in_specs=(
            rows, P(("batch", "dp"), None), P(), P(None, None, "head"), P(None, None, "head"), P("head", None), P(),
            P(), P(None, "head"), P("head"), P("head", None), P(), rows,
        ),
        out_specs=(
            rows, rows, P(), P(None, None, "head"), P(None, None, "head"), P("head", None),
            P(), P(), P(None, "head"), P("head"), P("head", None), P(),
        ),
        check_vma=False,
    )
```

time: 2300 us -> 1480 us (0.64)
  matrix products: 507 us -> 177 us
  local copies, waits for them, and re-layouts: 297 us -> 74.9 us
  other arithmetic: 268 us -> 89.8 us
  waiting for transfers between devices: 1100 us -> 925 us
  Pallas kernels: 0 us -> 70.7 us
  blocking collectives: 58.7 us -> 110 us
  loops' own time: 38.1 us -> 0 us
    all_gather x4 -> x7, waiting for transfers between devices: 553 us -> 158 us  [the longest x4 107 us: gathered(): return lax.all_gather(piece, ALL, axis=weight.ndim - 2, tiled=True)]
    dot_general x68 -> x18, matrix products: 507 us -> 177 us  [the longest x6 61.7 us: tn(): lax.dot_general(a, b, (((0,), (0,)), ((), ())), preferred_element_type=jn...]
    dynamic_update_slice x16 -> x0, local copies, waits for them, and re-layouts: 169 us -> none  [the longest x8 85 us: one_block(): lax.dynamic_update_slice_in_dim(value_grad, lax.dynamic_slice_in_dim(valu...]
    all_gather x0 -> x3, blocking collectives: none -> 110 us  [the longest x1 80.5 us: on_device(): up_bias_all = lax.all_gather(up_bias, 'head', axis=0, tiled=True)]
    convert_element_type x16 -> x5, other arithmetic: 114 us -> 28.5 us  [the longest x2 21.4 us: convolve(): sum((kernel_all[j, i] * back(values, i) for i in range(3)))]
    psum x1, waiting for transfers between devices: 27.6 us -> 110 us  [on_device(): lax.psum((gain_one_grad, gain_two_grad, out_bias_grad, down_bias_grad, up...]
    reduce_scatter x4, waiting for transfers between devices: 519 us -> 598 us  [reduced(): lax.psum_scatter(grad.astype(jnp.bfloat16), ALL, scatter_dimension=axis,...]
    pallas_call x0 -> x2, Pallas kernels: none -> 70.7 us  [the longest x1 47.2 us: attention_backward(): pl.pallas_call(functools.partial(backward_kernel, shards=shards, bq=bq, k...]
  transfers between devices with their start and end apart: 9 -> 14, of which waited for: 9 -> 11; matrix products, arithmetic and copies ran while one was open for 6% -> 13% of each run, Pallas kernels for 0% -> 2%
where the time goes in v1:
time: 1480 us; the launch traced here: 1470 us
  waiting for transfers between devices  925 us (62%)
  matrix products  177 us (12%)
  blocking collectives  110 us (7%)
  other arithmetic  89.8 us (6%)
  local copies, waits for them, and re-layouts  74.9 us (5%)
  Pallas kernels  70.7 us (5%)
  between operations  15.7 us (1%)
    reduce_scatter x4, waiting for transfers between devices, reduced(): lax.psum_scatter(grad.astype(jnp.bfloat16), ALL, scatter_dimension=axis,...  598 us
    psum x1, waiting for transfers between devices, on_device(): lax.psum((gain_one_grad, gain_two_grad, out_bias_grad, down_bias_grad, up...  110 us
    all_gather x4, waiting for transfers between devices, gathered(): return lax.all_gather(piece, ALL, axis=weight.ndim - 2, tiled=True)  107 us
    all_gather x1, blocking collectives, on_device(): up_bias_all = lax.all_gather(up_bias, 'head', axis=0, tiled=True)  80.5 us
    dot_general x6, matrix products, tn(): lax.dot_general(a, b, (((0,), (0,)), ((), ())), preferred_element_type=jn...  61.7 us
    dot_general x6, matrix products, nn(): return lax.dot_general(a, b, NN, preferred_element_type=jnp.float32)  60.5 us
    ppermute x1, waiting for transfers between devices, on_device(): lax.ppermute(part, 'head', [(i + hop, i) for i in range(parts - hop)])  59.2 us
    dot_general x6, matrix products, nt(): return lax.dot_general(a, b, NT, preferred_element_type=jnp.float32)  54.9 us
  transfers between devices with their start and end apart: 14, of which 11 were waited for; matrix products, arithmetic and copies ran while one was open for 13% of the time, Pallas kernels for 2%

profile of v1, /device:TPU:0, one launch (start us, length us, event | category | flops | bytes accessed | tf_op | source)
XLA Modules:
  0.0 1471.8 jit_solution(18126246508011731786)
XLA Ops:
  25.9 80.5 %all_gather.34 = f32[4096]{0:T(1024)S(1)} all-gather(f32[1024]{0:T(1024)S(1)} %copy-done.36), channel_id=1, replica_groups=mesh['head'=4,'batch'=4,'dp'=2] {'head'}, dimensions={0}, use_global_device_ids=true | all-gather | bytes 20480 | tf_op jit(solution)/shard_map/all_gather | solution.py:235
  106.4 13.2 all_gather.30
  158.8 19.7 %add_convert_fusion.2 = (bf16[2048,1024]{1,0:T(8,128)(2,1)}, bf16[2048,1024]{1,0:T(8,128)(2,1)}) fusion(f32[2046,1024]{1,0:T(8,128)} %slice.149, f32[2047,1024]{1,0:T(8,128)} %slice.147, f32[1024]{0:T(1024)S(1)} %bitcast.112, f32[1024]{0:T(1024)S(1)} %bitcast.114, bf16[2048,1024]{1,0:T(8,128)(2,1)} %copy-done.5, f32[1024]{0:T(1024)S(1)} %bitcast.110, ...), kind=kLoop, calls=%fused_computation.15 | loop fusion | flops 29360128 | bytes 50331648 | tf_op jit(solution)/shard_map/convert_element_type | solution.py:254
  178.5 23.5 %shard_map.220 = (bf16[1024,1024]{1,0:T(8,128)(2,1)S(1)}, f32[8,8,1024]{2,1,0:T(8,128)S(1)}) custom-call(s32[1]{0:T(128)} %bitcast.3.before_ref, bf16[1024,1024]{1,0:T(8,128)(2,1)S(1)} %fusion.16.q_ref, bf16[2048,1024]{1,0:T(8,128)(2,1)} %get-tuple-element.86.k_ref, bf16[2048,1024]{1,0:T(8,128)(2,1)} %get-tuple-element.85.v_ref), custom_call_target="tpu_custom_call" | custom-call | tf_op jit(solution)/shard_map/pallas_call | solution.py:81
  210.7 43.8 %all-gather.12.cloned.1.call-done = bf16[4096,1024]{0,1:T(8,128)(2,1)} async-done(((bf16[128,1024]{0,1:T(8,128)(2,1)}), bf16[4096,1024]{0,1:T(8,128)(2,1)}) %all-gather.12.cloned.1.call-update) | async-done | bytes 8388624 | tf_op jit(solution)/shard_map/all_gather | solution.py:223
  254.6 16.3 %fusion.33 = f32[1024,4096]{1,0:T(8,128)} fusion(bf16[4096,1024]{0,1:T(8,128)(2,1)} %all-gather.12.cloned.1.call-done, f32[1024,1024]{1,0:T(8,128)} %get-tuple-element.81, f32[1024]{0:T(1024)S(1)} %copy-done.35, f32[1024]{0:T(1024)S(1)} %add_rsqrt_fusion), kind=kOutput, calls=%fused_computation.103 | convolution fusion | flops 8593080320 | bytes 29368320 | tf_op jit(solution)/shard_map/dot_general | solution.py:192
  270.9 62.7 %all-gather.14.cloned.1.call-done = bf16[4096,1024]{1,0:T(8,128)(2,1)} async-done(((bf16[128,1024]{1,0:T(8,128)(2,1)}), bf16[4096,1024]{1,0:T(8,128)(2,1)}) %all-gather.14.cloned.1.call-update) | async-done | bytes 8388624 | tf_op jit(solution)/shard_map/all_gather | solution.py:223
  333.6 18.0 %convert_reduce_fusion = (f32[4096]{0:T(1024)}, bf16[1024,4096]{1,0:T(8,128)(2,1)}) fusion(bf16[4096,1024]{1,0:T(8,128)(2,1)} %all-gather.14.cloned.1.call-done, bf16[1,1024,1024]{2,1,0:T(8,128)(2,1)} %param.25, f32[1024,4096]{1,0:T(8,128)} %fusion.33, f32[4096]{0:T(1024)S(1)} %all_gather.34), kind=kOutput, calls=%fused_computation.2 | convolution fusion | flops 8627679232 | bytes 35684352 | tf_op jit(solution)/shard_map/dot_general | solution.py:192
  351.7 15.0 %multiply_reduce_fusion.9 = (f32[1024]{0:T(1024)}, f32[1024]{0:T(1024)S(1)}, f32[1024,1024]{1,0:T(8,128)S(1)}) fusion(f32[1024,1024]{1,0:T(8,128)S(1)} %copy-done.19, f32[1024]{0:T(1024)S(1)} %add_rsqrt_fusion, f32[1024]{0:T(1024)S(1)} %copy-done.35, bf16[1024,4096]{1,0:T(8,128)(2,1)} %get-tuple-element.84, bf16[4096,1024]{0,1:T(8,128)(2,1)} %all-gather.12.cloned.1.call-done), kind=kOutput, calls=%fused_computation.52 | convolution fusion | flops 8596224000 | bytes 25182208 | tf_op jit(solution)/shard_map/dot_general | solution.py:196
  371.4 47.2 %shard_map.221 = (f32[1024,1024]{1,0:T(8,128)}, f32[2048,1024]{1,0:T(8,128)}, f32[2048,1024]{1,0:T(8,128)}) custom-call(s32[1]{0:T(128)} %bitcast.3.before_ref, bf16[1024,1024]{1,0:T(8,128)(2,1)S(1)} %fusion.16.q_ref, bf16[2048,1024]{1,0:T(8,128)(2,1)} %get-tuple-element.86.k_ref, bf16[2048,1024]{1,0:T(8,128)(2,1)} %get-tuple-element.85.v_ref, ...), custom_call_target="tpu_custom_call" | custom-call | tf_op jit(solution)/shard_map/pallas_call | solution.py:151
  462.7 16.0 %multiply_reduce_fusion.5 = (f32[1024]{0:T(1024)S(1)}, f32[1024]{0:T(1024)S(1)}, f32[1024]{0:T(1024)S(1)}, bf16[2048,1024]{1,0:T(8,128)(2,1)S(1)}) fusion(f32[2048,1024]{1,0:T(8,128)} %get-tuple-element.19, bf16[2048,1024]{1,0:T(8,128)(2,1)S(1)} %copy-done.8, f32[2046,1024]{1,0:T(8,128)} %slice.143, f32[2047,1024]{1,0:T(8,128)} %slice.141, ...), kind=kLoop, calls=%fused_computation.11 | loop fusion | flops 27259904 | bytes 50331648 | tf_op jit(solution)/shard_map/reduce_sum | solution.py:282
  488.2 15.7 %multiply_reduce_fusion.2 = (f32[1024]{0:T(1024)S(1)}, f32[1024]{0:T(1024)S(1)}, f32[1024]{0:T(1024)S(1)}, bf16[2048,1024]{1,0:T(8,128)(2,1)}) fusion(f32[2048,1024]{1,0:T(8,128)} %get-tuple-element.20, bf16[2048,1024]{1,0:T(8,128)(2,1)S(1)} %copy-done.6, f32[2046,1024]{1,0:T(8,128)S(1)} %bitcast.104, f32[2047,1024]{1,0:T(8,128)} %slice.147, ...), kind=kLoop, calls=%fused_computation.8 | loop fusion | flops 27259904 | bytes 50331648 | tf_op jit(solution)/shard_map/reduce_sum | solution.py:282
  514.8 15.8 %convolution_convert_fusion.1 = bf16[4096,1024]{1,0:T(8,128)(2,1)} fusion(bf16[1024,4096]{1,0:T(8,128)(2,1)} %get-tuple-element.84, f32[1024,1024]{1,0:T(8,128)} %get-tuple-element.81, f32[1024]{0:T(1024)S(1)} %copy-done.35, f32[1024]{0:T(1024)S(1)} %add_rsqrt_fusion), kind=kOutput, calls=%fused_computation.18 | convolution fusion | flops 8597274624 | bytes 20979712 | tf_op jit(solution)/shard_map/dot_general | solution.py:200
  532.1 17.0 %convolution_convert_fusion = bf16[4096,1024]{1,0:T(8,128)(2,1)} fusion(bf16[1,1024,1024]{2,1,0:T(8,128)(2,1)S(1)} %copy-done.25, f32[1024,4096]{1,0:T(8,128)} %fusion.33, f32[4096]{0:T(1024)S(1)} %all_gather.34), kind=kOutput, calls=%fused_computation.17 | convolution fusion | flops 8610906112 | bytes 27279360 | tf_op jit(solution)/shard_map/dot_general | solution.py:200
  573.1 59.2 %collective-permute-done.1 = bf16[1024,1024]{1,0:T(8,128)(2,1)S(1)} collective-permute-done((bf16[1024,1024]{1,0:T(8,128)(2,1)S(1)}, bf16[1024,1024]{1,0:T(8,128)(2,1)S(1)}, u32[]{:S(2)}, u32[]{:S(2)}) %collective-permute-start.1) | collective-permute-done | bytes 2097184 | tf_op jit(solution)/shard_map/ppermute | solution.py:298
  641.0 89.1 %reduce-scatter.5.cloned.1.call-done = bf16[3,32,1024]{2,1,0:T(8,128)(2,1)} async-done(((bf16[3,1024,1024]{2,1,0:T(8,128)(2,1)}), bf16[3,32,1024]{2,1,0:T(8,128)(2,1)}) %reduce-scatter.5.cloned.1.call-update) | async-done | bytes 196624 | tf_op jit(solution)/shard_map/reduce_scatter | solution.py:227
  730.1 183.4 %reduce-scatter.9.cloned.1.call-done = bf16[128,1024]{1,0:T(8,128)(2,1)} async-done(((bf16[4096,1024]{1,0:T(8,128)(2,1)}), bf16[128,1024]{1,0:T(8,128)(2,1)}) %reduce-scatter.9.cloned.1.call-update) | async-done | bytes 262160 | tf_op jit(solution)/shard_map/reduce_scatter | solution.py:227
  913.6 186.3 %reduce-scatter.11.cloned.1.call-done = bf16[128,1024]{1,0:T(8,128)(2,1)} async-done(((bf16[4096,1024]{1,0:T(8,128)(2,1)}), bf16[128,1024]{1,0:T(8,128)(2,1)}) %reduce-scatter.11.cloned.1.call-update) | async-done | bytes 262160 | tf_op jit(solution)/shard_map/reduce_scatter | solution.py:227
  1100.0 16.8 %fusion.19 = bf16[1,1024,1024]{2,1,0:T(8,128)(2,1)} fusion(f32[1024,1024]{1,0:T(8,128)} %get-tuple-element.81, f32[1024]{0:T(1024)S(1)} %copy-done.44, bf16[4096,1024]{1,0:T(8,128)(2,1)} %all-gather.14.cloned.1.call-done, f32[1024,4096]{1,0:T(8,128)} %fusion.33, f32[4096]{0:T(1024)S(1)} %all_gather.34), kind=kOutput, calls=%fused_computation.66 | convolution fusion | flops 8609857536 | bytes 31477760 | tf_op jit(solution)/shard_map/dot_general | solution.py:196
  1121.0 110.2 %all-reduce.17.cloned.1.call-done = (f32[1024]{0:T(1024)}, f32[3,3,1024]{2,1,0:T(4,128)}, f32[1024]{0:T(1024)}, f32[1024]{0:T(1024)}, f32[4096]{0:T(1024)}, /*index=5*/f32[1024]{0:T(1024)}) async-done(((f32[1024]{0:T(1024)}, f32[3,3,1024]{2,1,0:T(4,128)}, f32[1024]{0:T(1024)}, f32[1024]{0:T(1024)}, f32[4096]{0:T(1024)}, /*index=5*/f32[1024]{0:T(1024)}), (f32[1024]{0:T(1024)}, f32[3,3,1024]{2,1,0:T(4,128)}, ...) | async-done | bytes 69648 | tf_op jit(solution)/shard_map/psum | solution.py:304
  1233.8 139.2 %reduce-scatter.7.cloned.1.call-done = bf16[32,1024]{1,0:T(8,128)(2,1)} async-done(((bf16[1024,1024]{1,0:T(8,128)(2,1)}), bf16[32,1024]{1,0:T(8,128)(2,1)}) %reduce-scatter.7.cloned.1.call-update) | async-done | bytes 65552 | tf_op jit(solution)/shard_map/reduce_scatter | solution.py:227
  1373.0 16.6 %all_gather.37 = bf16[256,1024]{1,0:T(8,128)(2,1)S(1)} all-gather(bf16[32,1024]{1,0:T(8,128)(2,1)} %reduce-scatter.7.cloned.1.call-done), channel_id=1, replica_groups=mesh['head'=4,'batch'=4,'dp'=2] {'batch','dp'}, dimensions={0}, use_global_device_ids=true | all-gather | bytes 589824 | tf_op jit(solution)/shard_map/all_gather | solution.py:228
  1405.4 23.0 %all-gather.18.cloned.1.call-done = bf16[1024,1024]{1,0:T(8,128)(2,1)} async-done(((bf16[128,1024]{1,0:T(8,128)(2,1)}), bf16[1024,1024]{1,0:T(8,128)(2,1)}) %all-gather.18.cloned.1.call-update) | async-done | bytes 2097168 | tf_op jit(solution)/shard_map/all_gather | solution.py:228
  1437.9 20.3 %all-gather.20.cloned.1.call-done = bf16[1024,1024]{1,0:T(8,128)(2,1)} async-done(((bf16[128,1024]{1,0:T(8,128)(2,1)}), bf16[1024,1024]{1,0:T(8,128)(2,1)}) %all-gather.20.cloned.1.call-update) | async-done | bytes 2097168 | tf_op jit(solution)/shard_map/all_gather | solution.py:228
  (202 shorter events, 207.7 us)
Async XLA Ops:
  7.2 112.6 %all-gather.8.cloned.1.call-start = ((), (), s32[]{:S(2)}) async-start(), calls=%async_computation.4 | async-start | bytes 6488064 | tf_op jit(solution)/shard_map/all_gather | solution.py:223
  9.8 96.6 %copy-start.34 = (f32[3,3,256]{2,1,0:T(4,128)S(1)}, f32[3,3,256]{2,1,0:T(4,128)}, u32[]{:S(2)}) copy-start(f32[3,3,256]{2,1,0:T(4,128)} %param.17) | copy-start | bytes 27652
  9.8 193.6 %all-gather.10.cloned.1.call-start = ((), (), s32[]{:S(2)}) async-start(), calls=%async_computation.5 | async-start | bytes 2162688 | tf_op jit(solution)/shard_map/all_gather | solution.py:223
  11.3 243.3 %all-gather.12.cloned.1.call-start = ((), (), s32[]{:S(2)}) async-start(), calls=%async_computation.6 | async-start | bytes 8650752 | tf_op jit(solution)/shard_map/all_gather | solution.py:223
  12.2 321.4 %all-gather.14.cloned.1.call-start = ((), (), s32[]{:S(2)}) async-start(), calls=%async_computation.7 | async-start | bytes 8650752 | tf_op jit(solution)/shard_map/all_gather | solution.py:223
  14.1 716.0 %reduce-scatter.5.cloned.1.call-start = ((), (), s32[]{:S(2)}) async-start(), calls=%async_computation.8 | async-start | bytes 6488064 | tf_op jit(solution)/shard_map/reduce_scatter | solution.py:227
  18.1 101.5 %collective-permute-start = (bf16[1024,1024]{1,0:T(8,128)(2,1)}, bf16[1024,1024]{1,0:T(8,128)(2,1)}, u32[]{:S(2)}, u32[]{:S(2)}) collective-permute-start(bf16[1024,1024]{1,0:T(8,128)(2,1)} %fusion.6), channel_id=1, source_target_pairs={{0,8},{8,16},{16,24},{1,9},{9,17},{17,25},{2,10},{10,18},{18,26},{... | collective-permute-start | bytes 6291464 | tf_op jit(solution)/shard_map/ppermute | solution.py:243
  119.8 32.5 %copy-start.26 = (bf16[1024,1024]{1,0:T(8,128)(2,1)}, bf16[1024,1024]{1,0:T(8,128)(2,1)S(1)}, u32[]{:S(2)}) copy-start(bf16[1024,1024]{1,0:T(8,128)(2,1)S(1)} %broadcast_select_fusion) | copy-start | bytes 6291460
  203.4 51.2 %copy-start.35 = (f32[1024]{0:T(1024)S(1)}, f32[1024]{0:T(1024)}, u32[]{:S(2)}) copy-start(f32[1024]{0:T(1024)} %param.20) | copy-start | bytes 12292
  514.7 398.8 %reduce-scatter.9.cloned.1.call-start = ((), (), s32[]{:S(2)}) async-start(), calls=%async_computation.11 | async-start | bytes 8650752 | tf_op jit(solution)/shard_map/reduce_scatter | solution.py:227
  530.6 569.3 %reduce-scatter.11.cloned.1.call-start = ((), (), s32[]{:S(2)}) async-start(), calls=%async_computation.13 | async-start | bytes 8650752 | tf_op jit(solution)/shard_map/reduce_scatter | solution.py:227
  549.2 682.1 %all-reduce.17.cloned.1.call-start = ((), (), s32[]{:S(2)}) async-start(), calls=%async_computation.15 | async-start | bytes 163840 | tf_op jit(solution)/shard_map/psum | solution.py:304
  570.6 64.3 %copy-start.16 = (f32[2048,1024]{1,0:T(8,128)}, f32[2048,1024]{1,0:T(8,128)S(1)}, u32[]{:S(2)}) copy-start(f32[2048,1024]{1,0:T(8,128)S(1)} %pad_add_fusion) | copy-start | bytes 25165828
  570.6 61.7 %copy-start.12 = (bf16[1,1024,1024]{2,1,0:T(8,128)(2,1)S(1)}, bf16[1,1024,1024]{2,1,0:T(8,128)(2,1)}, u32[]{:S(2)}) copy-start(bf16[1,1024,1024]{2,1,0:T(8,128)(2,1)} %param.13) | copy-start | bytes 6291460
  570.6 61.7 %copy-start.31 = (f32[1024]{0:T(1024)S(1)}, f32[1024]{0:T(1024)}, u32[]{:S(2)}) copy-start(f32[1024]{0:T(1024)} %copy-done.30) | copy-start | bytes 12292
  570.6 61.7 %copy-start.33 = (f32[1024]{0:T(1024)S(1)}, f32[1024]{0:T(1024)}, u32[]{:S(2)}) copy-start(f32[1024]{0:T(1024)} %param.15) | copy-start | bytes 12292
  570.9 61.4 %collective-permute-start.1 = (bf16[1024,1024]{1,0:T(8,128)(2,1)S(1)}, bf16[1024,1024]{1,0:T(8,128)(2,1)S(1)}, u32[]{:S(2)}, u32[]{:S(2)}) collective-permute-start(bf16[1024,1024]{1,0:T(8,128)(2,1)S(1)} %fusion.20), channel_id=1, source_target_pairs={{8,0},{16,8},{24,16},{9,1},{17,9},{25,17},{10,2},{18,10},{26,18},{... | collective-permute-start | bytes 6291464 | tf_op jit(solution)/shard_map/ppermute | solution.py:298
  573.1 61.9 %copy-start.3 = (bf16[1024,1024]{1,0:T(8,128)(2,1)S(1)}, bf16[1024,1024]{1,0:T(8,128)(2,1)}, u32[]{:S(2)}) copy-start(bf16[1024,1024]{1,0:T(8,128)(2,1)} %copy-done.2) | copy-start | bytes 6291460
  634.9 465.0 %copy-start.44 = (f32[1024]{0:T(1024)S(1)}, f32[1024]{0:T(1024)}, u32[]{:S(2)}) copy-start(f32[1024]{0:T(1024)} %param.24) | copy-start | bytes 12292
  635.0 738.1 %reduce-scatter.7.cloned.1.call-start = ((), (), s32[]{:S(2)}) async-start(), calls=%async_computation.10 | async-start | bytes 2162688 | tf_op jit(solution)/shard_map/reduce_scatter | solution.py:227
  641.0 757.4 %all-gather.16.cloned.1.call-start = ((), (), s32[]{:S(2)}) async-start(), calls=%async_computation.9 | async-start | bytes 1769472 | tf_op jit(solution)/shard_map/all_gather | solution.py:228
  730.1 698.3 %all-gather.18.cloned.1.call-start = ((), (), s32[]{:S(2)}) async-start(), calls=%async_computation.12 | async-start | bytes 2359296 | tf_op jit(solution)/shard_map/all_gather | solution.py:228
  913.5 544.7 %all-gather.20.cloned.1.call-start = ((), (), s32[]{:S(2)}) async-start(), calls=%async_computation.14 | async-start | bytes 2359296 | tf_op jit(solution)/shard_map/all_gather | solution.py:228
  1432.4 32.2 %copy-start.1 = (bf16[1024,1024]{1,0:T(8,128)(2,1)S(1)}, bf16[1024,1024]{1,0:T(8,128)(2,1)}, u32[]{:S(2)}) copy-start(bf16[1024,1024]{1,0:T(8,128)(2,1)} %param.21) | copy-start | bytes 6291460
  (44 other events, 461.4 us)
Sparse Core Ops, SparseCore 0:
  11.7 86.5 all-gather.7
  101.3 58.6 all-gather.9
  163.4 91.1 all-gather.11
  258.0 75.5 all-gather.13
  514.8 215.1 reduce-scatter.4
  732.2 181.2 reduce-scatter.8
  915.8 184.0 reduce-scatter.10
  1107.5 123.7 all-reduce.16
  1234.1 138.9 reduce-scatter.6
  1374.9 23.4 all-gather.15
  1400.4 27.8 all-gather.17
  1430.3 27.8 all-gather.19

commit v2 on v1

v2 whole, which is shorter than its diff:
```python
import functools
import math

import jax
import jax.numpy as jnp
from jax import lax
from jax.experimental import pallas as pl
from jax.experimental.pallas import tpu as pltpu
from jax.sharding import PartitionSpec as P

LONG = 2048
EPSILON = 1e-06
ALL = ("head", "batch", "dp")

HS = 64
LANES = 128
EDGE = 16
LOG2E = math.log2(math.e)
NT = (((1,), (1,)), ((), ()))
NN = (((1,), (0,)), ((), ()))
TN = (((0,), (0,)), ((), ()))


def dot(a, b, dims=NN):
    return lax.dot_general(a, b, dims, preferred_element_type=jnp.float32)


def spans(first, last, step):
    return [(at, min(step, last - at)) for at in range(first, last, step)]


def earlier(ref, start, size):
    if start == 0:
        rows = jnp.concatenate([jnp.zeros((EDGE, LANES), jnp.float32), ref[pl.ds(0, size), :].astype(jnp.float32)], axis=0)
    else:
        rows = ref[pl.ds(start - EDGE, size + EDGE), :].astype(jnp.float32)
    return [pltpu.roll(rows, i, 0)[EDGE:] if i else rows[EDGE:] for i in range(3)]


def convolve(linear_ref, kern_ref, member, target_ref, skip, step=256):
    total = linear_ref.shape[0]
    for start, size in spans(skip, total, step):
        taps = earlier(linear_ref, start, size)
        value = sum(kern_ref[3 * member + i:3 * member + i + 1, :] * taps[i] for i in range(3))
        target_ref[pl.ds(start - skip, size), :] = value.astype(jnp.bfloat16)


def convolve_back(grad_ref, linear_ref, kern_ref, member, target_ref, sums_ref, step=256):
    total = linear_ref.shape[0]
    parts = [jnp.zeros((8, LANES), jnp.float32)] * 3
    for start, size in spans(0, total, step):
        rows = grad_ref[pl.ds(start, size + 8), :]
        value = kern_ref[3 * member:3 * member + 1, :] * rows[:size]
        for i in (1, 2):
            value += kern_ref[3 * member + i:3 * member + i + 1, :] * pltpu.roll(rows, size + 8 - i, 0)[:size]
        target_ref[pl.ds(start, size), :] = value.astype(jnp.bfloat16)
        taps = earlier(linear_ref, start, size)
        for i in range(3):
            parts[i] += jnp.sum((rows[:size] * taps[i]).reshape(size // 8, 8, LANES), axis=0)
    for i in range(3):
        sums_ref[3 * member + i:3 * member + i + 1, :] = jnp.sum(parts[i], axis=0, keepdims=True)


def forward_kernel(
    before_ref, lq_ref, lk_ref, lv_ref, kern_ref, out_ref, mass_ref, q_ref, k_ref, v_ref, s0_ref, s1_ref, *, shards, bq, kc,
):
    rows = q_ref.shape[0]
    own = (shards - 1) * rows
    lane = lax.broadcasted_iota(jnp.int32, (bq, LANES), 1) < HS
    scale = 1.0 / math.sqrt(HS)
    convolve(lq_ref, kern_ref, 0, q_ref, lq_ref.shape[0] - rows)
    convolve(lk_ref, kern_ref, 1, k_ref, 0)
    convolve(lv_ref, kern_ref, 2, v_ref, 0)

    def block(at, first):
        query = q_ref[pl.ds(at, bq), :] * jnp.bfloat16(scale)
        zero = jnp.zeros_like(query)
        queries = (jnp.where(lane, query, zero), jnp.where(lane, zero, query))
        stores = (s0_ref, s1_ref)
        peaks = [None, None]
        parts = spans(first, own + at, kc) + [(own + at, bq)]
        for start, size in parts:
            key = k_ref[pl.ds(start, size), :]
            for h in range(2):
                s = dot(queries[h], key, NT)
                if start == own + at:
                    row = lax.broadcasted_iota(jnp.int32, (bq, size), 0)
                    col = lax.broadcasted_iota(jnp.int32, (bq, size), 1)
                    s = jnp.where(col <= row, s, -1e30)
                stores[h][:, pl.ds(start, size)] = s
                top = jnp.max(s, axis=1, keepdims=True)
                peaks[h] = top if peaks[h] is None else jnp.maximum(peaks[h], top)
        sums = [None, None]
        scaled = [peak * LOG2E for peak in peaks]
        for start, size in parts:
            value = v_ref[pl.ds(start, size), :]
            wide = lax.broadcasted_iota(jnp.int32, (size, LANES), 1) < HS
            one = jnp.ones_like(value)
            values = (jnp.where(wide, value, one), jnp.where(wide, one, value))
            for h in range(2):
                p = jnp.exp2(stores[h][:, pl.ds(start, size)] * LOG2E - scaled[h]).astype(jnp.bfloat16)
                o = dot(p, values[h])
                sums[h] = o if sums[h] is None else sums[h] + o
        total = pltpu.roll(jnp.where(lane, sums[1], sums[0]), HS, 1)
        out_ref[pl.ds(at, bq), :] = (jnp.where(lane, sums[0], sums[1]) / total).astype(out_ref.dtype)
        mass = jnp.where(lane, peaks[0], peaks[1]) + jnp.log(total)
        mass = mass.T
        mass_ref[0, 0:1, pl.ds(at, bq)] = mass[0:1]
        mass_ref[0, 1:2, pl.ds(at, bq)] = mass[HS:HS + 1]

    for before in range(shards):
        @pl.when(before_ref[0] == before)
        def _():
            for at in range(0, rows, bq):
                block(at, own - before * rows)


def column(n):
    return pl.BlockSpec((n, LANES), lambda i, b: (0, i))


def attention_forward(before, late, linear_k, linear_v, kern, rows):
    edged, width = late.shape
    window = linear_k.shape[0]
    shards = window // rows
    pairs = width // LANES
    bq = min(256, rows)
    return pl.pallas_call(
        functools.partial(forward_kernel, shards=shards, bq=bq, kc=512),
        out_shape=(jax.ShapeDtypeStruct((rows, width), jnp.bfloat16), jax.ShapeDtypeStruct((pairs, 8, rows), jnp.float32)),
        grid_spec=pltpu.PrefetchScalarGridSpec(
            num_scalar_prefetch=1, grid=(pairs,),
            in_specs=[column(edged), column(window), column(window), column(16)],
            out_specs=[column(rows), pl.BlockSpec((1, 8, rows), lambda i, b: (i, 0, 0))],
            scratch_shapes=[
                pltpu.VMEM((rows, LANES), jnp.bfloat16), pltpu.VMEM((window, LANES), jnp.bfloat16),
                pltpu.VMEM((window, LANES), jnp.bfloat16),
                pltpu.VMEM((bq, window), jnp.float32), pltpu.VMEM((bq, window), jnp.float32),
            ],
        ),
        compiler_params=pltpu.CompilerParams(vmem_limit_bytes=48 << 20),
    )(before, late, linear_k, linear_v, kern)


def backward_kernel(
    before_ref, lq_ref, lk_ref, lv_ref, kern_ref, g_ref, o_ref, mass_ref, gq_ref, gk_ref, gv_ref, sums_ref,
    q_ref, k_ref, v_ref, kt_ref, dq_ref, dk_ref, dv_ref, *, shards, bq, kc,
):
    rows = q_ref.shape[0]
    window = k_ref.shape[0]
    own = window - rows
    edge = lq_ref.shape[0] - rows
    lane = lax.broadcasted_iota(jnp.int32, (bq, LANES), 1) < HS
    scale = 1.0 / math.sqrt(HS)
    convolve(lq_ref, kern_ref, 0, q_ref, edge)
    convolve(lk_ref, kern_ref, 1, k_ref, 0)
    convolve(lv_ref, kern_ref, 2, v_ref, 0)
    dk_ref[...] = jnp.zeros_like(dk_ref)
    dv_ref[...] = jnp.zeros_like(dv_ref)
    if edge:
        dq_ref[pl.ds(0, edge), :] = jnp.zeros((edge, LANES), jnp.float32)
    dq_ref[pl.ds(edge + rows, 8), :] = jnp.zeros((8, LANES), jnp.float32)
    kt_ref[...] = k_ref[...].astype(jnp.float32).T.astype(jnp.bfloat16)

    def block(at, first):
        query = q_ref[pl.ds(at, bq), :] * jnp.bfloat16(scale)
        grad = g_ref[pl.ds(at, bq), :]
        zero = jnp.zeros_like(query)
        queries = (jnp.where(lane, query, zero), jnp.where(lane, zero, query))
        grads = (jnp.where(lane, grad, zero), jnp.where(lane, zero, grad))
        product = (grad.astype(jnp.float32) * o_ref[pl.ds(at, bq), :].astype(jnp.float32)).T
        query_grads = [jnp.zeros((HS, bq), jnp.float32)] * 2
        deltas = [jnp.sum(product[h * HS:(h + 1) * HS], axis=0, keepdims=True) for h in range(2)]
        masses = [mass_ref[0, h:h + 1, pl.ds(at, bq)] * LOG2E for h in range(2)]
        parts = spans(first, own + at, kc) + [(own + at, bq)]
        for start, size in parts:
            key = k_ref[pl.ds(start, size), :]
            value = v_ref[pl.ds(start, size), :]
            key_part = value_part = None
            for h in range(2):
                s = dot(key, queries[h], NT)
                if start == own + at:
                    row = lax.broadcasted_iota(jnp.int32, (size, bq), 1)
                    col = lax.broadcasted_iota(jnp.int32, (size, bq), 0)
                    s = jnp.where(col <= row, s, -1e30)
                p = jnp.exp2(s * LOG2E - masses[h])
                dp = dot(value, grads[h], NT)
                ds = (p * (dp - deltas[h])).astype(jnp.bfloat16)
                a = dot(p.astype(jnp.bfloat16), grads[h])
                b = dot(ds, queries[h])
                value_part = a if value_part is None else value_part + a
                key_part = b if key_part is None else key_part + b
                query_grads[h] += dot(kt_ref[h * HS:(h + 1) * HS, pl.ds(start, size)], ds)
            dk_ref[pl.ds(start, size), :] += key_part
            dv_ref[pl.ds(start, size), :] += value_part
        dq_ref[pl.ds(edge + at, bq), :] = jnp.concatenate(query_grads, axis=0).T * scale

    for before in range(shards):
        @pl.when(before_ref[0] == before)
        def _():
            for at in range(0, rows, bq):
                block(at, own - before * rows)

    sums_ref[...] = jnp.zeros_like(sums_ref)
    convolve_back(dq_ref, lq_ref, kern_ref, 0, gq_ref, sums_ref)
    convolve_back(dk_ref, lk_ref, kern_ref, 1, gk_ref, sums_ref)
    convolve_back(dv_ref, lv_ref, kern_ref, 2, gv_ref, sums_ref)


def attention_backward(before, late, linear_k, linear_v, kern, grads, outs, mass):
    rows = grads.shape[0]
    edged, width = late.shape
    window = linear_k.shape[0]
    shards = window // rows
    pairs = width // LANES
    bq = min(256, rows)
    bf = jnp.bfloat16
    return pl.pallas_call(
        functools.partial(backward_kernel, shards=shards, bq=bq, kc=256),
        out_shape=(jax.ShapeDtypeStruct((edged, width), bf), jax.ShapeDtypeStruct((window, width), bf),
                   jax.ShapeDtypeStruct((window, width), bf), jax.ShapeDtypeStruct((16, width), jnp.float32)),
        grid_spec=pltpu.PrefetchScalarGridSpec(
            num_scalar_prefetch=1, grid=(pairs,),
            in_specs=[column(edged), column(window), column(window), column(16), column(rows), column(rows),
                      pl.BlockSpec((1, 8, rows), lambda i, b: (i, 0, 0))],
            out_specs=[column(edged), column(window), column(window), column(16)],
            scratch_shapes=[
                pltpu.VMEM((rows, LANES), bf), pltpu.VMEM((window, LANES), bf), pltpu.VMEM((window, LANES), bf),
                pltpu.VMEM((LANES, window), bf), pltpu.VMEM((edged + 8, LANES), jnp.float32),
                pltpu.VMEM((window + 8, LANES), jnp.float32), pltpu.VMEM((window + 8, LANES), jnp.float32),
            ],
        ),
        compiler_params=pltpu.CompilerParams(vmem_limit_bytes=48 << 20),
    )(before, late, linear_k, linear_v, kern, grads, outs, mass)


MESH = pl.DeviceIdType.MESH


class Copies:
    def __init__(self, send_sems, recv_sems):
        self.send_sems, self.recv_sems, self.all = send_sems, recv_sems, []

    def start(self, source, target, device):
        n = len(self.all)
        copy = pltpu.make_async_remote_copy(
            src_ref=source, dst_ref=target, send_sem=self.send_sems.at[n], recv_sem=self.recv_sems.at[n],
            device_id=device, device_id_type=MESH,
        )
        copy.start()
        self.all.append(copy)
        return copy

    def finish(self):
        for copy in self.all:
            copy.wait_send()


class Place:
    def __init__(self, nz, ny, nx):
        self.nz, self.ny, self.nx = nz, ny, nx
        self.z, batch, self.x = lax.axis_index("head"), lax.axis_index("batch"), lax.axis_index("dp")
        self.y, self.c = batch // 2, batch % 2

    def along_z(self, step):
        return {"head": (self.z + step) % self.nz}

    def along_y(self, step):
        return {"batch": (self.y + step) % self.ny * 2 + self.c}

    def along_x(self, step):
        return {"dp": (self.x + step) % self.nx}

    def other_core(self):
        return {"batch": self.y * 2 + 1 - self.c}

    def meet(self, z_steps):
        partners = [self.along_z(s) for s in z_steps]
        partners += [self.along_y(s) for s in range(1, self.ny)] + [self.along_x(s) for s in range(1, self.nx)]
        partners.append(self.other_core())
        barrier = pltpu.get_barrier_semaphore()
        for partner in partners:
            pl.semaphore_signal(barrier, inc=1, device_id=partner, device_id_type=MESH)
        pl.semaphore_wait(barrier, len(partners))


def spread(place, copies, spot, members):
    ny, nx, y, c, x = place.ny, place.nx, place.y, place.c, place.x
    half = members // 2
    own = spot(y, c, x, 0, members)
    over_x = [copies.start(own, own, place.along_x(s)) for s in range(1, nx)]
    over_y = [copies.start(own, own, place.along_y(s)) for s in range(1, ny)]
    yield
    corner = []
    for s, copy in enumerate(over_x, 1):
        copy.wait_recv()
        part = spot(y, c, (x - s) % nx, 0, half)
        corner += [copies.start(part, part, place.along_y(t)) for t in range(1, ny)]
    for t, copy in enumerate(over_y, 1):
        copy.wait_recv()
        part = spot((y - t) % ny, c, x, half, members)
        corner += [copies.start(part, part, place.along_x(s)) for s in range(1, nx)]
    yield
    for copy in corner:
        copy.wait_recv()
    cores = []
    for row in range(ny):
        part = spot(row, c, None, 0, members)
        cores.append(copies.start(part, part, place.other_core()))
    yield
    for copy in cores:
        copy.wait_recv()


def run_staggered(makers):
    live = []
    makers = list(makers)
    while makers or live:
        if makers:
            live.append(makers.pop(0)())
        for task in list(live):
            try:
                next(task)
            except StopIteration:
                live.remove(task)


def gather_kernel(nz, ny, nx, shard_ref, full_ref, send_sems, recv_sems):
    place = Place(nz, ny, nx)
    copies = Copies(send_sems, recv_sems)
    height, width = shard_ref.shape[1], shard_ref.shape[2]
    rows = height // (ny * 2 * nx)
    z = place.z

    def spot_of(block):
        def spot(y, c, x, lo, hi):
            first = (y * 2 + c) * nx * rows
            size = nx * rows
            if x is not None:
                first, size = first + x * rows, rows
            return full_ref.at[lo:hi, pl.ds(pl.multiple_of(first, rows), size), pl.ds(pl.multiple_of(block * width, width), width)]
        return spot

    place.meet((1, nz - 1) if nz > 2 else (1,))
    own = ((place.y * 2 + place.c) * nx + place.x) * rows
    mine = shard_ref.at[:, pl.ds(pl.multiple_of(own, rows), rows), :]
    rings = [copies.start(mine, spot_of(z)(place.y, place.c, place.x, 0, shard_ref.shape[0]), place.along_z(1))]
    for m in range(shard_ref.shape[0]):
        full_ref[m, :, pl.ds(pl.multiple_of(z * width, width), width)] = shard_ref[m]

    def arrival(step):
        def task():
            rings[step].wait_recv()
            spot = spot_of((z - 1 - step) % nz)
            if step < nz - 2:
                part = spot(place.y, place.c, place.x, 0, shard_ref.shape[0])
                rings.append(copies.start(part, part, place.along_z(1)))
            yield from spread(place, copies, spot, shard_ref.shape[0])
        return task

    run_staggered(arrival(step) for step in range(nz - 1))
    copies.finish()


def gather(shard, nz, ny, nx):
    members, height, width = shard.shape
    per_step = (nx - 1) + (ny - 1) + 2 * (nx - 1) * (ny - 1) + ny
    count = (nz - 1) * (1 + per_step)
    return pl.pallas_call(
        functools.partial(gather_kernel, nz, ny, nx),
        out_shape=jax.ShapeDtypeStruct((members, height, width * nz), shard.dtype),
        in_specs=[pl.BlockSpec(memory_space=pltpu.VMEM)],
        out_specs=pl.BlockSpec(memory_space=pltpu.VMEM),
        scratch_shapes=[pltpu.SemaphoreType.DMA((count,)), pltpu.SemaphoreType.DMA((count,))],
        compiler_params=pltpu.CompilerParams(collective_id=0, has_side_effects=True, vmem_limit_bytes=48 << 20),
        cost_estimate=pl.CostEstimate(flops=0, bytes_accessed=2 * members * height * width * nz * 2, transcendentals=0),
    )(shard)


def reduce_kernel(
    nz, ny, nx, grad_ref, small_ref, out_ref, small_out_ref,
    core_buf, y1_buf, x1_buf, x2_buf, y2_buf, z_send, z_buf, s_acc, s_buf, send_sems, recv_sems,
):
    place = Place(nz, ny, nx)
    copies = Copies(send_sems, recv_sems)
    members, height, width = grad_ref.shape[1:]
    half = members // 2
    rows = height // (ny * 2 * nx)
    band = nx * rows
    y, c, x, z = place.y, place.c, place.x, place.z
    f32, bf = jnp.float32, jnp.bfloat16
    place.meet(range(1, nz))

    def bands(row, core):
        return pl.ds(pl.multiple_of((row * 2 + core) * band, band), band)

    def xrows(at):
        return pl.ds(pl.multiple_of(at * rows, rows), rows)

    def chunk(t):
        block = (z + 1 + t) % nz

        def task():
            sent = [
                copies.start(grad_ref.at[block, :, bands(row, 1 - c), :], core_buf.at[t, row], place.other_core())
                for row in range(ny)
            ]
            yield
            for row, copy in enumerate(sent):
                copy.wait_recv()
                for m in range(members):
                    total = core_buf[t, row, m].astype(f32) + grad_ref[block, m, bands(row, c), :].astype(f32)
                    core_buf[t, row, m] = total.astype(bf)
            over_y = [
                copies.start(core_buf.at[t, (y + s) % ny, 0:half], y1_buf.at[t, s - 1], place.along_y(s))
                for s in range(1, ny)
            ]
            over_x = [
                copies.start(core_buf.at[t, :, half:, xrows((x + s) % nx), :], x1_buf.at[t, s - 1], place.along_x(s))
                for s in range(1, nx)
            ]
            yield
            for copy in over_y:
                copy.wait_recv()
            for m in range(half):
                total = core_buf[t, y, m].astype(f32)
                for s in range(ny - 1):
                    total = total + y1_buf[t, s, m].astype(f32)
                core_buf[t, y, m] = total.astype(bf)
            last = [
                copies.start(core_buf.at[t, y, 0:half, xrows((x + s) % nx), :], x2_buf.at[t, s - 1], place.along_x(s))
                for s in range(1, nx)
            ]
            for copy in over_x:
                copy.wait_recv()
            for row in range(ny):
                for m in range(half):
                    total = core_buf[t, row, half + m, xrows(x), :].astype(f32)
                    for s in range(nx - 1):
                        total = total + x1_buf[t, s, row, m].astype(f32)
                    core_buf[t, row, half + m, xrows(x), :] = total.astype(bf)
            last += [
                copies.start(core_buf.at[t, (y + s) % ny, half:, xrows(x), :], y2_buf.at[t, s - 1], place.along_y(s))
                for s in range(1, ny)
            ]
            yield
            for copy in last:
                copy.wait_recv()
            for m in range(members):
                total = core_buf[t, y, m, xrows(x), :].astype(f32)
                buf, n = (x2_buf, nx - 1) if m < half else (y2_buf, ny - 1)
                for s in range(n):
                    total = total + buf[t, s, m % half].astype(f32)
                z_send[t, m] = total.astype(bf)
            if t < nz - 1:
                sums.append(copies.start(z_send.at[t], z_buf.at[t], place.along_z(1 + t)))
        return task

    def small():
        s_acc[0] = small_ref[...]
        stages = ([place.other_core()], [place.along_x(s) for s in range(1, nx)],
                  [place.along_y(s) for s in range(1, ny)], [place.along_z(s) for s in range(1, nz)])
        used = 0
        for k, partners in enumerate(stages):
            sent = [copies.start(s_acc.at[k], s_buf.at[used + i], partner) for i, partner in enumerate(partners)]
            yield
            total = s_acc[k]
            for i, copy in enumerate(sent):
                copy.wait_recv()
                total = total + s_buf[used + i]
            used += len(sent)
            if k < 3:
                s_acc[k + 1] = total
            else:
                small_out_ref[...] = total

    sums = []
    run_staggered([chunk(0), small] + [chunk(t) for t in range(1, nz)])
    for copy in sums:
        copy.wait_recv()

    def spot(y_at, c_at, x_at, lo, hi):
        first, size = (y_at * 2 + c_at) * band, band
        if x_at is not None:
            first, size = first + x_at * rows, rows
        return out_ref.at[lo:hi, pl.ds(pl.multiple_of(first, rows), size), :]

    own = pl.ds(pl.multiple_of(((y * 2 + c) * nx + x) * rows, rows), rows)
    for m in range(members):
        total = z_send[nz - 1, m].astype(f32)
        for t in range(nz - 1):
            total = total + z_buf[t, m].astype(f32)
        out_ref[m, own, :] = total.astype(bf)
    for _ in spread(place, copies, spot, members):
        pass
    copies.finish()


def reduce(grad, small, ny, nx, collective_id):
    nz, members, height, width = grad.shape
    half = members // 2
    rows = height // (ny * 2 * nx)
    band = nx * rows
    bf = jnp.bfloat16
    per_chunk = ny + 2 * (ny - 1) + 2 * (nx - 1)
    spread_count = (nx - 1) + (ny - 1) + 2 * (nx - 1) * (ny - 1) + ny
    small_count = 1 + (nx - 1) + (ny - 1) + (nz - 1)
    count = nz * per_chunk + (nz - 1) + spread_count + small_count
    vmem = pl.BlockSpec(memory_space=pltpu.VMEM)
    return pl.pallas_call(
        functools.partial(reduce_kernel, nz, ny, nx),
        out_shape=(jax.ShapeDtypeStruct((members, height, width), bf), jax.ShapeDtypeStruct(small.shape, jnp.float32)),
        in_specs=[vmem, vmem],
        out_specs=(vmem, vmem),
        scratch_shapes=[
            pltpu.VMEM((nz, ny, members, band, width), bf),
            pltpu.VMEM((nz, ny - 1, half, band, width), bf),
            pltpu.VMEM((nz, nx - 1, ny, half, rows, width), bf),
            pltpu.VMEM((nz, nx - 1, half, rows, width), bf),
            pltpu.VMEM((nz, ny - 1, half, rows, width), bf),
            pltpu.VMEM((nz, members, rows, width), bf),
            pltpu.VMEM((nz - 1, members, rows, width), bf),
            pltpu.VMEM((4,) + small.shape, jnp.float32),
            pltpu.VMEM((small_count,) + small.shape, jnp.float32),
            pltpu.SemaphoreType.DMA((count,)),
            pltpu.SemaphoreType.DMA((count,)),
        ],
        compiler_params=pltpu.CompilerParams(collective_id=collective_id, has_side_effects=True, vmem_limit_bytes=56 << 20),
        cost_estimate=pl.CostEstimate(flops=0, bytes_accessed=grad.size * 2, transcendentals=0),
    )(grad, small)


def factor_of(values):
    return lax.rsqrt(jnp.mean(values * values, axis=-1, keepdims=True) + EPSILON)


def norm_backward(values, gain, upstream):
    factor = factor_of(values)
    unit = values * factor
    scaled = gain * upstream
    result = factor * (scaled - unit * jnp.mean(scaled * unit, axis=-1, keepdims=True))
    return result, upstream * unit


def on_device(
    layer_input, lengths, norm1_gain, qkv_weight, kernels, out_weight, out_bias,
    norm2_gain, up_weight, up_bias, down_weight, down_bias, out_grad,
):
    rows = layer_input.shape[1]
    nz, nb, nx = lax.axis_size("head"), lax.axis_size("batch"), lax.axis_size("dp")
    ny, copies = nb // 2, nb * nx
    shards = max(1, LONG // rows)
    place = lax.axis_index("head")
    mine = lax.axis_index("batch") * nx + lax.axis_index("dp")
    width = qkv_weight.shape[2]
    hidden_units = up_weight.shape[1]

    first_row = place * rows
    ends = jnp.cumsum(lengths[0])
    begins = jnp.max(jnp.where(ends <= first_row, ends, 0))
    before = ((first_row - begins) // rows).astype(jnp.int32)

    own_float = layer_input[0].astype(jnp.float32)
    cotangent = out_grad[0]
    normed_own = (own_float * factor_of(own_float) * norm1_gain).astype(jnp.bfloat16)
    pieces = [normed_own]
    for hop in range(1, shards):
        came = lax.ppermute(normed_own, "head", [(i, i + hop) for i in range(nz - hop)])
        pieces.insert(0, jnp.where(before >= hop, came, jnp.zeros_like(came)))

    full = gather(jnp.concatenate([qkv_weight, out_weight.T[None]], axis=0), nz, ny, nx)

    def gathered(weight):
        share = weight.shape[0] // copies
        piece = lax.dynamic_slice_in_dim(weight, mine * share, share, 0)
        return lax.all_gather(piece, ALL, axis=0, tiled=True)

    up_rows = gathered(up_weight.T)
    down_rows = gathered(down_weight)
    kernel_all = lax.all_gather(kernels, "head", axis=2, tiled=True)
    up_bias_all = lax.all_gather(up_bias, "head", axis=0, tiled=True)
    kern = jnp.pad(kernel_all.reshape(9, -1), ((0, 7), (0, 0)))

    window = jnp.concatenate(pieces, axis=0)
    window_rows = shards * rows
    edge = EDGE if shards > 1 else 0
    late = window[window_rows - rows - edge:]
    linear_q = dot(late, full[0]).astype(jnp.bfloat16)
    linear_k = dot(window, full[1]).astype(jnp.bfloat16)
    linear_v = dot(window, full[2]).astype(jnp.bfloat16)
    attended, mass = attention_forward(before[None], linear_q, linear_k, linear_v, kern, rows)
    hidden = own_float + dot(attended, full[3], NT) + out_bias
    normed_two = (hidden * factor_of(hidden) * norm2_gain).astype(jnp.bfloat16)
    gate = jnp.maximum(dot(normed_two, up_rows, NT) + up_bias_all, 0.0)
    activation = jnp.square(gate).astype(jnp.bfloat16)
    gate_low = gate.astype(jnp.bfloat16)
    layer_output = (hidden + dot(activation, down_rows) + down_bias).astype(jnp.bfloat16)

    gate_grad = (2.0 * gate_low.astype(jnp.float32) * dot(cotangent, down_rows, NT)).astype(jnp.bfloat16)
    normed_two_grad = dot(gate_grad, up_rows)
    back_two, gain_rows = norm_backward(hidden, norm2_gain, normed_two_grad)
    hidden_grad = cotangent.astype(jnp.float32) + back_two
    hidden_low = hidden_grad.astype(jnp.bfloat16)
    attended_grad = dot(hidden_low, full[3]).astype(jnp.bfloat16)

    def blocks(columns):
        return columns.reshape(columns.shape[0], nz, -1).transpose(1, 0, 2)

    ff_grad = jnp.stack([
        jnp.stack([
            dot(normed_two, gate_grad[:, k * hidden_units:(k + 1) * hidden_units], TN).astype(jnp.bfloat16)
            if member == 0 else
            dot(cotangent, activation[:, k * hidden_units:(k + 1) * hidden_units], TN).astype(jnp.bfloat16)
            for member in range(2)
        ]) for k in range(nz)
    ])
    early = jnp.concatenate([
        jnp.sum(gain_rows, axis=0), jnp.sum(hidden_low.astype(jnp.float32), axis=0),
        jnp.sum(cotangent.astype(jnp.float32), axis=0), jnp.sum(gate_grad.astype(jnp.float32), axis=0),
    ]).reshape(-1, 1024)
    early = jnp.pad(early, ((0, -early.shape[0] % 8), (0, 0)))
    ff_sum, early = reduce(ff_grad, early, ny, nx, 1)

    grad_q, grad_k, grad_v, kernel_sums = attention_backward(
        before[None], linear_q, linear_k, linear_v, kern, attended_grad, attended, mass)
    normed_grad = dot(grad_k, full[1], NT) + dot(grad_v, full[2], NT)
    query_part = dot(grad_q, full[0], NT)
    normed_grad = normed_grad + jnp.pad(query_part, ((window_rows - rows - edge, 0), (0, 0)))
    normed_own_grad = normed_grad[window_rows - rows:]
    for hop in range(1, shards):
        at = window_rows - (hop + 1) * rows
        part = normed_grad[at:at + rows].astype(jnp.bfloat16)
        part = jnp.where(before >= hop, part, jnp.zeros_like(part))
        came = lax.ppermute(part, "head", [(i + hop, i) for i in range(nz - hop)])
        normed_own_grad = normed_own_grad + came.astype(jnp.float32)
    back_one, gain_rows_one = norm_backward(own_float, norm1_gain, normed_own_grad)
    layer_grad = (hidden_grad + back_one).astype(jnp.bfloat16)
    qkvo_grad = jnp.stack([
        blocks(dot(late, grad_q, TN).astype(jnp.bfloat16)),
        blocks(dot(window, grad_k, TN).astype(jnp.bfloat16)),
        blocks(dot(window, grad_v, TN).astype(jnp.bfloat16)),
        blocks(dot(hidden_low, attended, TN).astype(jnp.bfloat16)),
    ], axis=1)
    tail = jnp.concatenate([kernel_sums[:9], jnp.sum(gain_rows_one, axis=0)[None]], axis=0)
    tail = jnp.pad(tail, ((0, 6), (0, 0)))
    qkvo_sum, tail = reduce(qkvo_grad, tail, ny, nx, 2)

    width_all = norm1_gain.shape[0]
    early = early.reshape(-1)
    up_bias_grad = lax.dynamic_slice_in_dim(early[3 * width_all:], place * hidden_units, hidden_units, 0)
    kernels_grad = lax.dynamic_slice_in_dim(tail[:9].reshape(3, 3, -1), place * width, width, 2)
    f32 = jnp.float32
    return (
        layer_output[None], layer_grad[None], tail[9], qkvo_sum[:3].astype(f32), kernels_grad,
        qkvo_sum[3].T.astype(f32), early[width_all:2 * width_all], early[:width_all], ff_sum[0].astype(f32),
        up_bias_grad, ff_sum[1].T.astype(f32), early[2 * width_all:3 * width_all],
    )


def solution(mesh):
    rows = P(("batch", "dp"), "head", None)
    return jax.shard_map(
        on_device,
        mesh=mesh,
        in_specs=(
            rows, P(("batch", "dp"), None), P(), P(None, None, "head"), P(None, None, "head"), P("head", None), P(),
            P(), P(None, "head"), P("head"), P("head", None), P(), rows,
        ),
        out_specs=(
            rows, rows, P(), P(None, None, "head"), P(None, None, "head"), P("head", None),
            P(), P(), P(None, "head"), P("head"), P("head", None), P(),
        ),
        check_vma=False,
    )
```

time: 1480 us -> 835 us (0.56)
  waiting for transfers between devices: 925 us -> 15.8 us
  Pallas kernels: 70.7 us -> 427 us
  other arithmetic: 89.8 us -> 50.9 us
  local copies, waits for them, and re-layouts: 74.9 us -> 38.1 us
    reduce_scatter x4 -> x0, waiting for transfers between devices: 598 us -> none  [reduced(): lax.psum_scatter(grad.astype(jnp.bfloat16), ALL, scatter_dimension=axis,...]
    pallas_call x0 -> x3, Pallas kernels: none -> 327 us  [the longest x2 270 us: reduce(): pl.pallas_call(functools.partial(reduce_kernel, nz, ny, nx), out_shape=(j...]
    all_gather x7 -> x2, waiting for transfers between devices: 158 us -> 0.01 us  [gathered(): return lax.all_gather(piece, ALL, axis=0, tiled=True)]
    psum x1 -> x0, waiting for transfers between devices: 110 us -> none  [on_device(): lax.psum((gain_one_grad, gain_two_grad, out_bias_grad, down_bias_grad, up...]
    all_gather x1, blocking collectives: 13.2 us -> 82.2 us  [on_device(): kernel_all = lax.all_gather(kernels, 'head', axis=2, tiled=True)]
    all_gather x1, blocking collectives: 80.5 us -> 13.8 us  [on_device(): up_bias_all = lax.all_gather(up_bias, 'head', axis=0, tiled=True)]
    slice x11 -> x4, local copies, waits for them, and re-layouts: 48.1 us -> 2.84 us  [the longest x1 1.48 us: on_device(): early[2 * width_all:3 * width_all]]
    ppermute x2, waiting for transfers between devices: 59.2 us -> 15.8 us  [the longest x1 15.8 us: on_device(): came = lax.ppermute(part, 'head', [(i + hop, i) for i in range(nz - hop)])]
  transfers between devices with their start and end apart: 14 -> 4, of which waited for: 11 -> 1; matrix products, arithmetic and copies ran while one was open for 13% -> 11% of each run, Pallas kernels for 2% -> 11%
where the time goes in v2:
time: 835 us; the launch traced here: 827 us
  Pallas kernels  427 us (51%)
  matrix products  177 us (21%)
  blocking collectives  96 us (11%)
  other arithmetic  50.9 us (6%)
  local copies, waits for them, and re-layouts  38.1 us (5%)
  waiting for transfers between devices  15.8 us (2%)
  between operations  15.6 us (2%)
    pallas_call x2, Pallas kernels, reduce(): pl.pallas_call(functools.partial(reduce_kernel, nz, ny, nx), out_shape=(j...  270 us
    dot_general x24, matrix products, dot(): return lax.dot_general(a, b, dims, preferred_element_type=jnp.float32)  177 us
    all_gather x1, blocking collectives, on_device(): kernel_all = lax.all_gather(kernels, 'head', axis=2, tiled=True)  82.2 us
    pallas_call x1, Pallas kernels, attention_backward(): pl.pallas_call(functools.partial(backward_kernel, shards=shards, bq=bq, k...  68.3 us
    pallas_call x1, Pallas kernels, gather(): pl.pallas_call(functools.partial(gather_kernel, nz, ny, nx), out_shape=ja...  56.9 us
    pallas_call x1, Pallas kernels, attention_forward(): pl.pallas_call(functools.partial(forward_kernel, shards=shards, bq=bq, kc...  30.9 us
  transfers between devices with their start and end apart: 4, of which 1 were waited for; matrix products, arithmetic and copies ran while one was open for 11% of the time, Pallas kernels for 11%

profile of v2, /device:TPU:0, one launch (start us, length us, event | category | flops | bytes accessed | tf_op | source)
XLA Modules:
  0.0 826.6 jit_solution(17993395369299139068)
XLA Ops:
  22.7 82.2 %all_gather.12 = f32[3,3,1024]{2,1,0:T(4,128)S(1)} all-gather(f32[3,3,256]{2,1,0:T(4,128)S(1)} %copy-done.30), channel_id=1, replica_groups=mesh['head'=4,'batch'=4,'dp'=2] {'head'}, dimensions={2}, use_global_device_ids=true | all-gather | bytes 46080 | tf_op jit(solution)/shard_map/all_gather | solution.py:580
  106.8 56.9 %shard_map.220 = bf16[4,1024,1024]{2,1,0:T(8,128)(2,1)} custom-call(bf16[4,1024,256]{2,1,0:T(8,128)(2,1)S(1)} %pad_maximum_fusion.4.shard_ref), custom_call_target="tpu_custom_call" | custom-call | bytes 16777216 | tf_op jit(solution)/shard_map/pallas_call | solution.py:369
  163.8 13.8 %all_gather.14 = f32[4096]{0:T(1024)S(1)} all-gather(f32[1024]{0:T(1024)S(1)} %copy-done.31), channel_id=1, replica_groups=mesh['head'=4,'batch'=4,'dp'=2] {'head'}, dimensions={0}, use_global_device_ids=true | all-gather | bytes 20480 | tf_op jit(solution)/shard_map/all_gather | solution.py:581
  183.3 8.8 %convolution_convert_fusion.1.lv_ref = bf16[2048,1024]{1,0:T(8,128)(2,1)} fusion(bf16[4,1024,1024]{2,1,0:T(8,128)(2,1)S(1)} %bitcast.166, bf16[1024,1024]{1,0:T(8,128)(2,1)} %fusion.6, bf16[1024,1024]{1,0:T(8,128)(2,1)S(1)} %broadcast_select_fusion), kind=kOutput, calls=%fused_computation.42 | convolution fusion | flops 4305453056 | bytes 10485760 | tf_op jit(solution)/shard_map/dot_general | solution.py:25
  192.1 7.7 convolution_convert_fusion.2.lk_ref
  199.8 30.9 %shard_map.221 = (bf16[1024,1024]{1,0:T(8,128)(2,1)S(1)}, f32[8,8,1024]{2,1,0:T(8,128)S(1)}) custom-call(s32[1]{0:T(128)} %bitcast.3.before_ref, bf16[1040,1024]{1,0:T(8,128)(2,1)S(1)} %convolution_convert_fusion.lq_ref, bf16[2048,1024]{1,0:T(8,128)(2,1)} %convolution_convert_fusion.2.lk_ref, bf16[2048,1024]{1,0:T(8,128)(2,1)} %convolution_convert_fusion.1.lv_ref, ...), custom_call_target="tpu_custom_call" | custom-call | tf_op jit(solution)/shard_map/pallas_call | solution.py:128
  239.5 18.0 %multiply_convert_fusion = (bf16[1024,4096]{1,0:T(8,128)(2,1)}, f32[1024,4096]{1,0:T(8,128)}) fusion(f32[4096]{0:T(1024)S(1)} %all_gather.14, bf16[1024,1024]{1,0:T(8,128)(2,1)} %multiply_convert_fusion.1, bf16[4096,1024]{0,1:T(8,128)(2,1)} %all-gather.3.cloned.1.call-done), kind=kOutput, calls=%fused_computation.4 | convolution fusion | flops 8606711808 | bytes 35667968 | tf_op jit(solution)/shard_map/dot_general | solution.py:25
  257.5 16.8 %convert_reduce_fusion = (f32[4096]{0:T(1024)S(1)}, bf16[1024,4096]{1,0:T(8,128)(2,1)}) fusion(bf16[4096,1024]{1,0:T(8,128)(2,1)} %all-gather.5.cloned.1.call-done, bf16[1,1024,1024]{2,1,0:T(8,128)(2,1)S(1)} %copy-done.15, f32[1024,4096]{1,0:T(8,128)} %get-tuple-element.83, f32[4096]{0:T(1024)S(1)} %all_gather.14), kind=kOutput, calls=%fused_computation.3 | convolution fusion | flops 8627679232 | bytes 35684352 | tf_op jit(solution)/shard_map/dot_general | solution.py:25
  274.3 14.5 %multiply_reduce_fusion = (f32[1024]{0:T(1024)S(1)}, f32[1024]{0:T(1024)S(1)}, f32[1024,1024]{1,0:T(8,128)S(1)}) fusion(f32[1024,1024]{1,0:T(8,128)S(1)} %copy-done.10, f32[1024]{0:T(1024)S(1)} %add_rsqrt_fusion, f32[1024]{0:T(1024)S(1)} %copy-done.29, bf16[1024,4096]{1,0:T(8,128)(2,1)} %get-tuple-element.85, ...), kind=kOutput, calls=%fused_computation.36 | convolution fusion | flops 8596224000 | bytes 25182208 | tf_op jit(solution)/shard_map/dot_general | solution.py:25
  294.5 5.4 fusion.51.g_ref
  337.7 6.9 pad_maximum_fusion.grad_ref
  344.7 138.2 %shard_map.224 = (bf16[2,1024,1024]{2,1,0:T(8,128)(2,1)}, f32[8,1024]{1,0:T(8,128)}) custom-call(bf16[4,2,1024,1024]{3,2,1,0:T(8,128)(2,1)} %pad_maximum_fusion.grad_ref, f32[8,1024]{1,0:T(8,128)} %pad.19.small_ref), custom_call_target="tpu_custom_call" | custom-call | bytes 16777216 | tf_op jit(solution)/shard_map/pallas_call | solution.py:510
  485.1 68.3 %shard_map.222 = (bf16[1040,1024]{1,0:T(8,128)(2,1)}, bf16[2048,1024]{1,0:T(8,128)(2,1)}, bf16[2048,1024]{1,0:T(8,128)(2,1)}, f32[16,1024]{1,0:T(8,128)S(1)}) custom-call(s32[1]{0:T(128)} %bitcast.3.before_ref, bf16[1040,1024]{1,0:T(8,128)(2,1)} %copy-done.2, bf16[2048,1024]{1,0:T(8,128)(2,1)} %convolution_convert_fusion.2.lk_ref, ...), custom_call_target="tpu_custom_call" | custom-call | tf_op jit(solution)/shard_map/pallas_call | solution.py:218
  553.5 6.6 convolution_convert_fusion.6
  564.6 7.4 convolution_convert_fusion.5
  572.1 7.0 fusion.45
  586.0 9.3 %convolution_convert_fusion.4 = bf16[1024,1024]{0,1:T(8,128)(2,1)} fusion(bf16[2048,1024]{1,0:T(8,128)(2,1)} %get-tuple-element.25, bf16[1024,1024]{1,0:T(8,128)(2,1)} %fusion.6, bf16[1024,1024]{1,0:T(8,128)(2,1)} %copy-done.17), kind=kOutput, calls=%fused_computation.94 | convolution fusion | flops 4304404480 | bytes 10485760 | tf_op jit(solution)/shard_map/dot_general | solution.py:25
  603.2 11.5 %pad_add_fusion = f32[2048,1024]{1,0:T(8,128)S(1)} fusion(f32[1040,1024]{1,0:T(8,128)} %fusion.48, f32[2048,1024]{1,0:T(8,128)} %fusion.45, bf16[2048,1024]{1,0:T(8,128)(2,1)} %get-tuple-element.25, bf16[4,1024,1024]{2,1,0:T(8,128)(2,1)} %shard_map.220), kind=kOutput, calls=%fused_computation.8 | convolution fusion | flops 4299161600 | bytes 27328512 | tf_op jit(solution)/shard_map/dot_general | solution.py:25
  625.4 5.5 copy.53
  631.6 7.7 pad_maximum_fusion.1.grad_ref
  639.3 14.8 %fusion.15 = bf16[1,1024,1024]{2,1,0:T(8,128)(2,1)} fusion(f32[1024,1024]{1,0:T(8,128)S(1)} %copy-done.11, f32[1024]{0:T(1024)S(1)} %copy-done.35, bf16[1024,4096]{1,0:T(8,128)(2,1)} %get-tuple-element.82, bf16[4096,1024]{1,0:T(8,128)(2,1)} %all-gather.5.cloned.1.call-done), kind=kOutput, calls=%fused_computation.45 | convolution fusion | flops 8593080320 | bytes 23072768 | tf_op jit(solution)/shard_map/dot_general | solution.py:25
  654.1 15.8 %collective-permute-done.1 = bf16[1024,1024]{1,0:T(8,128)(2,1)} collective-permute-done((bf16[1024,1024]{1,0:T(8,128)(2,1)}, bf16[1024,1024]{1,0:T(8,128)(2,1)}, u32[]{:S(2)}, u32[]{:S(2)}) %collective-permute-start.1) | collective-permute-done | bytes 2097184 | tf_op jit(solution)/shard_map/ppermute | solution.py:634
  673.8 132.2 %shard_map.223 = (bf16[4,1024,256]{2,1,0:T(8,128)(2,1)}, f32[16,1024]{1,0:T(8,128)}) custom-call(bf16[4,4,1024,256]{3,2,1,0:T(8,128)(2,1)} %pad_maximum_fusion.1.grad_ref, f32[16,1024]{1,0:T(8,128)} %select_maximum_fusion.small_ref), custom_call_target="tpu_custom_call" | custom-call | bytes 8388608 | tf_op jit(solution)/shard_map/pallas_call | solution.py:510
  813.0 6.5 fusion.17
  (160 shorter events, 118.0 us)
Async XLA Ops:
  7.2 14.0 %copy-start.36 = (s32[1,3]{1,0:T(1,128)S(1)}, s32[1,3]{1,0:T(1,128)}, u32[]{:S(2)}) copy-start(s32[1,3]{1,0:T(1,128)} %param.14) | copy-start | bytes 40
  7.2 15.5 %copy-start.30 = (f32[3,3,256]{2,1,0:T(4,128)S(1)}, f32[3,3,256]{2,1,0:T(4,128)}, u32[]{:S(2)}) copy-start(f32[3,3,256]{2,1,0:T(4,128)} %param.17) | copy-start | bytes 27652
  7.2 97.8 %copy-start.24 = (bf16[256,1024]{1,0:T(8,128)(2,1)S(1)}, bf16[256,1024]{1,0:T(8,128)(2,1)}, u32[]{:S(2)}) copy-start(bf16[256,1024]{1,0:T(8,128)(2,1)} %param.18) | copy-start | bytes 1572868
  7.2 232.3 %all-gather.3.cloned.1.call-start = ((), (), s32[]{:S(2)}) async-start(), calls=%async_computation | async-start | bytes 8650752 | tf_op jit(solution)/shard_map/all_gather | solution.py:576
  9.6 247.9 %all-gather.5.cloned.1.call-start = ((), (), s32[]{:S(2)}) async-start(), calls=%async_computation.1 | async-start | bytes 8650752 | tf_op jit(solution)/shard_map/all_gather | solution.py:576
  16.1 161.5 %collective-permute-start = (bf16[1024,1024]{1,0:T(8,128)(2,1)}, bf16[1024,1024]{1,0:T(8,128)(2,1)S(1)}, u32[]{:S(2)}, u32[]{:S(2)}) collective-permute-start(bf16[1024,1024]{1,0:T(8,128)(2,1)} %fusion.6), channel_id=1, source_target_pairs={{0,8},{8,16},{16,24},{1,9},{9,17},{17,25},{2,10},{10,18},{18,26},{... | collective-permute-start | bytes 6291464 | tf_op jit(solution)/shard_map/ppermute | solution.py:568
  106.8 57.0 %copy-start.31 = (f32[1024]{0:T(1024)S(1)}, f32[1024]{0:T(1024)}, u32[]{:S(2)}) copy-start(f32[1024]{0:T(1024)} %param.22) | copy-start | bytes 12292
  177.8 14.3 %copy-start.17 = (bf16[1024,1024]{1,0:T(8,128)(2,1)}, bf16[1024,1024]{1,0:T(8,128)(2,1)S(1)}, u32[]{:S(2)}) copy-start(bf16[1024,1024]{1,0:T(8,128)(2,1)S(1)} %broadcast_select_fusion) | copy-start | bytes 6291460
  183.2 16.5 %copy-start.2 = (bf16[1040,1024]{1,0:T(8,128)(2,1)}, bf16[1040,1024]{1,0:T(8,128)(2,1)S(1)}, u32[]{:S(2)}) copy-start(bf16[1040,1024]{1,0:T(8,128)(2,1)S(1)} %convolution_convert_fusion.lq_ref) | copy-start | bytes 6389764
  199.8 30.9 %copy-start.7 = (bf16[1,1024,1024]{2,1,0:T(8,128)(2,1)S(1)}, bf16[1,1024,1024]{2,1,0:T(8,128)(2,1)}, u32[]{:S(2)}) copy-start(bf16[1,1024,1024]{2,1,0:T(8,128)(2,1)} %param.13) | copy-start | bytes 6291460
  199.8 30.9 %copy-start.34 = (f32[1024]{0:T(1024)S(1)}, f32[1024]{0:T(1024)}, u32[]{:S(2)}) copy-start(f32[1024]{0:T(1024)} %param.19) | copy-start | bytes 12292
  239.5 18.0 %copy-start.15 = (bf16[1,1024,1024]{2,1,0:T(8,128)(2,1)S(1)}, bf16[1,1024,1024]{2,1,0:T(8,128)(2,1)}, u32[]{:S(2)}) copy-start(bf16[1,1024,1024]{2,1,0:T(8,128)(2,1)} %param.25) | copy-start | bytes 6291460
  257.5 16.8 %copy-start.10 = (f32[1024,1024]{1,0:T(8,128)S(1)}, f32[1024,1024]{1,0:T(8,128)}, u32[]{:S(2)}) copy-start(f32[1024,1024]{1,0:T(8,128)} %copy-done.9) | copy-start | bytes 12582916
  274.3 14.5 %copy-start.16 = (bf16[1,1024,1024]{2,1,0:T(8,128)(2,1)S(1)}, bf16[1,1024,1024]{2,1,0:T(8,128)(2,1)}, u32[]{:S(2)}) copy-start(bf16[1,1024,1024]{2,1,0:T(8,128)(2,1)} %param.25) | copy-start | bytes 6291460
  290.7 9.2 %copy-start.12 = (f32[1024,1024]{1,0:T(8,128)}, f32[1024,1024]{1,0:T(8,128)S(1)}, u32[]{:S(2)}) copy-start(f32[1024,1024]{1,0:T(8,128)S(1)} %get-tuple-element.73) | copy-start | bytes 12582916
  344.7 140.5 %copy-start.5 = (bf16[1024,1024]{1,0:T(8,128)(2,1)S(1)}, bf16[1024,1024]{1,0:T(8,128)(2,1)}, u32[]{:S(2)}) copy-start(bf16[1024,1024]{1,0:T(8,128)(2,1)} %fusion.51.g_ref) | copy-start | bytes 6291460
  485.1 68.3 %copy-start.18 = (bf16[1024,1024]{1,0:T(8,128)(2,1)S(1)}, bf16[1024,1024]{1,0:T(8,128)(2,1)}, u32[]{:S(2)}) copy-start(bf16[1024,1024]{1,0:T(8,128)(2,1)} %copy-done.17) | copy-start | bytes 6291460
  485.1 75.0 %slice-start.4 = ((s8[8388608]{0:T(1024)(128)(4,1)}), s8[4194304]{0:T(1024)(128)(4,1)S(1)}, s32[]{:S(2)}) async-start(s8[8388608]{0:T(1024)(128)(4,1)} %bitcast.167), calls=%async_computation.6 | async-start | bytes 8388608
  619.6 50.3 %collective-permute-start.1 = (bf16[1024,1024]{1,0:T(8,128)(2,1)}, bf16[1024,1024]{1,0:T(8,128)(2,1)}, u32[]{:S(2)}, u32[]{:S(2)}) collective-permute-start(bf16[1024,1024]{1,0:T(8,128)(2,1)} %fusion.16), channel_id=1, source_target_pairs={{8,0},{16,8},{24,16},{9,1},{17,9},{25,17},{10,2},{18,10},{26,18},{... | collective-permute-start | bytes 6291464 | tf_op jit(solution)/shard_map/ppermute | solution.py:634
  631.6 38.3 %slice-start = ((s8[8388608]{0:T(1024)(128)(4,1)}), s8[4194304]{0:T(1024)(128)(4,1)S(1)}, s32[]{:S(2)}) async-start(s8[8388608]{0:T(1024)(128)(4,1)} %bitcast.163), calls=%async_computation.2 | async-start | bytes 8388608
  639.3 30.6 %copy-start.8 = (bf16[1,1024,1024]{2,1,0:T(8,128)(2,1)S(1)}, bf16[1,1024,1024]{2,1,0:T(8,128)(2,1)}, u32[]{:S(2)}) copy-start(bf16[1,1024,1024]{2,1,0:T(8,128)(2,1)} %param.13) | copy-start | bytes 6291460
  639.3 30.6 %slice-start.1 = ((s8[8388608]{0:T(1024)(128)(4,1)}), s8[4194304]{0:T(1024)(128)(4,1)S(1)}, s32[]{:S(2)}) async-start(s8[8388608]{0:T(1024)(128)(4,1)} %bitcast.163), calls=%async_computation.3 | async-start | bytes 8388608
  639.3 30.6 %copy-start.27 = (f32[1024]{0:T(1024)S(1)}, f32[1024]{0:T(1024)}, u32[]{:S(2)}) copy-start(f32[1024]{0:T(1024)} %copy-done.26) | copy-start | bytes 12292
  639.3 30.6 %copy-start.28 = (f32[1024]{0:T(1024)S(1)}, f32[1024]{0:T(1024)}, u32[]{:S(2)}) copy-start(f32[1024]{0:T(1024)} %param.15) | copy-start | bytes 12292
  (27 other events, 145.2 us)
Sparse Core Ops, SparseCore 0:
  11.5 122.8 all-gather.2
  137.4 77.4 all-gather.4

commit v3 on v1

v3 whole, which is shorter than its diff:
```python
import functools
import math

import jax
import jax.numpy as jnp
from jax import lax
from jax.experimental import pallas as pl
from jax.experimental.pallas import tpu as pltpu
from jax.sharding import PartitionSpec as P

LONG = 2048
EPSILON = 1e-06
ALL = ("head", "batch", "dp")

MESH = pl.DeviceIdType.MESH
VMEM = pl.BlockSpec(memory_space=pltpu.VMEM)


class Copy:
    def __init__(self, source, target, device, send_sem, recv_sem):
        self.parts = source, target, device, send_sem, recv_sem

    def make(self):
        source, target, device, send_sem, recv_sem = self.parts
        return pltpu.make_async_remote_copy(
            src_ref=source(), dst_ref=target(), send_sem=send_sem(), recv_sem=recv_sem(), device_id=device(), device_id_type=MESH)

    def start(self):
        self.make().start()

    def wait_recv(self):
        self.make().wait_recv()

    def wait_send(self):
        self.make().wait_send()


class Copies:
    def __init__(self, send_sems, recv_sems):
        self.send_sems, self.recv_sems, self.made = send_sems, recv_sems, []

    def plan(self, source, target, device):
        n = len(self.made)
        copy = Copy(source, target, device, lambda: self.send_sems.at[n], lambda: self.recv_sems.at[n])
        self.made.append(copy)
        return copy

    def finish(self):
        for copy in self.made:
            copy.wait_send()


def start(copies):
    for copy in copies:
        copy.start()


def arrive(copies):
    for copy in copies:
        copy.wait_recv()


class Place:
    def __init__(self, nz, ny, nx):
        self.nz, self.ny, self.nx = nz, ny, nx
        self.z, batch, self.x = lax.axis_index("head"), lax.axis_index("batch"), lax.axis_index("dp")
        self.y, self.c = batch // 2, batch % 2

    def along_z(self, step):
        return lambda: {"head": (self.z + step) % self.nz}

    def along_y(self, step):
        return lambda: {"batch": (self.y + step) % self.ny * 2 + self.c}

    def along_x(self, step):
        return lambda: {"dp": (self.x + step) % self.nx}

    def other_core(self):
        return {"batch": self.y * 2 + 1 - self.c}

    def meet(self):
        partners = [self.along_z(s) for s in range(1, self.nz)]
        partners += [self.along_y(s) for s in range(1, self.ny)] + [self.along_x(s) for s in range(1, self.nx)]
        partners.append(self.other_core)
        barrier = pltpu.get_barrier_semaphore()
        for partner in partners:
            pl.semaphore_signal(barrier, inc=1, device_id=partner(), device_id_type=MESH)
        pl.semaphore_wait(barrier, len(partners))

    def band(self, rows, dy, core=0):
        size = self.nx * rows
        core = self.c if core == 0 else 1 - self.c
        return pl.ds(pl.multiple_of(((self.y - dy) % self.ny * 2 + core) * size, size), size)

    def piece(self, rows, dy, dx):
        if dx is None:
            return self.band(rows, dy)
        at = ((self.y - dy) % self.ny * 2 + self.c) * self.nx + (self.x - dx) % self.nx
        return pl.ds(pl.multiple_of(at * rows, rows), rows)


def spread(place, copies, spots):
    ny, nx = place.ny, place.nx

    def plan(spot, dy, dx, device):
        part = lambda: spot(dy, dx)
        return copies.plan(part, part, device)

    over_x = [[plan(spot, 0, 0, place.along_x(s)) for s in range(1, nx)] for spot in spots]
    over_y = [[plan(spot, 0, 0, place.along_y(t)) for t in range(1, ny)] for spot in spots]
    corner_y = [plan(spots[0], 0, s, place.along_y(t)) for s in range(1, nx) for t in range(1, ny)]
    corner_x = [plan(spots[1], t, 0, place.along_x(s)) for s in range(1, nx) for t in range(1, ny)]
    cores = [plan(spot, dy, None, place.other_core) for spot in spots for dy in range(ny)]

    def out():
        for k in (0, 1):
            start(over_x[k])
            start(over_y[k])

    def turn():
        arrive(over_x[0])
        start(corner_y)
        arrive(over_y[1])
        start(corner_x)
        arrive(over_x[1])
        arrive(over_y[0])

    def cross():
        arrive(corner_y)
        arrive(corner_x)
        start(cores)

    return [out, turn, cross, lambda: arrive(cores)]


def spread_count(ny, nx):
    return 2 * ((nx - 1) + (ny - 1) + (nx - 1) * (ny - 1) + ny)


def gather_tasks(place, copies, shards, fulls):
    nz = place.nz

    def part(k, step):
        return lambda: fulls[k]((place.z - step) % nz, 0, 0)

    rings = [
        [copies.plan(part(k, step) if step else shards[k], part(k, step), place.along_z(1)) for k in range(2)]
        for step in range(nz - 1)
    ]

    def task(step):
        spots = [lambda dy, dx, k=k: fulls[k]((place.z - 1 - step) % nz, dy, dx) for k in range(2)]
        out, *others = spread(place, copies, spots)

        def arrival():
            arrive(rings[step])
            if step < nz - 2:
                start(rings[step + 1])
            out()

        return [arrival] + others

    return lambda: start(rings[0]), [task(step) for step in range(nz - 1)]


def gather_count(nz, ny, nx):
    return (nz - 1) * (2 + spread_count(ny, nx))


def run_staggered(tasks):
    phases = [(at + n, n, phase) for n, task in enumerate(tasks) for at, phase in enumerate(task)]
    for _, _, phase in sorted(phases, key=lambda entry: entry[:2]):
        phase()


class Timetable:
    def __init__(self, per_step, steps):
        self.per_step, self.steps, self.at = per_step, steps, {}

    def add(self, task, times):
        for time, phase in zip(times, task, strict=True):
            self.at.setdefault(time, []).append(phase)

    def tick(self, slot):
        for time in range(slot, self.per_step * self.steps, self.per_step):
            if time in self.at:
                @pl.when(pl.program_id(0) == time // self.per_step)
                def _():
                    for phase in self.at[time]:
                        phase()

    def finish(self):
        for time in sorted(self.at):
            if time >= self.per_step * self.steps:
                for phase in self.at[time]:
                    phase()


def open_kernel(nz, ny, nx, shard_ref, small_ref, full_ref, all_ref, send_sems, recv_sems):
    place = Place(nz, ny, nx)
    copies = Copies(send_sems, recv_sems)
    members, height, width = shard_ref.shape
    half = members // 2
    rows = height // (ny * 2 * nx)

    def columns(block):
        return pl.ds(pl.multiple_of(block * width, width), width)

    fulls = [
        lambda block, dy, dx, lo=lo, hi=hi: full_ref.at[lo:hi, place.piece(rows, dy, dx), columns(block)]
        for lo, hi in ((0, half), (half, members))
    ]
    shards = [lambda lo=lo, hi=hi: shard_ref.at[lo:hi, place.piece(rows, 0, 0), :] for lo, hi in ((0, half), (half, members))]
    begin, tasks = gather_tasks(place, copies, shards, fulls)
    small = [copies.plan(lambda: small_ref, lambda: all_ref.at[place.z], place.along_z(s)) for s in range(1, nz)]
    place.meet()
    begin()
    start(small)
    all_ref[place.z] = small_ref[...]
    for m in range(members):
        full_ref[m, :, columns(place.z)] = shard_ref[m]
    run_staggered(tasks)
    arrive(small)
    copies.finish()


def gather_open(shard, small, nz, ny, nx):
    members, height, width = shard.shape
    count = gather_count(nz, ny, nx) + nz - 1
    return pl.pallas_call(
        functools.partial(open_kernel, nz, ny, nx),
        out_shape=(jax.ShapeDtypeStruct((members, height, width * nz), shard.dtype),
                   jax.ShapeDtypeStruct((nz,) + small.shape, small.dtype)),
        in_specs=[VMEM, VMEM],
        out_specs=(VMEM, VMEM),
        scratch_shapes=[pltpu.SemaphoreType.DMA((count,)), pltpu.SemaphoreType.DMA((count,))],
        compiler_params=pltpu.CompilerParams(collective_id=0, has_side_effects=True, vmem_limit_bytes=48 << 20),
        cost_estimate=pl.CostEstimate(flops=0, bytes_accessed=2 * members * height * width * nz * 2, transcendentals=0),
    )(shard, small)


class Reduction:
    def __init__(self, place, copies, grad_ref, out_ref, buffers):
        self.place, self.copies, self.grad, self.out = place, copies, grad_ref, out_ref
        self.core, self.y1, self.x1, self.x2, self.y2, self.z_send, self.z_buf = buffers
        self.members, self.height, self.width = grad_ref.shape[1:]
        self.half = self.members // 2
        self.rows = self.height // (place.ny * 2 * place.nx)
        self.sums = []

    @staticmethod
    def scratch(nz, ny, nx, members, height, width):
        half, rows, bf = members // 2, height // (ny * 2 * nx), jnp.bfloat16
        band = nx * rows
        return [
            pltpu.VMEM((nz, ny, members, band, width), bf),
            pltpu.VMEM((nz, ny - 1, half, band, width), bf),
            pltpu.VMEM((nz, nx - 1, ny, half, rows, width), bf),
            pltpu.VMEM((nz, nx - 1, half, rows, width), bf),
            pltpu.VMEM((nz, ny - 1, half, rows, width), bf),
            pltpu.VMEM((nz, members, rows, width), bf),
            pltpu.VMEM((nz - 1, members, rows, width), bf),
        ]

    @staticmethod
    def count(nz, ny, nx):
        return nz * (ny + 2 * (ny - 1) + 2 * (nx - 1)) + nz - 1 + spread_count(ny, nx)

    def chunk(self, t):
        place, copies, half, rows = self.place, self.copies, self.half, self.rows
        ny, nx, nz = place.ny, place.nx, place.nz
        core, x1, y1, x2, y2, f32, bf = self.core, self.x1, self.y1, self.x2, self.y2, jnp.float32, jnp.bfloat16

        def xrows(step):
            return pl.ds(pl.multiple_of((place.x + step) % nx * rows, rows), rows)

        sent = [
            copies.plan(
                lambda dy=dy: self.grad.at[(place.z + 1 + t) % nz, :, place.band(rows, dy, 1), :],
                lambda dy=dy: core.at[t, dy], place.other_core)
            for dy in range(ny)
        ]
        over_y = [
            copies.plan(lambda s=s: core.at[t, ny - s, 0:half], lambda s=s: y1.at[t, s - 1], place.along_y(s))
            for s in range(1, ny)
        ]
        over_x = [
            copies.plan(lambda s=s: core.at[t, :, half:, xrows(s), :], lambda s=s: x1.at[t, s - 1], place.along_x(s))
            for s in range(1, nx)
        ]
        then_x = [
            copies.plan(lambda s=s: core.at[t, 0, 0:half, xrows(s), :], lambda s=s: x2.at[t, s - 1], place.along_x(s))
            for s in range(1, nx)
        ]
        then_y = [
            copies.plan(lambda s=s: core.at[t, ny - s, half:, xrows(0), :], lambda s=s: y2.at[t, s - 1], place.along_y(s))
            for s in range(1, ny)
        ]
        along = [copies.plan(lambda: self.z_send.at[t], lambda: self.z_buf.at[t], place.along_z(1 + t))] if t < nz - 1 else []
        self.sums += along

        def both_cores():
            arrive(sent)
            for dy in range(ny):
                for m in range(self.members):
                    own = self.grad[(place.z + 1 + t) % nz, m, place.band(rows, dy), :]
                    core[t, dy, m] = (core[t, dy, m].astype(f32) + own.astype(f32)).astype(bf)
            start(over_y)
            start(over_x)

        def turn():
            arrive(over_y)
            for m in range(half):
                total = core[t, 0, m].astype(f32)
                for s in range(ny - 1):
                    total = total + y1[t, s, m].astype(f32)
                core[t, 0, m] = total.astype(bf)
            start(then_x)
            arrive(over_x)
            for dy in range(ny):
                for m in range(half):
                    total = core[t, dy, half + m, xrows(0), :].astype(f32)
                    for s in range(nx - 1):
                        total = total + x1[t, s, dy, m].astype(f32)
                    core[t, dy, half + m, xrows(0), :] = total.astype(bf)
            start(then_y)

        def send_on():
            arrive(then_x)
            arrive(then_y)
            for m in range(self.members):
                total = core[t, 0, m, xrows(0), :].astype(f32)
                buf, n = (x2, nx - 1) if m < half else (y2, ny - 1)
                for s in range(n):
                    total = total + buf[t, s, m % half].astype(f32)
                self.z_send[t, m] = total.astype(bf)
            start(along)

        return [lambda: start(sent), both_cores, turn, send_on]

    def ending(self):
        place, nz = self.place, self.place.nz
        spots = [
            lambda dy, dx, lo=lo, hi=hi: self.out.at[lo:hi, place.piece(self.rows, dy, dx), :]
            for lo, hi in ((0, self.half), (self.half, self.members))
        ]
        out, *others = spread(place, self.copies, spots)

        def total():
            arrive(self.sums)
            for m in range(self.members):
                total = self.z_send[nz - 1, m].astype(jnp.float32)
                for t in range(nz - 1):
                    total = total + self.z_buf[t, m].astype(jnp.float32)
                self.out[m, place.piece(self.rows, 0, 0), :] = total.astype(jnp.bfloat16)
            out()

        return [total] + others


def small_sum(place, copies, small_ref, out_ref, s_acc, s_buf):
    nz, ny, nx = place.nz, place.ny, place.nx
    stages = ([place.other_core], [place.along_x(s) for s in range(1, nx)],
              [place.along_y(s) for s in range(1, ny)], [place.along_z(s) for s in range(1, nz)])
    firsts = [0, 1, nx, nx + ny - 1]
    sent = [
        [copies.plan(lambda k=k: s_acc.at[k], lambda n=firsts[k] + i: s_buf.at[n], partner) for i, partner in enumerate(partners)]
        for k, partners in enumerate(stages)
    ]

    def add(k):
        arrive(sent[k])
        total = s_acc[k]
        for i in range(len(sent[k])):
            total = total + s_buf[firsts[k] + i]
        return total

    def first():
        s_acc[0] = small_ref[...]
        start(sent[0])

    def middle(k):
        s_acc[k + 1] = add(k)
        start(sent[k + 1])

    def last():
        out_ref[...] = add(3)

    return [first] + [functools.partial(middle, k) for k in range(3)] + [last]


def small_scratch(nz, ny, nx, shape):
    return [pltpu.VMEM((4,) + shape, jnp.float32), pltpu.VMEM((nx + ny + nz - 2,) + shape, jnp.float32)]


def reduce_kernel(nz, ny, nx, grad_ref, small_ref, out_ref, small_out_ref, *scratch):
    *buffers, s_acc, s_buf, send_sems, recv_sems = scratch
    place = Place(nz, ny, nx)
    copies = Copies(send_sems, recv_sems)
    place.meet()
    whole = Reduction(place, copies, grad_ref, out_ref, buffers)
    run_staggered([whole.chunk(0), small_sum(place, copies, small_ref, small_out_ref, s_acc, s_buf)]
                  + [whole.chunk(t) for t in range(1, nz)])
    for phase in whole.ending():
        phase()
    copies.finish()


def reduce(grad, small, ny, nx, collective_id):
    nz, members, height, width = grad.shape
    count = Reduction.count(nz, ny, nx) + nx + ny + nz - 2
    return pl.pallas_call(
        functools.partial(reduce_kernel, nz, ny, nx),
        out_shape=(jax.ShapeDtypeStruct((members, height, width), jnp.bfloat16), jax.ShapeDtypeStruct(small.shape, jnp.float32)),
        in_specs=[VMEM, VMEM],
        out_specs=(VMEM, VMEM),
        scratch_shapes=Reduction.scratch(nz, ny, nx, members, height, width) + small_scratch(nz, ny, nx, small.shape) + [
            pltpu.SemaphoreType.DMA((count,)), pltpu.SemaphoreType.DMA((count,)),
        ],
        compiler_params=pltpu.CompilerParams(collective_id=collective_id, has_side_effects=True, vmem_limit_bytes=56 << 20),
        cost_estimate=pl.CostEstimate(flops=0, bytes_accessed=grad.size * 2, transcendentals=0),
    )(grad, small)


HS = 64
LANES = 128
EDGE = 16
LOG2E = math.log2(math.e)
NT = (((1,), (1,)), ((), ()))
NN = (((1,), (0,)), ((), ()))
TN = (((0,), (0,)), ((), ()))


def dot(a, b, dims=NN):
    return lax.dot_general(a, b, dims, preferred_element_type=jnp.float32)


def spans(first, last, step):
    return [(at, min(step, last - at)) for at in range(first, last, step)]


def earlier(ref, start, size):
    if start == 0:
        rows = jnp.concatenate([jnp.zeros((EDGE, LANES), jnp.float32), ref[pl.ds(0, size), :].astype(jnp.float32)], axis=0)
    else:
        rows = ref[pl.ds(start - EDGE, size + EDGE), :].astype(jnp.float32)
    return [pltpu.roll(rows, i, 0)[EDGE:] if i else rows[EDGE:] for i in range(3)]


def convolve(linear_ref, kern_ref, member, target_ref, skip, step=256):
    total = linear_ref.shape[0]
    for start, size in spans(skip, total, step):
        taps = earlier(linear_ref, start, size)
        value = sum(kern_ref[3 * member + i:3 * member + i + 1, :] * taps[i] for i in range(3))
        target_ref[pl.ds(start - skip, size), :] = value.astype(jnp.bfloat16)


def convolve_back(grad_ref, linear_ref, kern_ref, member, target_ref, sums_ref, step=256):
    total = linear_ref.shape[0]
    parts = [jnp.zeros((8, LANES), jnp.float32)] * 3
    for start, size in spans(0, total, step):
        rows = grad_ref[pl.ds(start, size + 8), :]
        value = kern_ref[3 * member:3 * member + 1, :] * rows[:size]
        for i in (1, 2):
            value += kern_ref[3 * member + i:3 * member + i + 1, :] * pltpu.roll(rows, size + 8 - i, 0)[:size]
        target_ref[pl.ds(start, size), :] = value.astype(jnp.bfloat16)
        taps = earlier(linear_ref, start, size)
        for i in range(3):
            parts[i] += jnp.sum((rows[:size] * taps[i]).reshape(size // 8, 8, LANES), axis=0)
    for i in range(3):
        sums_ref[3 * member + i:3 * member + i + 1, :] = jnp.sum(parts[i], axis=0, keepdims=True)


def parts_of(rows, shards, at, size, step):
    own = (shards - 1) * rows
    pieces = []
    for hop in range(shards - 1, 0, -1):
        pieces += [(start, n, hop) for start, n in spans(own - hop * rows, own - (hop - 1) * rows, step)]
    pieces += [(start, n, 0) for start, n in spans(own, own + at, step)]
    return pieces + [(own + at, size, None)]


def forward_kernel(
    nz, ny, nx, steps, bq, kc, plan, far_ref, lq_ref, lk_ref, lv_ref, kern_ref, up_ref, down_ref,
    out_ref, mass_ref, up_out_ref, down_out_ref, q_ref, k_ref, v_ref, s0_ref, s1_ref, up_all_ref, down_all_ref,
    send_sems, recv_sems, out_sems,
):
    rows, window = q_ref.shape[0], k_ref.shape[0]
    shards = window // rows
    lane = lax.broadcasted_iota(jnp.int32, (bq, LANES), 1) < HS
    scale = 1.0 / math.sqrt(HS)

    place = Place(nz, ny, nx)
    copies = Copies(send_sems, recv_sems)
    units = up_ref.shape[0]
    share = units // (ny * 2 * nx)

    def spot(ref):
        def at(block, dy, dx):
            return ref.at[pl.ds(pl.multiple_of(block * units, units), units), :].at[place.piece(share, dy, dx), :]
        return at

    begin, tasks = gather_tasks(
        place, copies, [lambda ref=ref: ref.at[place.piece(share, 0, 0), :] for ref in (up_ref, down_ref)],
        [spot(up_all_ref), spot(down_all_ref)])

    def store(step):
        part = pl.ds(pl.multiple_of((place.z - step) % nz * units, units), units)
        pairs = ((up_ref, up_all_ref, up_out_ref), (down_ref, down_all_ref, down_out_ref))
        return [
            pltpu.make_async_copy(whole.at[part, :] if step else own, out.at[part, :], out_sems.at[2 * step + k])
            for k, (own, whole, out) in enumerate(pairs)
        ]

    def and_store(phase, step):
        def both():
            phase()
            start(store(step))
        return both

    @pl.when(pl.program_id(0) == 0)
    def _():
        place.meet()
        begin()
        start(store(0))

    table = Timetable(rows // bq, steps)
    for step, (task, ticks) in enumerate(zip(tasks, plan, strict=True)):
        table.add(task[:-1] + [and_store(task[-1], step + 1)], ticks)

    convolve(lq_ref, kern_ref, 0, q_ref, lq_ref.shape[0] - rows)
    convolve(lk_ref, kern_ref, 1, k_ref, 0)
    convolve(lv_ref, kern_ref, 2, v_ref, 0)

    def block(at):
        query = q_ref[pl.ds(at, bq), :] * jnp.bfloat16(scale)
        zero = jnp.zeros_like(query)
        queries = (jnp.where(lane, query, zero), jnp.where(lane, zero, query))
        stores = (s0_ref, s1_ref)
        peaks = [{}, {}]
        parts = parts_of(rows, shards, at, bq, kc)
        for start, size, hop in parts:
            key = k_ref[pl.ds(start, size), :]
            for h in range(2):
                s = dot(queries[h], key, NT)
                if hop is None:
                    row = lax.broadcasted_iota(jnp.int32, (bq, size), 0)
                    col = lax.broadcasted_iota(jnp.int32, (bq, size), 1)
                    s = jnp.where(col <= row, s, -1e30)
                stores[h][:, pl.ds(start, size)] = s
                top = jnp.max(s, axis=1, keepdims=True)
                group = hop or 0
                peaks[h][group] = jnp.maximum(peaks[h][group], top) if group in peaks[h] else top
        sums = [None, None]
        peak, scaled = [], [{}, {}]
        for h in range(2):
            top = peaks[h][0]
            for hop in range(1, shards):
                top = jnp.maximum(top, peaks[h][hop] - far_ref[hop - 1:hop, 0:1])
            peak.append(top)
            scaled[h][0] = top * LOG2E
            for hop in range(1, shards):
                scaled[h][hop] = scaled[h][0] + far_ref[hop - 1:hop, 0:1]
        for start, size, hop in parts:
            value = v_ref[pl.ds(start, size), :]
            wide = lax.broadcasted_iota(jnp.int32, (size, LANES), 1) < HS
            one = jnp.ones_like(value)
            values = (jnp.where(wide, value, one), jnp.where(wide, one, value))
            for h in range(2):
                p = jnp.exp2(stores[h][:, pl.ds(start, size)] * LOG2E - scaled[h][hop or 0]).astype(jnp.bfloat16)
                o = dot(p, values[h])
                sums[h] = o if sums[h] is None else sums[h] + o
        total = pltpu.roll(jnp.where(lane, sums[1], sums[0]), HS, 1)
        out_ref[pl.ds(at, bq), :] = (jnp.where(lane, sums[0], sums[1]) / total).astype(out_ref.dtype)
        mass = jnp.where(lane, peak[0], peak[1]) + jnp.log(total)
        mass = mass.T
        mass_ref[0, 0:1, pl.ds(at, bq)] = mass[0:1]
        mass_ref[0, 1:2, pl.ds(at, bq)] = mass[HS:HS + 1]

    for slot, at in enumerate(range(0, rows, bq)):
        table.tick(slot)
        block(at)

    @pl.when(pl.program_id(0) == steps - 1)
    def _():
        table.finish()
        for step in range(nz):
            for copy in store(step):
                copy.wait()
        copies.finish()


def column(n):
    return pl.BlockSpec((n, LANES), lambda i: (0, i))


ANY = pl.BlockSpec(memory_space=pl.ANY)
WHOLE = pl.BlockSpec((8, LANES), lambda i: (0, 0))


def attention_forward(far, late, linear_k, linear_v, kern, up, down, rows, nz, ny, nx):
    edged, width = late.shape
    window = linear_k.shape[0]
    pairs = width // LANES
    bq = min(512, rows)
    units, depth = up.shape
    bf = jnp.bfloat16
    count = gather_count(nz, ny, nx)
    slots = rows // bq
    first = [round(3.6 * (s + 1)) for s in range(nz - 1)]
    plan = [(f, f + 4, f + 6, f + 7) for f in first]
    return pl.pallas_call(
        functools.partial(forward_kernel, nz, ny, nx, pairs, bq, 512, plan),
        out_shape=(jax.ShapeDtypeStruct((rows, width), bf), jax.ShapeDtypeStruct((pairs, 8, rows), jnp.float32),
                   jax.ShapeDtypeStruct((nz * units, depth), bf), jax.ShapeDtypeStruct((nz * units, depth), bf)),
        grid=(pairs,),
        in_specs=[WHOLE, column(edged), column(window), column(window), column(16), VMEM, VMEM],
        out_specs=[column(rows), pl.BlockSpec((1, 8, rows), lambda i: (i, 0, 0)), ANY, ANY],
        scratch_shapes=[
            pltpu.VMEM((rows, LANES), bf), pltpu.VMEM((window, LANES), bf), pltpu.VMEM((window, LANES), bf),
            pltpu.VMEM((bq, window), jnp.float32), pltpu.VMEM((bq, window), jnp.float32),
            pltpu.VMEM((nz * units, depth), bf), pltpu.VMEM((nz * units, depth), bf),
            pltpu.SemaphoreType.DMA((count,)), pltpu.SemaphoreType.DMA((count,)), pltpu.SemaphoreType.DMA((2 * nz,)),
        ],
        compiler_params=pltpu.CompilerParams(collective_id=1, has_side_effects=True, vmem_limit_bytes=56 << 20),
    )(far, late, linear_k, linear_v, kern, up, down)


def backward_kernel(
    nz, ny, nx, steps, bq, kc, plan, far_ref, lq_ref, lk_ref, lv_ref, kern_ref, g_ref, o_ref, mass_ref, grad_ref, small_ref,
    gq_ref, gk_ref, gv_ref, sums_ref, total_ref, small_out_ref,
    q_ref, k_ref, v_ref, kt_ref, dq_ref, dk_ref, dv_ref, *scratch,
):
    rows, window = q_ref.shape[0], k_ref.shape[0]
    shards = window // rows
    edge = lq_ref.shape[0] - rows
    lane = lax.broadcasted_iota(jnp.int32, (bq, LANES), 1) < HS
    scale = 1.0 / math.sqrt(HS)

    *buffers, s_acc, s_buf, sum_ref, send_sems, recv_sems, out_sem = scratch
    place = Place(nz, ny, nx)
    copies = Copies(send_sems, recv_sems)

    @pl.when(pl.program_id(0) == 0)
    def _():
        place.meet()

    whole = Reduction(place, copies, grad_ref, sum_ref, buffers)
    table = Timetable(rows // bq, steps)
    chunk_plan, small_plan, ending_plan = plan
    for t, ticks in enumerate(chunk_plan):
        table.add(whole.chunk(t), ticks)
    table.add(small_sum(place, copies, small_ref, small_out_ref, s_acc, s_buf), small_plan)
    table.add(whole.ending(), ending_plan)

    convolve(lq_ref, kern_ref, 0, q_ref, edge)
    convolve(lk_ref, kern_ref, 1, k_ref, 0)
    convolve(lv_ref, kern_ref, 2, v_ref, 0)
    dk_ref[...] = jnp.zeros_like(dk_ref)
    dv_ref[...] = jnp.zeros_like(dv_ref)
    if edge:
        dq_ref[pl.ds(0, edge), :] = jnp.zeros((edge, LANES), jnp.float32)
    dq_ref[pl.ds(edge + rows, 8), :] = jnp.zeros((8, LANES), jnp.float32)
    kt_ref[...] = k_ref[...].astype(jnp.float32).T.astype(jnp.bfloat16)

    def block(at):
        query = q_ref[pl.ds(at, bq), :] * jnp.bfloat16(scale)
        grad = g_ref[pl.ds(at, bq), :]
        zero = jnp.zeros_like(query)
        queries = (jnp.where(lane, query, zero), jnp.where(lane, zero, query))
        grads = (jnp.where(lane, grad, zero), jnp.where(lane, zero, grad))
        product = (grad.astype(jnp.float32) * o_ref[pl.ds(at, bq), :].astype(jnp.float32)).T
        query_grads = [jnp.zeros((HS, bq), jnp.float32)] * 2
        deltas = [jnp.sum(product[h * HS:(h + 1) * HS], axis=0, keepdims=True) for h in range(2)]
        masses = [mass_ref[0, h:h + 1, pl.ds(at, bq)] * LOG2E for h in range(2)]
        for start, size, hop in parts_of(rows, shards, at, bq, kc):
            key = k_ref[pl.ds(start, size), :]
            value = v_ref[pl.ds(start, size), :]
            key_part = value_part = None
            for h in range(2):
                s = dot(key, queries[h], NT)
                if hop is None:
                    row = lax.broadcasted_iota(jnp.int32, (size, bq), 1)
                    col = lax.broadcasted_iota(jnp.int32, (size, bq), 0)
                    s = jnp.where(col <= row, s, -1e30)
                mass = masses[h] + far_ref[hop - 1:hop, 0:1] if hop else masses[h]
                p = jnp.exp2(s * LOG2E - mass)
                dp = dot(value, grads[h], NT)
                ds = (p * (dp - deltas[h])).astype(jnp.bfloat16)
                a = dot(p.astype(jnp.bfloat16), grads[h])
                b = dot(ds, queries[h])
                value_part = a if value_part is None else value_part + a
                key_part = b if key_part is None else key_part + b
                query_grads[h] += dot(kt_ref[h * HS:(h + 1) * HS, pl.ds(start, size)], ds)
            dk_ref[pl.ds(start, size), :] += key_part
            dv_ref[pl.ds(start, size), :] += value_part
        dq_ref[pl.ds(edge + at, bq), :] = jnp.concatenate(query_grads, axis=0).T * scale

    for slot, at in enumerate(range(0, rows, bq)):
        table.tick(slot)
        block(at)

    sums_ref[...] = jnp.zeros_like(sums_ref)
    convolve_back(dq_ref, lq_ref, kern_ref, 0, gq_ref, sums_ref)
    convolve_back(dk_ref, lk_ref, kern_ref, 1, gk_ref, sums_ref)
    convolve_back(dv_ref, lv_ref, kern_ref, 2, gv_ref, sums_ref)

    @pl.when(pl.program_id(0) == steps - 1)
    def _():
        table.finish()
        out = pltpu.make_async_copy(sum_ref, total_ref, out_sem)
        out.start()
        copies.finish()
        out.wait()


def attention_backward(far, late, linear_k, linear_v, kern, grads, outs, mass, ff_grad, small, ny, nx):
    rows = grads.shape[0]
    edged, width = late.shape
    window = linear_k.shape[0]
    pairs = width // LANES
    bq = min(256, rows)
    bf = jnp.bfloat16
    nz, members, height, columns = ff_grad.shape
    count = Reduction.count(nz, ny, nx) + nx + ny + nz - 2
    ticks = pairs * (rows // bq)
    gap = max(1, ticks // 2 // nz)
    chunks = [(gap * t, gap * t + 3, gap * t + 7, gap * t + 10) for t in range(nz)]
    end = max(chunks[-1][-1] + 1, ticks - 5)
    plan = (chunks, range(2, 12, 2), (end, end + 4, end + 6, end + 7))
    return pl.pallas_call(
        functools.partial(backward_kernel, nz, ny, nx, pairs, bq, 1024, plan),
        out_shape=(jax.ShapeDtypeStruct((edged, width), bf), jax.ShapeDtypeStruct((window, width), bf),
                   jax.ShapeDtypeStruct((window, width), bf), jax.ShapeDtypeStruct((16, width), jnp.float32),
                   jax.ShapeDtypeStruct((members, height, columns), bf), jax.ShapeDtypeStruct(small.shape, jnp.float32)),
        grid=(pairs,),
        in_specs=[WHOLE, column(edged), column(window), column(window), column(16), column(rows), column(rows),
                  pl.BlockSpec((1, 8, rows), lambda i: (i, 0, 0)), VMEM, VMEM],
        out_specs=[column(edged), column(window), column(window), column(16), ANY, VMEM],
        scratch_shapes=[
            pltpu.VMEM((rows, LANES), bf), pltpu.VMEM((window, LANES), bf), pltpu.VMEM((window, LANES), bf),
            pltpu.VMEM((LANES, window), bf), pltpu.VMEM((edged + 8, LANES), jnp.float32),
            pltpu.VMEM((window + 8, LANES), jnp.float32), pltpu.VMEM((window + 8, LANES), jnp.float32),
        ] + Reduction.scratch(nz, ny, nx, members, height, columns) + small_scratch(nz, ny, nx, small.shape) + [
            pltpu.VMEM((members, height, columns), bf),
            pltpu.SemaphoreType.DMA((count,)), pltpu.SemaphoreType.DMA((count,)), pltpu.SemaphoreType.DMA,
        ],
        compiler_params=pltpu.CompilerParams(collective_id=2, has_side_effects=True, vmem_limit_bytes=60 << 20),
    )(far, late, linear_k, linear_v, kern, grads, outs, mass, ff_grad, small)


def factor_of(values):
    return lax.rsqrt(jnp.mean(values * values, axis=-1, keepdims=True) + EPSILON)


def norm_backward(values, gain, upstream):
    factor = factor_of(values)
    unit = values * factor
    scaled = gain * upstream
    result = factor * (scaled - unit * jnp.mean(scaled * unit, axis=-1, keepdims=True))
    return result, upstream * unit


def on_device(
    layer_input, lengths, norm1_gain, qkv_weight, kernels, out_weight, out_bias,
    norm2_gain, up_weight, up_bias, down_weight, down_bias, out_grad,
):
    rows = layer_input.shape[1]
    nz, nb, nx = lax.axis_size("head"), lax.axis_size("batch"), lax.axis_size("dp")
    ny = nb // 2
    shards = max(1, LONG // rows)
    place = lax.axis_index("head")
    width = qkv_weight.shape[2]
    hidden_units = up_weight.shape[1]

    first_row = place * rows
    ends = jnp.cumsum(lengths[0])
    begins = jnp.max(jnp.where(ends <= first_row, ends, 0))
    before = ((first_row - begins) // rows).astype(jnp.int32)

    own_float = layer_input[0].astype(jnp.float32)
    cotangent = out_grad[0]
    normed_own = (own_float * factor_of(own_float) * norm1_gain).astype(jnp.bfloat16)
    pieces = [normed_own]
    for hop in range(1, shards):
        came = lax.ppermute(normed_own, "head", [(i, i + hop) for i in range(nz - hop)])
        pieces.insert(0, jnp.where(before >= hop, came, jnp.zeros_like(came)))

    small = jnp.concatenate([kernels.reshape(9, width), up_bias.reshape(-1, width)], axis=0)
    small = jnp.pad(small, ((0, -small.shape[0] % 8), (0, 0)))
    full, small = gather_open(jnp.concatenate([qkv_weight, out_weight.T[None]], axis=0), small, nz, ny, nx)
    kern = jnp.pad(small[:, :9].transpose(1, 0, 2).reshape(9, -1), ((0, 7), (0, 0)))
    up_bias_all = small[:, 9:9 + hidden_units // width].reshape(-1)

    window = jnp.concatenate(pieces, axis=0)
    window_rows = shards * rows
    edge = EDGE if shards > 1 else 0
    late = window[window_rows - rows - edge:]
    linear_q = dot(late, full[0]).astype(jnp.bfloat16)
    linear_k = dot(window, full[1]).astype(jnp.bfloat16)
    linear_v = dot(window, full[2]).astype(jnp.bfloat16)
    hops = jnp.arange(1, 9)[:, None]
    far = jnp.broadcast_to(jnp.where(before >= hops, 0.0, 1e30), (8, LANES)).astype(jnp.float32)
    attended, mass, up_rows, down_rows = attention_forward(
        far, linear_q, linear_k, linear_v, kern, up_weight.T, down_weight, rows, nz, ny, nx)
    hidden = own_float + dot(attended, full[3], NT) + out_bias
    normed_two = (hidden * factor_of(hidden) * norm2_gain).astype(jnp.bfloat16)
    gate = jnp.maximum(dot(normed_two, up_rows, NT) + up_bias_all, 0.0)
    activation = jnp.square(gate).astype(jnp.bfloat16)
    gate_low = gate.astype(jnp.bfloat16)
    layer_output = (hidden + dot(activation, down_rows) + down_bias).astype(jnp.bfloat16)

    gate_grad = (2.0 * gate_low.astype(jnp.float32) * dot(cotangent, down_rows, NT)).astype(jnp.bfloat16)
    normed_two_grad = dot(gate_grad, up_rows)
    back_two, gain_rows = norm_backward(hidden, norm2_gain, normed_two_grad)
    hidden_grad = cotangent.astype(jnp.float32) + back_two
    hidden_low = hidden_grad.astype(jnp.bfloat16)
    attended_grad = dot(hidden_low, full[3]).astype(jnp.bfloat16)

    def blocks(columns):
        return columns.reshape(columns.shape[0], nz, -1).transpose(1, 0, 2)

    ff_grad = jnp.stack([
        jnp.stack([
            dot(gate_grad[:, k * hidden_units:(k + 1) * hidden_units], normed_two, TN).astype(jnp.bfloat16)
            if member == 0 else
            dot(activation[:, k * hidden_units:(k + 1) * hidden_units], cotangent, TN).astype(jnp.bfloat16)
            for member in range(2)
        ]) for k in range(nz)
    ])
    early = jnp.concatenate([
        jnp.sum(gain_rows, axis=0), jnp.sum(hidden_low.astype(jnp.float32), axis=0),
        jnp.sum(cotangent.astype(jnp.float32), axis=0), jnp.sum(gate_grad.astype(jnp.float32), axis=0),
    ]).reshape(-1, 1024)
    early = jnp.pad(early, ((0, -early.shape[0] % 8), (0, 0)))
    grad_q, grad_k, grad_v, kernel_sums, ff_sum, early = attention_backward(
        far, linear_q, linear_k, linear_v, kern, attended_grad, attended, mass, ff_grad, early, ny, nx)
    normed_grad = dot(grad_k, full[1], NT) + dot(grad_v, full[2], NT)
    query_part = dot(grad_q, full[0], NT)
    normed_grad = normed_grad + jnp.pad(query_part, ((window_rows - rows - edge, 0), (0, 0)))
    normed_own_grad = normed_grad[window_rows - rows:]
    for hop in range(1, shards):
        at = window_rows - (hop + 1) * rows
        part = normed_grad[at:at + rows].astype(jnp.bfloat16)
        part = jnp.where(before >= hop, part, jnp.zeros_like(part))
        came = lax.ppermute(part, "head", [(i + hop, i) for i in range(nz - hop)])
        normed_own_grad = normed_own_grad + came.astype(jnp.float32)
    back_one, gain_rows_one = norm_backward(own_float, norm1_gain, normed_own_grad)
    layer_grad = (hidden_grad + back_one).astype(jnp.bfloat16)
    qkvo_grad = jnp.stack([
        blocks(dot(late, grad_q, TN).astype(jnp.bfloat16)),
        blocks(dot(window, grad_k, TN).astype(jnp.bfloat16)),
        blocks(dot(window, grad_v, TN).astype(jnp.bfloat16)),
        blocks(dot(hidden_low, attended, TN).astype(jnp.bfloat16)),
    ], axis=1)
    tail = jnp.concatenate([kernel_sums[:9], jnp.sum(gain_rows_one, axis=0)[None]], axis=0)
    tail = jnp.pad(tail, ((0, 6), (0, 0)))
    qkvo_sum, tail = reduce(qkvo_grad, tail, ny, nx, 3)

    width_all = norm1_gain.shape[0]
    early = early.reshape(-1)
    up_bias_grad = lax.dynamic_slice_in_dim(early[3 * width_all:], place * hidden_units, hidden_units, 0)
    kernels_grad = lax.dynamic_slice_in_dim(tail[:9].reshape(3, 3, -1), place * width, width, 2)
    f32 = jnp.float32
    return (
        layer_output[None], layer_grad[None], tail[9], qkvo_sum[:3].astype(f32), kernels_grad,
        qkvo_sum[3].T.astype(f32), early[width_all:2 * width_all], early[:width_all], ff_sum[0].T.astype(f32),
        up_bias_grad, ff_sum[1].astype(f32), early[2 * width_all:3 * width_all],
    )


def solution(mesh):
    rows = P(("batch", "dp"), "head", None)
    return jax.shard_map(
        on_device,
        mesh=mesh,
        in_specs=(
            rows, P(("batch", "dp"), None), P(), P(None, None, "head"), P(None, None, "head"), P("head", None), P(),
            P(), P(None, "head"), P("head"), P("head", None), P(), rows,
        ),
        out_specs=(
            rows, rows, P(), P(None, None, "head"), P(None, None, "head"), P("head", None),
            P(), P(), P(None, "head"), P("head"), P("head", None), P(),
        ),
        check_vma=False,
    )
```

time: 1480 us -> 675 us (0.46)
  waiting for transfers between devices: 925 us -> 12.8 us
  Pallas kernels: 70.7 us -> 375 us
  blocking collectives: 110 us -> 0 us
  other arithmetic: 89.8 us -> 51.2 us
  local copies, waits for them, and re-layouts: 74.9 us -> 37 us
    reduce_scatter x4 -> x0, waiting for transfers between devices: 598 us -> none  [reduced(): lax.psum_scatter(grad.astype(jnp.bfloat16), ALL, scatter_dimension=axis,...]
    pallas_call x2 -> x4, Pallas kernels: 70.7 us -> 375 us  [the longest x1 137 us: attention_backward(): pl.pallas_call(functools.partial(backward_kernel, nz, ny, nx, pairs, bq,...]
    all_gather x7 -> x0, waiting for transfers between devices: 158 us -> none  [the longest x4 107 us: gathered(): return lax.all_gather(piece, ALL, axis=weight.ndim - 2, tiled=True)]
    all_gather x3 -> x0, blocking collectives: 110 us -> none  [the longest x1 80.5 us: on_device(): up_bias_all = lax.all_gather(up_bias, 'head', axis=0, tiled=True)]
    psum x1 -> x0, waiting for transfers between devices: 110 us -> none  [on_device(): lax.psum((gain_one_grad, gain_two_grad, out_bias_grad, down_bias_grad, up...]
    ppermute x2, waiting for transfers between devices: 59.2 us -> 12.8 us  [the longest x1 12.8 us: on_device(): came = lax.ppermute(part, 'head', [(i + hop, i) for i in range(nz - hop)])]
    slice x11 -> x4, local copies, waits for them, and re-layouts: 48.1 us -> 2.84 us  [the longest x1 1.48 us: on_device(): early[2 * width_all:3 * width_all]]
    reduce_sum x5 -> x2, other arithmetic: 42.4 us -> 5.04 us  [the longest x1 3.19 us: on_device(): jnp.sum(gain_rows_one, axis=0)[None]]
  transfers between devices with their start and end apart: 14 -> 2, of which waited for: 11 -> 1; matrix products, arithmetic and copies ran while one was open for 13% -> 6% of each run, Pallas kernels for 2% -> 12%
where the time goes in v3:
time: 675 us; the launch traced here: 666 us
  Pallas kernels  375 us (56%)
  matrix products  180 us (27%)
  other arithmetic  51.2 us (8%)
  local copies, waits for them, and re-layouts  37 us (5%)
  waiting for transfers between devices  12.8 us (2%)
  starting transfers between devices  7.82 us (1%)
    dot_general x24, matrix products, dot(): return lax.dot_general(a, b, dims, preferred_element_type=jnp.float32)  180 us
    pallas_call x1, Pallas kernels, attention_backward(): pl.pallas_call(functools.partial(backward_kernel, nz, ny, nx, pairs, bq,...  137 us
    pallas_call x1, Pallas kernels, attention_forward(): pl.pallas_call(functools.partial(forward_kernel, nz, ny, nx, pairs, bq, 5...  93.9 us
    pallas_call x1, Pallas kernels, gather_open(): pl.pallas_call(functools.partial(open_kernel, nz, ny, nx), out_shape=(jax...  79.4 us
    pallas_call x1, Pallas kernels, reduce(): pl.pallas_call(functools.partial(reduce_kernel, nz, ny, nx), out_shape=(j...  65.4 us
    unnamed x88, local copies, waits for them, and re-layouts  15.9 us
    reshape x4, local copies, waits for them, and re-layouts, blocks(): return columns.reshape(columns.shape[0], nz, -1).transpose(1, 0, 2)  15.1 us
  transfers between devices with their start and end apart: 2, of which 1 were waited for; matrix products, arithmetic and copies ran while one was open for 6% of the time, Pallas kernels for 12%

profile of v3, /device:TPU:0, one launch (start us, length us, event | category | flops | bytes accessed | tf_op | source)
XLA Modules:
  0.0 665.7 jit_solution(65328494197062958)
XLA Ops:
  6.4 6.3 collective-permute-start
  18.6 79.4 %shard_map.220 = (bf16[4,1024,1024]{2,1,0:T(8,128)(2,1)}, f32[4,16,256]{2,1,0:T(8,128)S(1)}) custom-call(bf16[4,1024,256]{2,1,0:T(8,128)(2,1)S(1)} %pad_maximum_fusion.4.shard_ref, f32[16,256]{1,0:T(8,128)S(1)} %select_maximum_fusion.1.small_ref), custom_call_target="tpu_custom_call" | custom-call | bytes 16777216 | tf_op jit(solution)/shard_map/pallas_call | solution.py:230
  99.0 6.8 %convolution_convert_fusion.lq_ref = bf16[1040,1024]{1,0:T(8,128)(2,1)} fusion(bf16[4,1024,1024]{2,1,0:T(8,128)(2,1)} %get-tuple-element.26, bf16[1024,1024]{1,0:T(8,128)(2,1)} %fusion.6, bf16[1024,1024]{1,0:T(8,128)(2,1)S(1)} %broadcast_select_fusion), kind=kOutput, calls=%fused_computation.41 | convolution fusion | flops 2186362880 | bytes 8421376 | tf_op jit(solution)/shard_map/dot_general | solution.py:435
  105.8 7.7 %convolution_convert_fusion.1.lv_ref = bf16[2048,1024]{1,0:T(8,128)(2,1)} fusion(bf16[4,1024,1024]{2,1,0:T(8,128)(2,1)S(1)} %bitcast.184, bf16[1024,1024]{1,0:T(8,128)(2,1)} %fusion.6, bf16[1024,1024]{1,0:T(8,128)(2,1)S(1)} %broadcast_select_fusion), kind=kOutput, calls=%fused_computation.42 | convolution fusion | flops 4305453056 | bytes 10485760 | tf_op jit(solution)/shard_map/dot_general | solution.py:435
  113.5 7.7 %convolution_convert_fusion.2.lk_ref = bf16[2048,1024]{1,0:T(8,128)(2,1)} fusion(bf16[4,1024,1024]{2,1,0:T(8,128)(2,1)S(1)} %bitcast.184, bf16[1024,1024]{1,0:T(8,128)(2,1)} %fusion.6, bf16[1024,1024]{1,0:T(8,128)(2,1)S(1)} %broadcast_select_fusion), kind=kOutput, calls=%fused_computation.43 | convolution fusion | flops 4305453056 | bytes 10485760 | tf_op jit(solution)/shard_map/dot_general | solution.py:435
  121.9 93.9 %shard_map.221 = (bf16[1024,1024]{1,0:T(8,128)(2,1)}, f32[8,8,1024]{2,1,0:T(8,128)}, bf16[4096,1024]{1,0:T(8,128)(2,1)}, bf16[4096,1024]{1,0:T(8,128)(2,1)}) custom-call(f32[8,128]{1,0:T(8,128)} %broadcast_in_dim.25.far_ref, bf16[1040,1024]{1,0:T(8,128)(2,1)} %convolution_convert_fusion.lq_ref, bf16[2048,1024]{1,0:T(8,128)(2,1)} %convolution_convert_fusion.2.lk_ref, ...), custom_call_target="tpu_custom_call" | custom-call | tf_op jit(solution)/shard_map/pallas_call | solution.py:612
  224.3 17.7 %multiply_convert_fusion = (bf16[1024,4096]{1,0:T(8,128)(2,1)}, f32[1024,4096]{1,0:T(8,128)}) fusion(f32[4096]{0:T(1024)S(1)} %bitcast.177, bf16[1024,1024]{1,0:T(8,128)(2,1)} %multiply_convert_fusion.1, bf16[4096,1024]{1,0:T(8,128)(2,1)} %get-tuple-element.29), kind=kOutput, calls=%fused_computation.4 | convolution fusion | flops 8606711808 | bytes 35667968 | tf_op jit(solution)/shard_map/dot_general | solution.py:435
  242.0 16.9 %convert_reduce_fusion = (f32[4096]{0:T(1024)S(1)}, bf16[1024,4096]{1,0:T(8,128)(2,1)}) fusion(bf16[4096,1024]{1,0:T(8,128)(2,1)} %get-tuple-element.30, bf16[1,1024,1024]{2,1,0:T(8,128)(2,1)S(1)} %copy-done.8, f32[1024,4096]{1,0:T(8,128)} %get-tuple-element.80, f32[4096]{0:T(1024)S(1)} %bitcast.178), kind=kOutput, calls=%fused_computation.3 | convolution fusion | flops 8627679232 | bytes 35684352 | tf_op jit(solution)/shard_map/dot_general | solution.py:435
  258.9 14.2 %multiply_reduce_fusion = (f32[1024]{0:T(1024)S(1)}, f32[1024]{0:T(1024)S(1)}, f32[1024,1024]{1,0:T(8,128)S(1)}) fusion(f32[1024,1024]{1,0:T(8,128)S(1)} %copy-done.3, f32[1024]{0:T(1024)S(1)} %add_rsqrt_fusion, f32[1024]{0:T(1024)S(1)} %copy-done.24, bf16[1024,4096]{1,0:T(8,128)(2,1)} %get-tuple-element.82, bf16[4096,1024]{1,0:T(8,128)(2,1)} %get-tuple-element.29), kind=kOutput, calls=%fused_computation.36 | convolution fusion | flops 8596224000 | bytes 25182208 | tf_op jit(solution)/shard_map/dot_general | solution.py:435
  278.8 5.4 fusion.51.g_ref
  322.1 6.9 %pad_maximum_fusion.grad_ref = bf16[4,2,1024,1024]{3,2,1,0:T(8,128)(2,1)} fusion(bf16[1,2,1024,1024]{3,2,1,0:T(8,128)(2,1)S(1)} %get-tuple-element.86, bf16[1,2,1024,1024]{3,2,1,0:T(8,128)(2,1)S(1)} %get-tuple-element.85, bf16[1,2,1024,1024]{3,2,1,0:T(8,128)(2,1)S(1)} %get-tuple-element.84, bf16[1,2,1024,1024]{3,2,1,0:T(8,128)(2,1)S(1)} %get-tuple-element.83), kind=kLoop, calls=%fused_computation | loop fusion | flops 25165824 | bytes 33554432 | tf_op jit(solution)/shard_map/stack | solution.py:823
  329.0 136.6 %shard_map.222 = (bf16[1040,1024]{1,0:T(8,128)(2,1)}, bf16[2048,1024]{1,0:T(8,128)(2,1)}, bf16[2048,1024]{1,0:T(8,128)(2,1)}, f32[16,1024]{1,0:T(8,128)}, bf16[2...) custom-call(f32[8,128]{1,0:T(8,128)} %broadcast_in_dim.25.far_ref, bf16[1040,1024]{1,0:T(8,128)(2,1)} %convolution_convert_fusion.lq_ref, ...), custom_call_target="tpu_custom_call" | custom-call | tf_op jit(solution)/shard_map/pallas_call | solution.py:731
  467.8 6.6 convolution_convert_fusion.6
  474.4 6.2 fusion.48
  480.6 7.3 %convolution_convert_fusion.5 = bf16[1024,1024]{0,1:T(8,128)(2,1)} fusion(bf16[2048,1024]{1,0:T(8,128)(2,1)S(1)} %copy-done.27, bf16[1024,1024]{1,0:T(8,128)(2,1)} %fusion.6, bf16[1024,1024]{1,0:T(8,128)(2,1)S(1)} %copy-done.12), kind=kOutput, calls=%fused_computation.95 | convolution fusion | flops 4304404480 | bytes 10485760 | tf_op jit(solution)/shard_map/dot_general | solution.py:435
  488.0 8.3 %fusion.45 = f32[2048,1024]{1,0:T(8,128)} fusion(bf16[2048,1024]{1,0:T(8,128)(2,1)S(1)} %copy-done.27, bf16[4,1024,1024]{2,1,0:T(8,128)(2,1)} %get-tuple-element.26), kind=kOutput, calls=%fused_computation.77 | convolution fusion | flops 4294967296 | bytes 14680064 | tf_op jit(solution)/shard_map/dot_general | solution.py:435
  503.5 9.3 %convolution_convert_fusion.4 = bf16[1024,1024]{0,1:T(8,128)(2,1)} fusion(bf16[2048,1024]{1,0:T(8,128)(2,1)} %get-tuple-element.33, bf16[1024,1024]{1,0:T(8,128)(2,1)} %fusion.6, bf16[1024,1024]{1,0:T(8,128)(2,1)} %copy-done.11), kind=kOutput, calls=%fused_computation.94 | convolution fusion | flops 4304404480 | bytes 10485760 | tf_op jit(solution)/shard_map/dot_general | solution.py:435
  520.8 11.5 %pad_add_fusion = f32[2048,1024]{1,0:T(8,128)S(1)} fusion(f32[1040,1024]{1,0:T(8,128)} %fusion.48, f32[2048,1024]{1,0:T(8,128)} %fusion.45, bf16[2048,1024]{1,0:T(8,128)(2,1)} %get-tuple-element.33, bf16[4,1024,1024]{2,1,0:T(8,128)(2,1)} %get-tuple-element.26), kind=kOutput, calls=%fused_computation.8 | convolution fusion | flops 4299161600 | bytes 27328512 | tf_op jit(solution)/shard_map/dot_general | solution.py:435
  542.0 5.5 copy.38
  548.1 7.7 %pad_maximum_fusion.1.grad_ref = bf16[4,4,1024,256]{3,2,1,0:T(8,128)(2,1)} fusion(bf16[4,1,1024,256]{3,2,1,0:T(8,128)(2,1)S(1)} %bitcast.163, bf16[4,1,1024,256]{3,2,1,0:T(8,128)(2,1)} %bitcast.166, bf16[4,1,1024,256]{3,2,1,0:T(8,128)(2,1)} %bitcast.164, bf16[4,1,1024,256]{3,2,1,0:T(8,128)(2,1)} %bitcast.165), kind=kLoop, calls=%fused_computation.7 | loop fusion | flops 12582912 | bytes 16777216 | tf_op jit(solution)/shard_map/stack | solution.py:850
  555.9 14.8 %fusion.15 = bf16[1,1024,1024]{2,1,0:T(8,128)(2,1)} fusion(f32[1024,1024]{1,0:T(8,128)S(1)} %copy-done.4, f32[1024]{0:T(1024)S(1)} %copy-done.30, bf16[1024,4096]{1,0:T(8,128)(2,1)} %get-tuple-element.79, bf16[4096,1024]{1,0:T(8,128)(2,1)} %get-tuple-element.30), kind=kOutput, calls=%fused_computation.45 | convolution fusion | flops 8593080320 | bytes 23072768 | tf_op jit(solution)/shard_map/dot_general | solution.py:435
  570.7 12.8 %collective-permute-done.1 = bf16[1024,1024]{1,0:T(8,128)(2,1)} collective-permute-done((bf16[1024,1024]{1,0:T(8,128)(2,1)}, bf16[1024,1024]{1,0:T(8,128)(2,1)}, u32[]{:S(2)}, u32[]{:S(2)}) %collective-permute-start.1) | collective-permute-done | bytes 2097184 | tf_op jit(solution)/shard_map/ppermute | solution.py:846
  587.3 65.4 %shard_map.223 = (bf16[4,1024,256]{2,1,0:T(8,128)(2,1)}, f32[16,1024]{1,0:T(8,128)}) custom-call(bf16[4,4,1024,256]{3,2,1,0:T(8,128)(2,1)} %pad_maximum_fusion.1.grad_ref, f32[16,1024]{1,0:T(8,128)} %select_maximum_fusion.small_ref), custom_call_target="tpu_custom_call" | custom-call | bytes 8388608 | tf_op jit(solution)/shard_map/pallas_call | solution.py:412
  659.7 5.8 fusion.17
  (145 shorter events, 102.9 us)
Async XLA Ops:
  0.6 12.0 %copy-start.31 = (s32[1,3]{1,0:T(1,128)S(1)}, s32[1,3]{1,0:T(1,128)}, u32[]{:S(2)}) copy-start(s32[1,3]{1,0:T(1,128)} %param.14) | copy-start | bytes 40
  0.7 13.5 %copy-start.26 = (f32[1024]{0:T(1024)S(1)}, f32[1024]{0:T(1024)}, u32[]{:S(2)}) copy-start(f32[1024]{0:T(1024)} %param.22) | copy-start | bytes 12292
  0.7 13.5 %copy-start.25 = (f32[3,3,256]{2,1,0:T(4,128)S(1)}, f32[3,3,256]{2,1,0:T(4,128)}, u32[]{:S(2)}) copy-start(f32[3,3,256]{2,1,0:T(4,128)} %param.17) | copy-start | bytes 27652
  0.7 13.5 %copy-start.18 = (bf16[256,1024]{1,0:T(8,128)(2,1)S(1)}, bf16[256,1024]{1,0:T(8,128)(2,1)}, u32[]{:S(2)}) copy-start(bf16[256,1024]{1,0:T(8,128)(2,1)} %param.18) | copy-start | bytes 1572868
  0.7 13.8 %copy-start.10 = (bf16[1024,1024]{1,0:T(8,128)(2,1)S(1)}, bf16[1024,1024]{1,0:T(8,128)(2,1)}, u32[]{:S(2)}) copy-start(bf16[1024,1024]{1,0:T(8,128)(2,1)} %param.21) | copy-start | bytes 6291460
  2.9 11.3 %copy-start.21 = (f32[1024]{0:T(1024)}, f32[1024]{0:T(1024)S(1)}, u32[]{:S(2)}) copy-start(f32[1024]{0:T(1024)S(1)} %add_rsqrt_fusion.1) | copy-start | bytes 12292
  6.4 92.4 %collective-permute-start = (bf16[1024,1024]{1,0:T(8,128)(2,1)}, bf16[1024,1024]{1,0:T(8,128)(2,1)}, u32[]{:S(2)}, u32[]{:S(2)}) collective-permute-start(bf16[1024,1024]{1,0:T(8,128)(2,1)} %fusion.6), channel_id=1, source_target_pairs={{0,8},{8,16},{16,24},{1,9},{9,17},{17,25},{2,10},{10,18},{18,26},{... | collective-permute-start | bytes 6291464 | tf_op jit(solution)/shard_map/ppermute | solution.py:786
  99.0 14.5 %copy-start.11 = (bf16[1024,1024]{1,0:T(8,128)(2,1)}, bf16[1024,1024]{1,0:T(8,128)(2,1)S(1)}, u32[]{:S(2)}) copy-start(bf16[1024,1024]{1,0:T(8,128)(2,1)S(1)} %broadcast_select_fusion) | copy-start | bytes 6291460
  121.9 93.9 %copy-start = (bf16[1,1024,1024]{2,1,0:T(8,128)(2,1)S(1)}, bf16[1,1024,1024]{2,1,0:T(8,128)(2,1)}, u32[]{:S(2)}) copy-start(bf16[1,1024,1024]{2,1,0:T(8,128)(2,1)} %param.13) | copy-start | bytes 6291460
  121.9 93.9 %copy-start.29 = (f32[1024]{0:T(1024)S(1)}, f32[1024]{0:T(1024)}, u32[]{:S(2)}) copy-start(f32[1024]{0:T(1024)} %param.19) | copy-start | bytes 12292
  224.3 17.7 %copy-start.8 = (bf16[1,1024,1024]{2,1,0:T(8,128)(2,1)S(1)}, bf16[1,1024,1024]{2,1,0:T(8,128)(2,1)}, u32[]{:S(2)}) copy-start(bf16[1,1024,1024]{2,1,0:T(8,128)(2,1)} %param.25) | copy-start | bytes 6291460
  242.0 16.9 %copy-start.3 = (f32[1024,1024]{1,0:T(8,128)S(1)}, f32[1024,1024]{1,0:T(8,128)}, u32[]{:S(2)}) copy-start(f32[1024,1024]{1,0:T(8,128)} %copy-done.2) | copy-start | bytes 12582916
  275.0 9.2 %slice-start.6 = ((s8[8388608]{0:T(1024)(128)(4,1)}), s8[4194304]{0:T(1024)(128)(4,1)S(1)}, s32[]{:S(2)}) async-start(s8[8388608]{0:T(1024)(128)(4,1)} %bitcast.188), calls=%async_computation.6 | async-start | bytes 8388608
  291.6 8.0 %slice-start.4 = ((s8[8388608]{0:T(1024)(128)(4,1)}), s8[4194304]{0:T(1024)(128)(4,1)S(1)}, s32[]{:S(2)}) async-start(s8[8388608]{0:T(1024)(128)(4,1)} %bitcast.186), calls=%async_computation.4 | async-start | bytes 8388608
  329.0 138.8 %copy-start.12 = (bf16[1024,1024]{1,0:T(8,128)(2,1)S(1)}, bf16[1024,1024]{1,0:T(8,128)(2,1)}, u32[]{:S(2)}) copy-start(bf16[1024,1024]{1,0:T(8,128)(2,1)} %copy-done.11) | copy-start | bytes 6291460
  532.3 9.7 %copy-start.6 = (f32[2048,1024]{1,0:T(8,128)}, f32[2048,1024]{1,0:T(8,128)S(1)}, u32[]{:S(2)}) copy-start(f32[2048,1024]{1,0:T(8,128)S(1)} %pad_add_fusion) | copy-start | bytes 25165828
  533.9 49.6 %collective-permute-start.1 = (bf16[1024,1024]{1,0:T(8,128)(2,1)}, bf16[1024,1024]{1,0:T(8,128)(2,1)}, u32[]{:S(2)}, u32[]{:S(2)}) collective-permute-start(bf16[1024,1024]{1,0:T(8,128)(2,1)} %fusion.16), channel_id=1, source_target_pairs={{8,0},{16,8},{24,16},{9,1},{17,9},{25,17},{10,2},{18,10},{26,18},{... | collective-permute-start | bytes 6291464 | tf_op jit(solution)/shard_map/ppermute | solution.py:846
  548.1 7.7 %copy-start.30 = (f32[1024]{0:T(1024)S(1)}, f32[1024]{0:T(1024)}, u32[]{:S(2)}) copy-start(f32[1024]{0:T(1024)} %param.24) | copy-start | bytes 12292
  548.1 35.3 %slice-start = ((s8[8388608]{0:T(1024)(128)(4,1)}), s8[4194304]{0:T(1024)(128)(4,1)S(1)}, s32[]{:S(2)}) async-start(s8[8388608]{0:T(1024)(128)(4,1)} %bitcast.160), calls=%async_computation | async-start | bytes 8388608
  555.8 27.6 %copy-start.1 = (bf16[1,1024,1024]{2,1,0:T(8,128)(2,1)S(1)}, bf16[1,1024,1024]{2,1,0:T(8,128)(2,1)}, u32[]{:S(2)}) copy-start(bf16[1,1024,1024]{2,1,0:T(8,128)(2,1)} %param.13) | copy-start | bytes 6291460
  555.8 27.6 %slice-start.1 = ((s8[8388608]{0:T(1024)(128)(4,1)}), s8[4194304]{0:T(1024)(128)(4,1)S(1)}, s32[]{:S(2)}) async-start(s8[8388608]{0:T(1024)(128)(4,1)} %bitcast.160), calls=%async_computation.1 | async-start | bytes 8388608
  555.8 27.6 %copy-start.22 = (f32[1024]{0:T(1024)S(1)}, f32[1024]{0:T(1024)}, u32[]{:S(2)}) copy-start(f32[1024]{0:T(1024)} %copy-done.21) | copy-start | bytes 12292
  555.9 27.6 %copy-start.23 = (f32[1024]{0:T(1024)S(1)}, f32[1024]{0:T(1024)}, u32[]{:S(2)}) copy-start(f32[1024]{0:T(1024)} %param.15) | copy-start | bytes 12292
  570.7 16.0 %copy-start.20 = (f32[16,1024]{1,0:T(8,128)S(1)}, f32[16,1024]{1,0:T(8,128)}, u32[]{:S(2)}) copy-start(f32[16,1024]{1,0:T(8,128)} %get-tuple-element.35) | copy-start | bytes 196612
  (18 other events, 93.6 us)

commit v4 on v3

--- a/solution.py
+++ b/solution.py
@@ -266,6 +266,12 @@
     def count(nz, ny, nx):
         return nz * (ny + 2 * (ny - 1) + 2 * (nx - 1)) + nz - 1 + spread_count(ny, nx)
 
+    def source(self, t, dy):
+        return self.grad.at[(self.place.z + 1 + t) % self.place.nz, :, self.place.band(self.rows, dy, 1), :]
+
+    def own(self, t, dy, m):
+        return self.grad[(self.place.z + 1 + t) % self.place.nz, m, self.place.band(self.rows, dy), :]
+
     def chunk(self, t):
         place, copies, half, rows = self.place, self.copies, self.half, self.rows
         ny, nx, nz = place.ny, place.nx, place.nz
@@ -276,7 +282,7 @@
 
         sent = [
             copies.plan(
-                lambda dy=dy: self.grad.at[(place.z + 1 + t) % nz, :, place.band(rows, dy, 1), :],
+                lambda dy=dy: self.source(t, dy),
                 lambda dy=dy: core.at[t, dy], place.other_core)
             for dy in range(ny)
         ]
@@ -303,8 +309,7 @@
             arrive(sent)
             for dy in range(ny):
                 for m in range(self.members):
-                    own = self.grad[(place.z + 1 + t) % nz, m, place.band(rows, dy), :]
-                    core[t, dy, m] = (core[t, dy, m].astype(f32) + own.astype(f32)).astype(bf)
+                    core[t, dy, m] = (core[t, dy, m].astype(f32) + self.own(t, dy, m).astype(f32)).astype(bf)
             start(over_y)
             start(over_x)
 
@@ -376,7 +381,8 @@
         return total
 
     def first():
-        s_acc[0] = small_ref[...]
+        if small_ref is not None:
+            s_acc[0] = small_ref[...]
         start(sent[0])
 
     def middle(k):
@@ -424,7 +430,8 @@
 
 HS = 64
 LANES = 128
-EDGE = 16
+EDGE = 128
+TAP = 16
 LOG2E = math.log2(math.e)
 NT = (((1,), (1,)), ((), ()))
 NN = (((1,), (0,)), ((), ()))
@@ -441,10 +448,10 @@
 
 def earlier(ref, start, size):
     if start == 0:
-        rows = jnp.concatenate([jnp.zeros((EDGE, LANES), jnp.float32), ref[pl.ds(0, size), :].astype(jnp.float32)], axis=0)
+        rows = jnp.concatenate([jnp.zeros((TAP, LANES), jnp.float32), ref[pl.ds(0, size), :].astype(jnp.float32)], axis=0)
     else:
-        rows = ref[pl.ds(start - EDGE, size + EDGE), :].astype(jnp.float32)
-    return [pltpu.roll(rows, i, 0)[EDGE:] if i else rows[EDGE:] for i in range(3)]
+        rows = ref[pl.ds(start - TAP, size + TAP), :].astype(jnp.float32)
+    return [pltpu.roll(rows, i, 0)[TAP:] if i else rows[TAP:] for i in range(3)]
 
 
 def convolve(linear_ref, kern_ref, member, target_ref, skip, step=256):
@@ -749,6 +756,213 @@
     )(far, late, linear_k, linear_v, kern, grads, outs, mass, ff_grad, small)
 
 
+class TailReduction(Reduction):
+    def __init__(self, place, copies, lefts, rights, send_ref, out_ref, buffers, shape):
+        self.place, self.copies, self.out = place, copies, out_ref
+        self.core, self.y1, self.x1, self.x2, self.y2, self.z_send, self.z_buf = buffers
+        self.lefts, self.rights, self.send = lefts, rights, send_ref
+        self.members, self.height, self.width = shape
+        self.half = self.members // 2
+        self.rows = self.height // (place.ny * 2 * place.nx)
+        self.sums = []
+
+    def product(self, t, dy, m, core):
+        block = (self.place.z + 1 + t) % self.place.nz
+        columns = pl.ds(pl.multiple_of(block * self.width, self.width), self.width)
+        left, first = self.lefts[m]
+        return dot(left[self.place.band(self.rows, dy, core), first:], self.rights[m][:, columns])
+
+    def source(self, t, dy):
+        return self.send.at[t, dy]
+
+    def own(self, t, dy, m):
+        return self.product(t, dy, m, 0)
+
+    def fill(self, t):
+        for dy in range(self.place.ny):
+            for m in range(self.members):
+                self.send[t, dy, m] = self.product(t, dy, m, 1).astype(jnp.bfloat16)
+
+
+def tail_kernel(
+    nz, ny, nx, rows, shards, far_ref, gain_ref, sums_ref, gq_in, gk_in, gv_in, window_in, turned_in, low_turned_in,
+    attended_in, weight_in, low_in, input_in, out_ref, small_out_ref, grad_out_ref, *scratch,
+):
+    (gq, gk, gv, window, turned, low_turned, attended, weight, low, own_input, partial, far_send, far_came, send,
+     *buffers, s_acc, s_buf, load_sems, send_sems, recv_sems) = scratch
+    place = Place(nz, ny, nx)
+    copies = Copies(send_sems, recv_sems)
+    edge = gq.shape[0] - rows
+    window_rows = window.shape[0]
+    f32, bf = jnp.float32, jnp.bfloat16
+    loads = {}
+    for n, (source, target) in enumerate((
+        (gk_in, gk), (weight_in.at[1:3], weight.at[1:3]), (gv_in, gv), (window_in, window), (gq_in, gq),
+        (weight_in.at[0:1], weight.at[0:1]), (turned_in, turned), (low_turned_in, low_turned), (attended_in, attended),
+        (low_in, low), (input_in, own_input),
+    )):
+        loads[n] = pltpu.make_async_copy(source, target, load_sems.at[n])
+        loads[n].start()
+
+    step = min(256, rows)
+    whole = TailReduction(
+        place, copies, [(turned, window_rows - rows - edge), (turned, 0), (turned, 0), (low_turned, 0)],
+        [gq, gk, gv, attended], send, out_ref, buffers, out_ref.shape)
+    chunks = [whole.chunk(t) for t in range(nz)]
+    ending = whole.ending()
+    small = small_sum(place, copies, None, small_out_ref, s_acc, s_buf)
+    backs = {
+        (hop, at): copies.plan(
+            lambda hop=hop, at=at: far_send.at[hop - 1, at:at + step, :], lambda hop=hop, at=at: far_came.at[hop - 1, at:at + step, :],
+            place.along_z(-hop))
+        for hop in range(1, shards) for at in range(0, rows, step)
+    }
+    place.meet()
+
+    gains = [jnp.zeros((8, window.shape[1]), f32)]
+
+    def normed_rows(at):
+        part = dot(gk[at:at + step, :], weight[1], NT) + dot(gv[at:at + step, :], weight[2], NT)
+        first = at - (window_rows - rows - edge)
+        if first >= 0:
+            part = part + dot(gq[first:first + step, :], weight[0], NT)
+        elif first + step > 0:
+            query = dot(gq[0:first + step, :], weight[0], NT)
+            part = part + jnp.concatenate([jnp.zeros((-first, part.shape[1]), f32), query], axis=0)
+        product = part * window[at:at + step, :].astype(f32)
+        gains[0] = gains[0] + jnp.sum(product.reshape(step // 8, 8, -1), axis=0)
+        return part
+
+    for n in range(6):
+        loads[n].wait()
+    for hop in range(shards - 1, 0, -1):
+        keep = jnp.where(far_ref[hop - 1:hop, 0:1] > 0, 0.0, 1.0)
+        for at in range(0, rows, step):
+            part = normed_rows(window_rows - (hop + 1) * rows + at) * keep
+            far_send[hop - 1, at:at + step, :] = part.astype(bf)
+            backs[hop, at].start()
+
+    def own_rows(at):
+        partial[at:at + step, :] = normed_rows(window_rows - rows + at).astype(bf)
+
+    def begin(t):
+        whole.fill(t)
+        chunks[t][0]()
+
+    for n in range(6, 9):
+        loads[n].wait()
+    owned = list(range(0, rows, step))
+    for tick in range(nz + 3):
+        for t in range(nz):
+            if 0 <= tick - t < 4:
+                if tick == t:
+                    begin(t)
+                else:
+                    chunks[t][tick - t]()
+        if tick and owned:
+            own_rows(owned.pop(0))
+    while owned:
+        own_rows(owned.pop(0))
+    s_acc[0] = sums_ref[...]
+    s_acc[0, 9:10, :] = jnp.sum(gains[0], axis=0, keepdims=True)
+    small[0]()
+    ending[0]()
+    small[1]()
+    loads[9].wait()
+    loads[10].wait()
+    for copy in backs.values():
+        copy.wait_recv()
+    small[2]()
+    gain = gain_ref[0:1, :]
+    for at in range(0, rows, step):
+        values = own_input[at:at + step, :].astype(f32)
+        upstream = partial[at:at + step, :].astype(f32)
+        for hop in range(1, shards):
+            upstream = upstream + far_came[hop - 1, at:at + step, :].astype(f32)
+        factor = lax.rsqrt(jnp.mean(values * values, axis=-1, keepdims=True) + EPSILON)
+        unit = values * factor
+        scaled = gain * upstream
+        back = factor * (scaled - unit * jnp.mean(scaled * unit, axis=-1, keepdims=True))
+        grad_out_ref[at:at + step, :] = (low[at:at + step, :].astype(f32) + back).astype(bf)
+    small[3]()
+    ending[1]()
+    small[4]()
+    ending[2]()
+    ending[3]()
+    copies.finish()
+
+
+def tail(far, gain, sums, grads, window, turned, low_turned, attended, weight, low, own_input, rows, nz, ny, nx):
+    grad_q, grad_k, grad_v = grads
+    window_rows, depth = window.shape
+    shards = window_rows // rows
+    width = depth // nz
+    members, bf = 4, jnp.bfloat16
+    band = nx * (depth // (ny * 2 * nx))
+    step = min(256, rows)
+    count = Reduction.count(nz, ny, nx) + nx + ny + nz - 2 + (shards - 1) * (rows // step)
+    buffers = [pltpu.VMEM(t.shape, bf) for t in (grad_q, grad_k, grad_v, window, turned, low_turned, attended)]
+    hops = max(1, shards - 1)
+    return pl.pallas_call(
+        functools.partial(tail_kernel, nz, ny, nx, rows, shards),
+        out_shape=(jax.ShapeDtypeStruct((members, depth, width), bf), jax.ShapeDtypeStruct(sums.shape, jnp.float32),
+                   jax.ShapeDtypeStruct((rows, depth), bf)),
+        in_specs=[VMEM, VMEM, VMEM] + [ANY] * 10,
+        out_specs=(VMEM, VMEM, VMEM),
+        scratch_shapes=buffers + [
+            pltpu.VMEM((3, depth, depth), bf), pltpu.VMEM((rows, depth), bf), pltpu.VMEM((rows, depth), bf),
+            pltpu.VMEM((rows, depth), bf), pltpu.VMEM((hops, rows, depth), bf), pltpu.VMEM((hops, rows, depth), bf),
+            pltpu.VMEM((nz, ny, members, band, width), bf),
+        ] + Reduction.scratch(nz, ny, nx, members, depth, width) + small_scratch(nz, ny, nx, sums.shape) + [
+            pltpu.SemaphoreType.DMA((11,)), pltpu.SemaphoreType.DMA((count,)), pltpu.SemaphoreType.DMA((count,)),
+        ],
+        compiler_params=pltpu.CompilerParams(collective_id=3, has_side_effects=True, vmem_limit_bytes=62 << 20),
+        cost_estimate=pl.CostEstimate(flops=24 << 30, bytes_accessed=60 << 20, transcendentals=0),
+    )(far, gain, sums, grad_q, grad_k, grad_v, window, turned, low_turned, attended, weight, low, own_input)
+
+
+def feed_forward_kernel(
+    normed_ref, normed_t_ref, grad_ref, grad_t_ref, up_ref, down_ref, bias_ref, weights_ref, bias_grad_ref, normed_grad_ref, out_ref,
+):
+    @pl.when(pl.program_id(0) == 0)
+    def _():
+        normed_grad_ref[...] = jnp.zeros_like(normed_grad_ref)
+        out_ref[...] = jnp.zeros_like(out_ref)
+
+    bf = jnp.bfloat16
+    gate = jnp.maximum(dot(up_ref[...], normed_t_ref[...]) + bias_ref[...], 0.0)
+    activation = (gate * gate).astype(bf)
+    gate_grad = (2.0 * gate * dot(down_ref[...], grad_t_ref[...])).astype(bf)
+    weights_ref[0, 0] = dot(gate_grad, normed_ref[...]).astype(bf)
+    weights_ref[0, 1] = dot(activation, grad_ref[...]).astype(bf)
+    total = jnp.sum(gate_grad.astype(jnp.float32), axis=1, keepdims=True)
+    bias_grad_ref[...] = jnp.broadcast_to(total, bias_grad_ref.shape)
+    normed_grad_ref[...] += dot(gate_grad, up_ref[...], TN)
+    out_ref[...] += dot(activation, down_ref[...], TN)
+
+
+def feed_forward(normed, grad, up_rows, down_rows, bias, nz):
+    rows, depth = normed.shape
+    units = up_rows.shape[0] // nz
+    step = min(1024, units)
+    per = units // step
+    whole = lambda shape: pl.BlockSpec(shape, lambda i: (0, 0))
+    block = pl.BlockSpec((step, depth), lambda i: (i, 0))
+    f32, bf = jnp.float32, jnp.bfloat16
+    return pl.pallas_call(
+        feed_forward_kernel,
+        out_shape=(jax.ShapeDtypeStruct((nz, 2, units, depth), bf), jax.ShapeDtypeStruct((nz * units, LANES), f32),
+                   jax.ShapeDtypeStruct((rows, depth), f32), jax.ShapeDtypeStruct((rows, depth), f32)),
+        grid=(nz * per,),
+        in_specs=[whole((rows, depth)), whole((depth, rows)), whole((rows, depth)), whole((depth, rows)), block, block,
+                  pl.BlockSpec((step, 1), lambda i: (i, 0))],
+        out_specs=[pl.BlockSpec((1, 2, step, depth), lambda i: (i // per, 0, i % per, 0)),
+                   pl.BlockSpec((step, LANES), lambda i: (i, 0)), whole((rows, depth)), whole((rows, depth))],
+        compiler_params=pltpu.CompilerParams(vmem_limit_bytes=56 << 20),
+        cost_estimate=pl.CostEstimate(flops=12 * rows * depth * nz * units, bytes_accessed=48 << 20, transcendentals=0),
+    )(normed, normed.T, grad, grad.T, up_rows, down_rows, bias[:, None])
+
+
 def factor_of(values):
     return lax.rsqrt(jnp.mean(values * values, axis=-1, keepdims=True) + EPSILON)
 
@@ -805,65 +1019,31 @@
         far, linear_q, linear_k, linear_v, kern, up_weight.T, down_weight, rows, nz, ny, nx)
     hidden = own_float + dot(attended, full[3], NT) + out_bias
     normed_two = (hidden * factor_of(hidden) * norm2_gain).astype(jnp.bfloat16)
-    gate = jnp.maximum(dot(normed_two, up_rows, NT) + up_bias_all, 0.0)
-    activation = jnp.square(gate).astype(jnp.bfloat16)
-    gate_low = gate.astype(jnp.bfloat16)
-    layer_output = (hidden + dot(activation, down_rows) + down_bias).astype(jnp.bfloat16)
-
-    gate_grad = (2.0 * gate_low.astype(jnp.float32) * dot(cotangent, down_rows, NT)).astype(jnp.bfloat16)
-    normed_two_grad = dot(gate_grad, up_rows)
+    ff_grad, up_bias_sums, normed_two_grad, ff_out = feed_forward(normed_two, cotangent, up_rows, down_rows, up_bias_all, nz)
+    layer_output = (hidden + ff_out + down_bias).astype(jnp.bfloat16)
     back_two, gain_rows = norm_backward(hidden, norm2_gain, normed_two_grad)
     hidden_grad = cotangent.astype(jnp.float32) + back_two
     hidden_low = hidden_grad.astype(jnp.bfloat16)
     attended_grad = dot(hidden_low, full[3]).astype(jnp.bfloat16)
 
-    def blocks(columns):
-        return columns.reshape(columns.shape[0], nz, -1).transpose(1, 0, 2)
-
-    ff_grad = jnp.stack([
-        jnp.stack([
-            dot(gate_grad[:, k * hidden_units:(k + 1) * hidden_units], normed_two, TN).astype(jnp.bfloat16)
-            if member == 0 else
-            dot(activation[:, k * hidden_units:(k + 1) * hidden_units], cotangent, TN).astype(jnp.bfloat16)
-            for member in range(2)
-        ]) for k in range(nz)
-    ])
     early = jnp.concatenate([
         jnp.sum(gain_rows, axis=0), jnp.sum(hidden_low.astype(jnp.float32), axis=0),
-        jnp.sum(cotangent.astype(jnp.float32), axis=0), jnp.sum(gate_grad.astype(jnp.float32), axis=0),
+        jnp.sum(cotangent.astype(jnp.float32), axis=0), up_bias_sums[:, 0],
     ]).reshape(-1, 1024)
     early = jnp.pad(early, ((0, -early.shape[0] % 8), (0, 0)))
     grad_q, grad_k, grad_v, kernel_sums, ff_sum, early = attention_backward(
         far, linear_q, linear_k, linear_v, kern, attended_grad, attended, mass, ff_grad, early, ny, nx)
-    normed_grad = dot(grad_k, full[1], NT) + dot(grad_v, full[2], NT)
-    query_part = dot(grad_q, full[0], NT)
-    normed_grad = normed_grad + jnp.pad(query_part, ((window_rows - rows - edge, 0), (0, 0)))
-    normed_own_grad = normed_grad[window_rows - rows:]
-    for hop in range(1, shards):
-        at = window_rows - (hop + 1) * rows
-        part = normed_grad[at:at + rows].astype(jnp.bfloat16)
-        part = jnp.where(before >= hop, part, jnp.zeros_like(part))
-        came = lax.ppermute(part, "head", [(i + hop, i) for i in range(nz - hop)])
-        normed_own_grad = normed_own_grad + came.astype(jnp.float32)
-    back_one, gain_rows_one = norm_backward(own_float, norm1_gain, normed_own_grad)
-    layer_grad = (hidden_grad + back_one).astype(jnp.bfloat16)
-    qkvo_grad = jnp.stack([
-        blocks(dot(late, grad_q, TN).astype(jnp.bfloat16)),
-        blocks(dot(window, grad_k, TN).astype(jnp.bfloat16)),
-        blocks(dot(window, grad_v, TN).astype(jnp.bfloat16)),
-        blocks(dot(hidden_low, attended, TN).astype(jnp.bfloat16)),
-    ], axis=1)
-    tail = jnp.concatenate([kernel_sums[:9], jnp.sum(gain_rows_one, axis=0)[None]], axis=0)
-    tail = jnp.pad(tail, ((0, 6), (0, 0)))
-    qkvo_sum, tail = reduce(qkvo_grad, tail, ny, nx, 3)
+    qkvo_sum, totals, layer_grad = tail(
+        far, norm1_gain[None], kernel_sums, (grad_q, grad_k, grad_v), window, window.T, hidden_low.T, attended, full,
+        hidden_low, layer_input[0], rows, nz, ny, nx)
 
     width_all = norm1_gain.shape[0]
     early = early.reshape(-1)
     up_bias_grad = lax.dynamic_slice_in_dim(early[3 * width_all:], place * hidden_units, hidden_units, 0)
-    kernels_grad = lax.dynamic_slice_in_dim(tail[:9].reshape(3, 3, -1), place * width, width, 2)
+    kernels_grad = lax.dynamic_slice_in_dim(totals[:9].reshape(3, 3, -1), place * width, width, 2)
     f32 = jnp.float32
     return (
-        layer_output[None], layer_grad[None], tail[9], qkvo_sum[:3].astype(f32), kernels_grad,
+        layer_output[None], layer_grad[None], totals[9] / norm1_gain, qkvo_sum[:3].astype(f32), kernels_grad,
         qkvo_sum[3].T.astype(f32), early[width_all:2 * width_all], early[:width_all], ff_sum[0].T.astype(f32),
         up_bias_grad, ff_sum[1].astype(f32), early[2 * width_all:3 * width_all],
     )

time: 675 us -> 592 us (0.88)
  matrix products: 180 us -> 32.3 us
  Pallas kernels: 375 us -> 478 us
  other arithmetic: 51.2 us -> 32 us
  waiting for transfers between devices: 12.8 us -> 0.01 us
    dot_general x24 -> x5, matrix products: 180 us -> 32.3 us  [dot(): return lax.dot_general(a, b, dims, preferred_element_type=jnp.float32)]
    pallas_call x1 -> x2, Pallas kernels: 65.4 us -> 165 us  [the longest x1 103 us: tail(): pl.pallas_call(functools.partial(tail_kernel, nz, ny, nx, rows, shards),...]
    another operation x5 -> x1, other arithmetic: 19.5 us -> 0.18 us  [the longest x3 11.6 us: on_device(): jnp.stack([jnp.stack([dot(gate_grad[:, k * hidden_units:(k + 1) * hidden_...]
    reshape x5 -> x1, local copies, waits for them, and re-layouts: 15.1 us -> 0.02 us  [on_device(): totals[:9].reshape(3, 3, -1)]
    transpose x0 -> x4, local copies, waits for them, and re-layouts: none -> 14.2 us  [the longest x2 9.08 us: on_device(): qkvo_sum, totals, layer_grad = tail(far, norm1_gain[None], kernel_sums, (...]
    ppermute x1 -> x0, waiting for transfers between devices: 12.8 us -> none  [on_device(): came = lax.ppermute(part, 'head', [(i + hop, i) for i in range(nz - hop)])]
    unnamed x88 -> x51, local copies, waits for them, and re-layouts: 15.9 us -> 14.1 us
  transfers between devices with their start and end apart: 2 -> 1, of which waited for: 1 -> 0; matrix products, arithmetic and copies ran while one was open for 6% -> 2% of each run, Pallas kernels for 12% -> 14%
where the time goes in v4:
time: 592 us; the launch traced here: 589 us
  Pallas kernels  478 us (81%)
  local copies, waits for them, and re-layouts  38.5 us (7%)
  matrix products  32.3 us (5%)
  other arithmetic  32 us (5%)
  starting transfers between devices  6.26 us (1%)
    pallas_call x1, Pallas kernels, attention_backward(): pl.pallas_call(functools.partial(backward_kernel, nz, ny, nx, pairs, bq,...  138 us
    pallas_call x1, Pallas kernels, tail(): pl.pallas_call(functools.partial(tail_kernel, nz, ny, nx, rows, shards),...  103 us
    pallas_call x1, Pallas kernels, attention_forward(): pl.pallas_call(functools.partial(forward_kernel, nz, ny, nx, pairs, bq, 5...  91.9 us
    pallas_call x1, Pallas kernels, gather_open(): pl.pallas_call(functools.partial(open_kernel, nz, ny, nx), out_shape=(jax...  83.4 us
    pallas_call x1, Pallas kernels, feed_forward(): pl.pallas_call(feed_forward_kernel, out_shape=(jax.ShapeDtypeStruct((nz,...  62.2 us
    dot_general x5, matrix products, dot(): return lax.dot_general(a, b, dims, preferred_element_type=jnp.float32)  32.3 us
    unnamed x51, local copies, waits for them, and re-layouts  14.1 us
  transfers between devices with their start and end apart: 1, of which 0 were waited for; matrix products, arithmetic and copies ran while one was open for 2% of the time, Pallas kernels for 14%

profile of v4, /device:TPU:0, one launch (start us, length us, event | category | flops | bytes accessed | tf_op | source)
XLA Modules:
  0.0 589.1 jit_solution(2295495360300005832)
XLA Ops:
  2.9 3.5 fusion.3
  6.4 6.3 %collective-permute-start = (bf16[1024,1024]{1,0:T(8,128)(2,1)}, bf16[1024,1024]{1,0:T(8,128)(2,1)}, u32[]{:S(2)}, u32[]{:S(2)}) collective-permute-start(bf16[1024,1024]{1,0:T(8,128)(2,1)} %fusion.3), channel_id=1, source_target_pairs={{0,8},{8,16},{16,24},{1,9},{9,17},{17,25},{2,10},{10,18},{18,26},{... | collective-permute-start | bytes 6291464 | tf_op jit(solution)/shard_map/ppermute | solution.py:1000
  14.6 83.4 %shard_map.220 = (bf16[4,1024,1024]{2,1,0:T(8,128)(2,1)}, f32[4,16,256]{2,1,0:T(8,128)S(1)}) custom-call(bf16[4,1024,256]{2,1,0:T(8,128)(2,1)S(1)} %pad_maximum_fusion.1.shard_ref, f32[16,256]{1,0:T(8,128)S(1)} %select_maximum_fusion.small_ref), custom_call_target="tpu_custom_call" | custom-call | bytes 16777216 | tf_op jit(solution)/shard_map/pallas_call | solution.py:230
  98.8 4.1 copy.36
  102.9 3.3 broadcast_in_dim_reshape.4.bias_ref
  106.1 2.6 copy.38.grad_t_ref
  108.9 8.9 %convolution_convert_fusion.1.lv_ref = bf16[2048,1024]{1,0:T(8,128)(2,1)} fusion(bf16[4,1024,1024]{2,1,0:T(8,128)(2,1)} %get-tuple-element.31.weight_in, bf16[1024,1024]{1,0:T(8,128)(2,1)} %fusion.3, bf16[1024,1024]{1,0:T(8,128)(2,1)S(1)} %broadcast_select_fusion), kind=kOutput, calls=%fused_computation.21 | convolution fusion | flops 4305453056 | bytes 10485760 | tf_op jit(solution)/shard_map/dot_general | solution.py:442
  117.8 7.7 %convolution_convert_fusion.2.lk_ref = bf16[2048,1024]{1,0:T(8,128)(2,1)} fusion(bf16[4,1024,1024]{2,1,0:T(8,128)(2,1)S(1)} %bitcast.87, bf16[1024,1024]{1,0:T(8,128)(2,1)} %fusion.3, bf16[1024,1024]{1,0:T(8,128)(2,1)S(1)} %broadcast_select_fusion), kind=kOutput, calls=%fused_computation.22 | convolution fusion | flops 4305453056 | bytes 10485760 | tf_op jit(solution)/shard_map/dot_general | solution.py:442
  125.5 5.6 convolution_convert_fusion.lq_ref
  131.8 91.9 %shard_map.221 = (bf16[1024,1024]{1,0:T(8,128)(2,1)}, f32[8,8,1024]{2,1,0:T(8,128)}, bf16[4096,1024]{1,0:T(8,128)(2,1)}, bf16[4096,1024]{1,0:T(8,128)(2,1)}) custom-call(f32[8,128]{1,0:T(8,128)} %broadcast_in_dim.45.far_ref, bf16[1152,1024]{1,0:T(8,128)(2,1)} %convolution_convert_fusion.lq_ref, bf16[2048,1024]{1,0:T(8,128)(2,1)} %convolution_convert_fusion.2.lk_ref, ...), custom_call_target="tpu_custom_call" | custom-call | tf_op jit(solution)/shard_map/pallas_call | solution.py:619
  223.7 4.8 multiply_reduce_fusion.2
  232.3 4.8 fusion.27
  239.6 62.2 %shard_map.222 = (bf16[4,2,1024,1024]{3,2,1,0:T(8,128)(2,1)}, f32[4096,128]{1,0:T(8,128)}, f32[1024,1024]{1,0:T(8,128)}, f32[1024,1024]{1,0:T(8,128)}) custom-call(bf16[1024,1024]{1,0:T(8,128)(2,1)} %multiply_convert_fusion.normed_ref, bf16[1024,1024]{1,0:T(8,128)(2,1)} %copy.37.normed_t_ref, bf16[1024,1024]{1,0:T(8,128)(2,1)} %bitcast.71, ...), custom_call_target="tpu_custom_call" | custom-call | flops 51539607552 | bytes 50331648 | tf_op jit(solution)/shard_map/pallas_call | solution.py:952
  301.9 3.4 multiply_reduce_fusion
  305.3 3.0 slice_reduce_fusion
  308.4 3.0 convert_reduce_fusion.1
  312.1 5.3 fusion.18.g_ref
  317.4 2.6 copy.41.low_turned_in
  320.0 6.5 %copy.40.turned_in = bf16[1024,2048]{1,0:T(8,128)(2,1)} copy(bf16[1024,2048]{0,1:T(8,128)(2,1)} %get-tuple-element.80) | data formatting | bytes 8388608 | tf_op jit(solution)/shard_map/transpose | solution.py:1037
  326.5 137.8 %shard_map.223 = (bf16[1152,1024]{1,0:T(8,128)(2,1)}, bf16[2048,1024]{1,0:T(8,128)(2,1)}, bf16[2048,1024]{1,0:T(8,128)(2,1)}, f32[16,1024]{1,0:T(8,128)}, bf16[2...) custom-call(f32[8,128]{1,0:T(8,128)} %broadcast_in_dim.45.far_ref, bf16[1152,1024]{1,0:T(8,128)(2,1)} %convolution_convert_fusion.lq_ref, ...), custom_call_target="tpu_custom_call" | custom-call | tf_op jit(solution)/shard_map/pallas_call | solution.py:738
  464.3 102.8 %shard_map.224 = (bf16[4,1024,256]{2,1,0:T(8,128)(2,1)}, f32[16,1024]{1,0:T(8,128)}, bf16[1024,1024]{1,0:T(8,128)(2,1)}) custom-call(f32[8,128]{1,0:T(8,128)} %broadcast_in_dim.45.far_ref, f32[1,1024]{1,0:T(1,128)} %bitcast.82, f32[16,1024]{1,0:T(8,128)} %get-tuple-element.41.sums_ref, bf16[1152,1024]{1,0:T(8,128)(2,1)} %get-tuple-element.42.gq_in, ...), custom_call_target="tpu_custom_call" | custom-call | flops 25769803776 | bytes 62914560 | tf_op jit(solution)/shard_map/pallas_call | solution.py:906
  567.1 3.4 slice_convert_fusion
  574.2 6.6 %bitcast_convert_fusion = (f32[1024,1024]{1,0:T(8,128)}, f32[1024,1024]{0,1:T(8,128)}) fusion(bf16[2,1024,1024]{2,1,0:T(8,128)(2,1)} %get-tuple-element.49), kind=kLoop, calls=%fused_computation.26 | loop fusion | flops 2097152 | bytes 12582912 | tf_op jit(solution)/shard_map/convert_element_type | solution.py:1048
  580.8 5.5 copy.43
  (83 shorter events, 18.2 us)
Async XLA Ops:
  0.6 12.0 %copy-start.19 = (s32[1,3]{1,0:T(1,128)S(1)}, s32[1,3]{1,0:T(1,128)}, u32[]{:S(2)}) copy-start(s32[1,3]{1,0:T(1,128)} %param.14) | copy-start | bytes 40
  0.7 13.5 %copy-start.10 = (bf16[256,1024]{1,0:T(8,128)(2,1)S(1)}, bf16[256,1024]{1,0:T(8,128)(2,1)}, u32[]{:S(2)}) copy-start(bf16[256,1024]{1,0:T(8,128)(2,1)} %param.18) | copy-start | bytes 1572868
  0.7 13.7 %copy-start.15 = (f32[3,3,256]{2,1,0:T(4,128)S(1)}, f32[3,3,256]{2,1,0:T(4,128)}, u32[]{:S(2)}) copy-start(f32[3,3,256]{2,1,0:T(4,128)} %param.17) | copy-start | bytes 27652
  0.7 13.7 %copy-start.17 = (f32[1024]{0:T(1024)S(1)}, f32[1024]{0:T(1024)}, u32[]{:S(2)}) copy-start(f32[1024]{0:T(1024)} %param.22) | copy-start | bytes 12292
  0.7 13.8 %copy-start.9 = (bf16[3,1024,256]{2,1,0:T(8,128)(2,1)S(1)}, bf16[3,1024,256]{2,1,0:T(8,128)(2,1)}, u32[]{:S(2)}) copy-start(bf16[3,1024,256]{2,1,0:T(8,128)(2,1)} %param.16) | copy-start | bytes 4718596
  6.4 102.3 %collective-permute-start = (bf16[1024,1024]{1,0:T(8,128)(2,1)}, bf16[1024,1024]{1,0:T(8,128)(2,1)}, u32[]{:S(2)}, u32[]{:S(2)}) collective-permute-start(bf16[1024,1024]{1,0:T(8,128)(2,1)} %fusion.3), channel_id=1, source_target_pairs={{0,8},{8,16},{16,24},{1,9},{9,17},{17,25},{2,10},{10,18},{18,26},{... | collective-permute-start | bytes 6291464 | tf_op jit(solution)/shard_map/ppermute | solution.py:1000
  14.6 91.5 %copy-start.3 = (bf16[1,1024,1024]{2,1,0:T(8,128)(2,1)S(1)}, bf16[1,1024,1024]{2,1,0:T(8,128)(2,1)}, u32[]{:S(2)}) copy-start(bf16[1,1024,1024]{2,1,0:T(8,128)(2,1)} %param.25) | copy-start | bytes 6291460
  108.7 9.1 %slice-start = ((s8[8388608]{0:T(1024)(128)(4,1)}), s8[4194304]{0:T(1024)(128)(4,1)S(1)}, s32[]{:S(2)}) async-start(s8[8388608]{0:T(1024)(128)(4,1)} %bitcast.86), calls=%async_computation | async-start | bytes 8388608
  108.9 8.9 %slice-start.1 = ((s8[8388608]{0:T(1024)(128)(4,1)}), s8[4194304]{0:T(1024)(128)(4,1)S(1)}, s32[]{:S(2)}) async-start(s8[8388608]{0:T(1024)(128)(4,1)} %bitcast.86), calls=%async_computation.1 | async-start | bytes 8388608
  131.8 91.9 %copy-start.6 = (bf16[1,1024,1024]{2,1,0:T(8,128)(2,1)S(1)}, bf16[1,1024,1024]{2,1,0:T(8,128)(2,1)}, u32[]{:S(2)}) copy-start(bf16[1,1024,1024]{2,1,0:T(8,128)(2,1)} %param.13) | copy-start | bytes 6291460
  131.8 91.9 %copy-start.18 = (f32[1024]{0:T(1024)S(1)}, f32[1024]{0:T(1024)}, u32[]{:S(2)}) copy-start(f32[1024]{0:T(1024)} %param.19) | copy-start | bytes 12292
  223.7 4.8 copy-start.12
  228.5 2.1 copy-start
  239.6 62.2 %copy-start.1 = (f32[1024,1024]{1,0:T(8,128)S(1)}, f32[1024,1024]{1,0:T(8,128)}, u32[]{:S(2)}) copy-start(f32[1024,1024]{1,0:T(8,128)} %copy-done) | copy-start | bytes 12582916
  301.9 6.5 %copy-start.2 = (f32[1024,1024]{1,0:T(8,128)S(1)}, f32[1024,1024]{1,0:T(8,128)}, u32[]{:S(2)}) copy-start(f32[1024,1024]{1,0:T(8,128)} %get-tuple-element.37) | copy-start | bytes 12582916
  301.9 6.5 %copy-start.4 = (bf16[1,1024,1024]{2,1,0:T(8,128)(2,1)S(1)}, bf16[1,1024,1024]{2,1,0:T(8,128)(2,1)}, u32[]{:S(2)}) copy-start(bf16[1,1024,1024]{2,1,0:T(8,128)(2,1)} %param.25) | copy-start | bytes 6291460
  301.9 6.5 %copy-start.7 = (f32[1024,1024]{1,0:T(8,128)S(1)}, f32[1024,1024]{1,0:T(8,128)}, u32[]{:S(2)}) copy-start(f32[1024,1024]{1,0:T(8,128)} %get-tuple-element.36) | copy-start | bytes 12582916
  301.9 6.5 %copy-start.16 = (f32[1024]{0:T(1024)S(1)}, f32[1024]{0:T(1024)}, u32[]{:S(2)}) copy-start(f32[1024]{0:T(1024)} %param.24) | copy-start | bytes 12292
  311.4 6.0 %copy-start.5 = (bf16[1024,1024]{1,0:T(8,128)(2,1)}, bf16[1024,1024]{1,0:T(8,128)(2,1)S(1)}, u32[]{:S(2)}) copy-start(bf16[1024,1024]{1,0:T(8,128)(2,1)S(1)} %get-tuple-element.77.low_in) | copy-start | bytes 6291460
  567.1 4.5 copy-start.13
  567.1 6.4 %copy-start.11 = (f32[16,1024]{1,0:T(8,128)S(1)}, f32[16,1024]{1,0:T(8,128)}, u32[]{:S(2)}) copy-start(f32[16,1024]{1,0:T(8,128)} %get-tuple-element.46) | copy-start | bytes 196612
  567.1 6.5 %copy-start.14 = (f32[1024]{0:T(1024)S(1)}, f32[1024]{0:T(1024)}, u32[]{:S(2)}) copy-start(f32[1024]{0:T(1024)} %param.15) | copy-start | bytes 12292
  580.8 6.7 %copy-start.8 = (bf16[1024,1024]{1,0:T(8,128)(2,1)S(1)}, bf16[1024,1024]{1,0:T(8,128)(2,1)}, u32[]{:S(2)}) copy-start(bf16[1024,1024]{1,0:T(8,128)(2,1)} %get-tuple-element.45) | copy-start | bytes 6291460
